TPU v7x, 256 devices: a whole 4x4x8 slice. The times are simulated.
256 devices in a mesh: gy: 8 (over y, core), gx: 32 (over z, x).
Axes of the slice: x: 4, y: 4, z: 8, core: 2. Of those that a mesh axis runs over, the one named last changes fastest.
Arguments:
- tokens: bfloat16 [128, 96, 4096], P('gy', None, 'gx'), may hold values from -6 to 6
- in_weight: bfloat16 [96, 419], replicated, may hold values from -0.625 to 0.625
- conv_weight: float32 [3, 3, 224], replicated, may hold values from -2 to 2
- conv_bias: float32 [224], replicated, may hold values from -0.5 to 0.5
- step_bias: float32 [3], replicated, may hold values from -4 to -2
- decay_log: float32 [3], replicated, may hold values from -7.7 to 0, as said below
- skip_gain: float32 [3], replicated, may hold values from 0.5 to 1.5
- norm_gain: float32 [192], replicated, may hold values from 0.1 to 1.9
- out_weight: bfloat16 [192, 96], replicated, may hold values from -0.4375 to 0.4375
Outputs:
- layer_out: bfloat16 [128, 96, 4096], P('gy', None, 'gx')
Inputs may be any that keep to these rules, and one draw needn't show every extreme that they name: `decay_log`: one value a head.
All inputs are finite; a program needn't handle non-finite values.
Results may differ from a plain program's by a relative error of at most 0.00325.
The roundings to bfloat16 on the way count: a program that leaves them out, or rounds other values in their place, can miss the bound.
Values may be sent and summed in bfloat16 or wider, within the bound.
No kernel may reach another device: no remote copies, remote signals or barrier semaphores. Data moves between devices by JAX's collectives and lax.ppermute only.
A program may use at most 128 MiB of HBM per device.

v0:
```python
import jax
import jax.numpy as jnp
from jax import lax
from jax.sharding import PartitionSpec as P

norm_eps = 1e-05


def with_halo(shard, sides, width):
    for axis, dim in sides:
        count, length = (lax.axis_size(axis), shard.shape[dim])
        up = [(i, (i + 1) % count) for i in range(count - 1)]
        down = [(j, i) for i, j in up]
        last = lax.slice_in_dim(shard, length - width, length, axis=dim)
        first = lax.slice_in_dim(shard, 0, width, axis=dim)
        before = lax.ppermute(last, axis, up)
        after = lax.ppermute(first, axis, down)
        shard = jnp.concatenate([before, shard, after], axis=dim)
    return shard


def prefix(part, axis, combine, identity):
    place = lax.axis_index(axis)
    gathered = jax.tree.map(lambda a: lax.all_gather(a, axis), part)
    state = jax.tree.map(lambda a, e: jnp.zeros_like(a) + jnp.asarray(e, a.dtype), part, identity)

    def one(step, state):
        return combine(
            state, jax.tree.map(lambda a: lax.dynamic_index_in_dim(a, step, 0, False), gathered)
        )

    return lax.fori_loop(0, place, one, state)


def project(features, in_weight):
    return jnp.einsum(
        "rdc,dk->rkc", features, in_weight, preferred_element_type=jnp.float32
    ).astype(jnp.bfloat16)


def link(earlier, later):
    return (earlier[0] * later[0], later[0][..., None] * earlier[1] + later[1])


def on_device(
    tokens,
    in_weight,
    conv_weight,
    conv_bias,
    step_bias,
    decay_log,
    skip_gain,
    norm_gain,
    out_weight,
):
    highest = lax.Precision.HIGHEST
    row_count, width_d, col_count = tokens.shape
    inner_width = norm_gain.shape[0]
    head_count = skip_gain.shape[0]
    head_size = inner_width // head_count
    conv_count = conv_weight.shape[2]
    state_size = (conv_count - inner_width) // 2
    projected = project(tokens, in_weight)
    conv_pad = with_halo(
        projected[:, inner_width : inner_width + conv_count, :], (("gy", 0), ("gx", 2)), 1
    )
    summed = jnp.zeros((row_count, conv_count, col_count), jnp.float32) + conv_bias[None, :, None]
    for shift_row in range(3):
        for shift_col in range(3):
            summed = summed + conv_weight[shift_row, shift_col][None, :, None] * conv_pad[
                shift_row : shift_row + row_count, :, shift_col : shift_col + col_count
            ].astype(jnp.float32)
    activated = jax.nn.silu(summed).astype(jnp.bfloat16)
    step_raw = projected[:, inner_width + conv_count :, :].astype(jnp.float32)
    step_size = jax.nn.softplus(step_raw + step_bias[None, :, None])
    log_decay = -jnp.exp(decay_log)[None, :, None] * step_size
    inner_x = (
        activated[:, :inner_width, :]
        .astype(jnp.float32)
        .reshape(row_count, head_count, head_size, col_count)
    )
    input_map = activated[:, inner_width : inner_width + state_size, :].astype(jnp.float32)
    output_map = activated[:, inner_width + state_size :, :].astype(jnp.float32)
    scaled_x = step_size[:, :, None, :] * inner_x
    row_cumul = jnp.cumsum(log_decay, axis=2)
    col_cumul = jnp.cumsum(log_decay, axis=0)
    end_weights = jnp.exp(row_cumul[:, :, -1:] - row_cumul)
    row_ends = jnp.einsum(
        "ihpk,ink->ihpn", end_weights[:, :, None, :] * scaled_x, input_map, precision=highest
    )
    row_ends = row_ends.reshape(row_count, head_count, head_size * state_size)
    row_decay = jnp.exp(row_cumul[:, :, -1])
    identity = (jnp.ones_like(row_decay), jnp.zeros_like(row_ends))
    _, row_carry = prefix((row_decay, row_ends), "gx", link, identity)
    causal = jnp.arange(col_count)[:, None] >= jnp.arange(col_count)[None, :]
    group_count = row_count // 4

    def regroup(values):
        return values.reshape((group_count, 4) + values.shape[1:])

    def one_group(column_state, item):
        cumul_grp, decay_grp, scaled_grp, input_grp, output_grp, carry_grp = item
        readouts = []
        for offset in range(4):
            cumul_row = cumul_grp[offset]
            outer_terms = jnp.einsum(
                "hpk,nk->hkpn", scaled_grp[offset], input_grp[offset], precision=highest
            )
            outer_terms = outer_terms.reshape(head_count, col_count, head_size * state_size)
            spread = cumul_row[:, :, None] - cumul_row[:, None, :]
            weights = jnp.exp(jnp.where(causal[None], spread, -jnp.inf))
            row_states = jnp.einsum("hjk,hkq->hjq", weights, outer_terms, precision=highest)
            row_states = row_states + jnp.exp(cumul_row)[:, :, None] * carry_grp[offset][:, None, :]
            column_state = jnp.exp(decay_grp[offset])[:, :, None] * column_state + row_states
            readout = jnp.einsum(
                "hjpn,nj->hpj",
                column_state.reshape(head_count, col_count, head_size, state_size),
                output_grp[offset],
                precision=highest,
            )
            readouts.append(readout)
        return (column_state, jnp.stack(readouts, axis=0))

    start = jnp.zeros((head_count, col_count, head_size * state_size), jnp.float32)
    items = (
        regroup(row_cumul),
        regroup(log_decay),
        regroup(scaled_x),
        regroup(input_map),
        regroup(output_map),
        regroup(row_carry),
    )
    bottom, stacked = lax.scan(one_group, start, items)
    local_mixed = stacked.reshape(row_count, head_count, head_size, col_count)
    col_decay = jnp.exp(col_cumul[-1])
    identity = (jnp.ones_like(col_decay), jnp.zeros_like(bottom))
    _, col_carry = prefix((col_decay, bottom), "gy", link, identity)
    carried = jnp.einsum(
        "hjpn,inj->ihpj",
        col_carry.reshape(head_count, col_count, head_size, state_size),
        output_map,
        precision=highest,
    )
    mixed = (
        local_mixed
        + jnp.exp(col_cumul)[:, :, None, :] * carried
        + skip_gain[None, :, None, None] * inner_x
    )
    mixed = mixed.reshape(row_count, inner_width, col_count)
    gated = mixed * jax.nn.silu(projected[:, :inner_width, :].astype(jnp.float32))
    normed = (
        gated
        * lax.rsqrt(jnp.mean(gated * gated, axis=1, keepdims=True) + norm_eps)
        * norm_gain[None, :, None]
    )
    return jnp.einsum(
        "rec,ed->rdc", normed.astype(jnp.bfloat16), out_weight, preferred_element_type=jnp.float32
    ).astype(jnp.bfloat16)


def solution(mesh):
    return jax.shard_map(
        on_device,
        mesh=mesh,
        in_specs=(P("gy", None, "gx"), P(), P(), P(), P(), P(), P(), P(), P()),
        out_specs=P("gy", None, "gx"),
        check_vma=False,
    )
```

profile of v0, /device:TPU:27, one launch (start us, length us, event | category | flops | bytes accessed | tf_op | source)
XLA Modules:
  0.0 429.9 jit_solution(10954921283102572851)
XLA Ops:
  10.4 3.2 collective-permute-start.1
  22.4 3.1 collective-permute-start.2
  26.0 2.2 collective-permute-start.3
  31.0 1.9 maximum_maximum_fusion
  32.9 2.7 multiply_convert_fusion
  39.4 48.7 %all-gather = f32[512,3,1]{2,0,1:T(8,128)} all-gather(f32[16,3,1]{2,0,1:T(8,128)S(1)} %get-tuple-element.347), channel_id=2, replica_groups=mesh['gy'=8,'gx'=32] {'gx'}, dimensions={0}, use_global_device_ids=true | all-gather | bytes 6336 | tf_op jit(solution)/shard_map/all_gather | solution.py:24
  93.7 40.0 %all-gather.5.cloned.1.call-done = f32[32,16,3,1024]{3,1,2,0:T(8,128)} async-done(((f32[1,16,3,1024]{3,1,2,0:T(8,128)}), f32[32,16,3,1024]{3,1,2,0:T(8,128)}) %all-gather.5.cloned.1.call-update) | async-done | bytes 6291472 | tf_op jit(solution)/shard_map/all_gather | solution.py:24
  135.4 148.8 %while.40 = (s32[]{:T(128)}, f32[3,128,1024]{2,1,0:T(8,128)S(1)}, f32[4,4,3,64,128]{4,3,2,1,0:T(8,128)}, f32[4,4,3,128]{3,2,1,0:T(4,128)}, f32[4,4,3,128]{3,1,0,...) while((s32[]{:T(128)}, f32[3,128,1024]{2,1,0:T(8,128)S(1)}, ...), condition=%wide.region_4.5_spmd.clone.clone, body=%wide.region_3.4_spmd.clone.clone.sunk | while | flops 2427928576 | bytes 61191308 | solution.py:133
  143.3 3.1 fusion.103
  152.4 2.9 add_add_fusion.8
  155.4 3.0 copy.161
  160.1 3.0 copy.162
  180.5 3.1 fusion.103
  189.6 2.9 add_add_fusion.8
  192.6 3.0 copy.161
  197.3 3.0 copy.162
  217.7 3.1 fusion.103
  226.8 2.9 add_add_fusion.8
  229.8 3.0 copy.161
  234.5 3.0 copy.162
  254.8 3.1 fusion.103
  264.0 2.9 add_add_fusion.8
  266.9 3.0 copy.161
  271.7 3.0 copy.162
  286.3 12.1 %all_gather.19 = f32[8,3,128]{2,1,0:T(4,128)S(1)} all-gather(f32[1,3,128]{2,1,0:T(4,128)S(1)} %slice_exponential_fusion.1), channel_id=1, replica_groups=mesh['gy'=8,'gx'=32] {'gy'}, dimensions={0}, use_global_device_ids=true | all-gather | bytes 13824 | tf_op jit(solution)/shard_map/all_gather | solution.py:24
  298.4 2.3 copy.71
  301.9 3.0 copy.66
  304.9 88.2 %all-gather.7.cloned.1.call-done = f32[24,128,1024]{2,1,0:T(8,128)} async-done(((f32[3,128,1024]{2,1,0:T(8,128)}), f32[24,128,1024]{2,1,0:T(8,128)}) %all-gather.7.cloned.1.call-update) | async-done | bytes 12582928 | tf_op jit(solution)/shard_map/all_gather | solution.py:24
  393.3 12.3 %while.39 = (s32[]{:T(128)}, f32[3,128,1024]{2,1,0:T(8,128)S(1)}, s32[]{:T(128)}, f32[8,3,128]{2,1,0:T(4,128)S(1)}, f32[8,3,128,1024]{3,2,1,0:T(8,128)}, /*index=5*/s32[]{:T(128)}, s32[]{:T(128)}, s32[]{:T(128)}) while((s32[]{:T(128)}, f32[3,128,1024]{2,1,0:T(8,128)S(1)}, s32[]{:T(128)}, f32[8,3,128]{2,1,0:T(4,128)S(1)}, ...), condition=%wide.region_7.8_spmd, body=%wide.region_6.7_spmd.sunk | while | flops 786437 | bytes 4723327 | solution.py:32
  407.2 3.4 copy.70
  410.7 7.1 %fusion.50 = f32[16,3,64,128]{2,0,1,3:T(8,128)} fusion(f32[16,3,64,128]{2,0,1,3:T(8,128)} %bitcast.265, f32[16,3,64,128]{2,0,1,3:T(8,128)S(1)} %copy-done.9, bf16[16,16,128,1]{1,0,3,2:T(8,128)(2,1)} %copy.104, f32[3,128,64,16]{2,3,0,1:T(8,128)} %copy.70, f32[3]{0:T(128)S(1)} %copy-done.30, f32[16,3,128]{0,1,2:T(4,128)S(1)} %copy.67), kind=kOutput, calls=%fused_computation.98 | convolution fusion | flops 77070336 | bytes 6381580 | tf_op jit(solution)/shard_map/hjpn,inj->ihpj/dot_general | solution.py:138
  417.7 2.4 copy.72
  (308 shorter events, 147.6 us)
Async XLA Ops:
  6.5 7.1 %copy-start.31 = (f32[3]{0:T(128)S(1)}, f32[3]{0:T(128)}, u32[]{:S(2)}) copy-start(f32[3]{0:T(128)} %param.20) | copy-start | bytes 40
  6.5 7.1 %copy-start.29 = (f32[3]{0:T(128)S(1)}, f32[3]{0:T(128)}, u32[]{:S(2)}) copy-start(f32[3]{0:T(128)} %param.19) | copy-start | bytes 40
  6.5 127.2 %all-gather.5.cloned.1.call-start = ((), (), s32[]{:S(2)}) async-start(), calls=%async_computation | async-start | bytes 6488064 | tf_op jit(solution)/shard_map/all_gather | solution.py:24
  9.1 9.8 %copy-start.10 = (bf16[16,419,128]{2,1,0:T(8,128)(2,1)}, bf16[16,419,128]{2,1,0:T(8,128)(2,1)S(1)}, u32[]{:S(2)}) copy-start(bf16[16,419,128]{2,1,0:T(8,128)(2,1)S(1)} %fusion.57) | copy-start | bytes 5148676
  9.1 9.6 %collective-permute-start = (bf16[1,224,128]{2,1,0:T(8,128)(2,1)S(1)}, bf16[1,224,128]{2,1,0:T(8,128)(2,1)S(1)}, u32[]{:S(2)}, u32[]{:S(2)}) collective-permute-start(bf16[1,224,128]{2,1,0:T(8,128)(2,1)S(1)} %get-tuple-element.337), channel_id=1, source_target_pairs={{0,32},{32,64},{64,96},{96,128},{128,160},{160,192},{192,224},{1,3... | collective-permute-start | bytes 172040 | tf_op jit(solution)/shard_map/ppermute | solution.py:16
  10.4 8.3 %collective-permute-start.1 = (bf16[1,224,128]{2,1,0:T(8,128)(2,1)S(1)}, bf16[1,224,128]{2,1,0:T(8,128)(2,1)S(1)}, u32[]{:S(2)}, u32[]{:S(2)}) collective-permute-start(bf16[1,224,128]{2,1,0:T(8,128)(2,1)S(1)} %get-tuple-element.338), channel_id=1, source_target_pairs={{32,0},{64,32},{96,64},{128,96},{160,128},{192,160},{224,192},{33,... | collective-permute-start | bytes 172040 | tf_op jit(solution)/shard_map/ppermute | solution.py:17
  20.5 5.0 %copy-start.11 = (bf16[18,224,1]{2,1,0:T(8,128)(2,1)S(1)}, bf16[18,224,1]{2,1,0:T(8,128)(2,1)}, u32[]{:S(2)}) copy-start(bf16[18,224,1]{2,1,0:T(8,128)(2,1)} %get-tuple-element.342) | copy-start | bytes 24196
  20.5 7.7 %copy-start.26 = (f32[3,3,224]{2,1,0:T(4,128)S(1)}, f32[3,3,224]{2,1,0:T(4,128)}, u32[]{:S(2)}) copy-start(f32[3,3,224]{2,1,0:T(4,128)} %param.17) | copy-start | bytes 24196
  22.4 5.9 %collective-permute-start.2 = (bf16[18,224,1]{1,0,2:T(8,128)(2,1)S(1)}, bf16[18,224,1]{1,0,2:T(8,128)(2,1)S(1)}, u32[]{:S(2)}, u32[]{:S(2)}) collective-permute-start(bf16[18,224,1]{1,0,2:T(8,128)(2,1)S(1)} %copy.57), channel_id=1, source_target_pairs={{0,1},{1,2},{2,3},{3,4},{4,5},{5,6},{6,7},{7,8},{8,9},{9,10},{10,1... | collective-permute-start | bytes 24200 | tf_op jit(solution)/shard_map/ppermute | solution.py:16
  26.0 4.4 %collective-permute-start.3 = (bf16[18,224,1]{1,0,2:T(8,128)(2,1)S(1)}, bf16[18,224,1]{1,0,2:T(8,128)(2,1)S(1)}, u32[]{:S(2)}, u32[]{:S(2)}) collective-permute-start(bf16[18,224,1]{1,0,2:T(8,128)(2,1)S(1)} %copy.59), channel_id=1, source_target_pairs={{1,0},{2,1},{3,2},{4,3},{5,4},{6,5},{7,6},{8,7},{9,8},{10,9},{11,1... | collective-permute-start | bytes 24200 | tf_op jit(solution)/shard_map/ppermute | solution.py:17
  35.8 56.5 %copy-start.5 = (f32[16,192,128]{2,1,0:T(8,128)}, f32[16,192,128]{2,1,0:T(8,128)S(1)}, u32[]{:S(2)}) copy-start(f32[16,192,128]{2,1,0:T(8,128)S(1)} %slice_convert_fusion) | copy-start | bytes 4718596
  39.3 353.8 %all-gather.7.cloned.1.call-start = ((), (), s32[]{:S(2)}) async-start(), calls=%async_computation.1 | async-start | bytes 14155776 | tf_op jit(solution)/shard_map/all_gather | solution.py:24
  135.4 7.9 %copy-start.7 = (f32[4,4,3,1024]{3,2,1,0:T(4,128)}, f32[4,4,3,1024]{3,2,1,0:T(4,128)S(1)}, u32[]{:S(2)}) copy-start(f32[4,4,3,1024]{3,2,1,0:T(4,128)S(1)} %get-tuple-element.599) | copy-start | bytes 589828 | tf_op jit(solution)/shard_map/while
  143.3 3.2 copy-start.16
  169.9 2.7 copy-start.3
  169.9 2.7 copy-start.8
  172.6 7.9 %copy-start.7 = (f32[4,4,3,1024]{3,2,1,0:T(4,128)}, f32[4,4,3,1024]{3,2,1,0:T(4,128)S(1)}, u32[]{:S(2)}) copy-start(f32[4,4,3,1024]{3,2,1,0:T(4,128)S(1)} %get-tuple-element.599) | copy-start | bytes 589828 | tf_op jit(solution)/shard_map/while
  180.5 3.2 copy-start.16
  207.1 2.7 copy-start.3
  207.1 2.7 copy-start.8
  209.8 7.9 %copy-start.7 = (f32[4,4,3,1024]{3,2,1,0:T(4,128)}, f32[4,4,3,1024]{3,2,1,0:T(4,128)S(1)}, u32[]{:S(2)}) copy-start(f32[4,4,3,1024]{3,2,1,0:T(4,128)S(1)} %get-tuple-element.599) | copy-start | bytes 589828 | tf_op jit(solution)/shard_map/while
  217.6 3.2 copy-start.16
  244.3 2.7 copy-start.3
  244.3 2.7 copy-start.8
  247.0 7.9 %copy-start.7 = (f32[4,4,3,1024]{3,2,1,0:T(4,128)}, f32[4,4,3,1024]{3,2,1,0:T(4,128)S(1)}, u32[]{:S(2)}) copy-start(f32[4,4,3,1024]{3,2,1,0:T(4,128)S(1)} %get-tuple-element.599) | copy-start | bytes 589828 | tf_op jit(solution)/shard_map/while
  254.8 3.2 copy-start.16
  281.5 2.6 copy-start.8
  284.1 14.2 %copy-start.6 = (f32[16,192,128]{2,1,0:T(8,128)S(1)}, f32[16,192,128]{2,1,0:T(8,128)}, u32[]{:S(2)}) copy-start(f32[16,192,128]{2,1,0:T(8,128)} %copy-done.5) | copy-start | bytes 4718596
  298.4 3.5 copy-start.13
  407.2 3.5 copy-start.9
  407.2 3.5 copy-start.30
  420.1 2.9 copy-start.1
  (48 other events, 53.1 us)
Sparse Core Ops, SparseCore 0:
  39.4 94.2 all-gather.4
  285.5 107.5 all-gather.6
where the time goes:
time: 433 us; the launch traced here: 430 us
  waiting for transfers between devices  130 us (30%)
  local copies, waits for them, and re-layouts  100 us (23%)
  other arithmetic  65.4 us (15%)
  blocking collectives  60.7 us (14%)
  matrix products  48.6 us (11%)
  between operations  13.8 us (3%)
  starting transfers between devices  9.83 us (2%)
    all_gather x2, waiting for transfers between devices, prefix(): gathered = jax.tree.map(lambda a: lax.all_gather(a, axis), part)  128 us
    all_gather x2, blocking collectives, prefix(): gathered = jax.tree.map(lambda a: lax.all_gather(a, axis), part)  60.7 us
    while x132, local copies, waits for them, and re-layouts  51.6 us
    dot_general x16, matrix products, one_group(): jnp.einsum('hjk,hkq->hjq', weights, outer_terms, precision=highest)  37.9 us
    dot_general x16, other arithmetic, one_group(): jnp.einsum('hjpn,nj->hpj', column_state.reshape(head_count, col_count, he...  28.2 us
    add x8, other arithmetic, link(): return (earlier[0] * later[0], later[0][..., None] * earlier[1] + later[1])  12.3 us
  transfers between devices with their start and end apart: 6, of which 3 were waited for; matrix products, arithmetic and copies ran while one was open for 4% of the time, Pallas kernels for 0%

commit v1 on v0

v1 whole, which is shorter than its diff:
```python
import jax
import jax.numpy as jnp
from jax import lax
from jax.experimental import pallas as pl
from jax.experimental.pallas import tpu as pltpu
from jax.sharding import PartitionSpec as P

f32, bf16 = jnp.float32, jnp.bfloat16
norm_eps = 1e-05
ROWS, COLS, WIDTH, LANES = 16, 128, 96, 128
BLOCK, BLOCKS = 16, 8
VMEM = 56 * 1024 * 1024


def silu(v):
    return v / (1.0 + jnp.exp(-v))


def split(v):
    high = v.astype(bf16)
    return high, (v - high.astype(f32)).astype(bf16)


def dot(a, b, dims):
    return lax.dot_general(a, b, (dims, ((), ())), preferred_element_type=f32)


def lane_iota():
    return lax.broadcasted_iota(jnp.int32, (8, LANES), 1)


def fold_sublanes(parts):
    place = lax.broadcasted_iota(jnp.int32, (8, LANES), 0)
    step = 1
    while len(parts) > 1:
        first = (place & step) == 0
        parts = [
            jnp.where(first, a, b) + pltpu.roll(jnp.where(first, b, a), 8 - step, 0)
            for a, b in zip(parts[0::2], parts[1::2])
        ]
        step *= 2
    return parts[0]


def entry_kernel(
    tok, up, down, left, right, weight, taps, vec, xdt, decay, act, gate, bct, ends, proj
):
    lanes = lane_iota()

    def place_row(index, tokens):
        out = dot(tokens, weight[:, 0:384], ((0,), (0,))).astype(bf16).astype(f32)
        for g in range(3):
            proj[index, g, 8:136, :] = out[:, g * 128 : g * 128 + 128]

    place_row(0, up[0:WIDTH, :])
    place_row(ROWS + 1, down[0:WIDTH, :])

    def own_row(r, carry):
        out = dot(tok[r], weight[...], ((0,), (0,))).astype(bf16)
        for g in range(3):
            proj[r + 1, g, 8:136, :] = out[:, g * 128 : g * 128 + 128].astype(f32)
        for g in range(2):
            gate[r, g] = out[:, 640 + g * 128 : 768 + g * 128]
            raw = out[:, 384 + g * 128 : 512 + g * 128].astype(f32) + vec[g, 0:1, :]
            step = jnp.maximum(raw, 0.0) + jnp.log1p(jnp.exp(-jnp.abs(raw)))
            xdt[r, g] = step
        return carry

    lax.fori_loop(0, ROWS, own_row, 0)
    for side, at in ((left, 7), (right, 136)):
        out = dot(side[...], weight[:, 0:384], ((1,), (0,))).astype(bf16).astype(f32)
        for g in range(3):
            proj[:, g, at, :] = out[0 : ROWS + 2, g * 128 : g * 128 + 128]

    row_at = lax.broadcasted_iota(jnp.int32, (COLS, COLS), 0)
    col_at = lax.broadcasted_iota(jnp.int32, (COLS, COLS), 1)
    later = jnp.where(col_at > row_at, 1.0, 0.0).astype(bf16)
    later = jnp.concatenate([later, later], axis=1)

    def conv_row(r, carry):
        parts = []
        for g in range(3):
            acc = jnp.broadcast_to(taps[g, 9:10, :], (COLS, LANES))
            for a in range(3):
                for b in range(3):
                    k = a * 3 + b
                    acc = acc + taps[g, k : k + 1, :] * proj[r + a, g, 7 + b : 135 + b, :]
            parts.append(silu(acc).astype(bf16))
        turned = parts[2].astype(f32).T[0:32, :]
        bct[r] = turned
        b_pair = turned[0:16, :].astype(bf16)
        b_pair = jnp.concatenate([b_pair, b_pair], axis=1)
        states, totals = [], []
        for g in range(2):
            act[r, g] = parts[g]
            step = xdt[r, g]
            log_decay = vec[g, 1:2, :] * step
            scaled = step * parts[g].astype(f32)
            xdt[r, g] = scaled
            decay[r, g] = jnp.exp(log_decay)
            suffix = dot(later, jnp.concatenate(split(log_decay), axis=0), ((1,), (0,)))
            totals.append(jnp.exp(suffix[0:1, :] + log_decay[0:1, :]))
            weighted = scaled * jnp.exp(suffix)
            states.append(dot(b_pair, jnp.concatenate(split(weighted), axis=0), ((1,), (0,))))
        third = jnp.where(lanes < 64, states[1][0:8, :], states[1][8:16, :])
        rest = jnp.concatenate(totals + [jnp.zeros((2, LANES), f32)], axis=0)
        ends[2 * r] = jnp.concatenate([states[0][0:8, :], third[0:4, :], rest], axis=0)
        ends[2 * r + 1] = jnp.concatenate([states[0][8:16, :], third[4:8, :], rest], axis=0)
        return carry

    lax.fori_loop(0, ROWS, conv_row, 0)


def row_prefix_kernel(parts, out):
    count = parts.shape[0]
    first = jnp.zeros((8, LANES), f32)
    second = jnp.zeros((8, LANES), f32)
    for s in range(count):
        out[s, 0:8, :] = first
        out[s, 8:16, :] = second
        first = parts[s, 12:13, :] * first + parts[s, 0:8, :]
        second = parts[s, 13:14, :] * second + parts[s, 8:16, :]


def scan_kernel(xdt, decay, bct, carry, local, bottom):
    lanes = lane_iota()
    low = lanes < 64

    def group(rg, _):
        begin = []
        for i in range(4):
            r = rg * 4 + i
            begin.append(carry[2 * r, 0:8, :])
            begin.append(carry[2 * r + 1, 0:8, :])
            begin.append(
                jnp.concatenate([carry[2 * r, 8:12, :], carry[2 * r + 1, 8:12, :]], axis=0)
            )

        def block(cb, state):
            state = list(state)
            base = cb * BLOCK
            maps = [pltpu.roll(bct[rg * 4 + i], COLS - base, 1) for i in range(4)]
            for j in range(BLOCK):
                c = base + j
                cols = [
                    jnp.where(rg == 0, 0.0, bottom[cb, j * 24 + 8 * q : j * 24 + 8 * q + 8, :])
                    for q in range(3)
                ]
                reads = []
                for i in range(4):
                    r = rg * 4 + i
                    wide = [
                        jnp.broadcast_to(maps[i][8 * q : 8 * q + 8, j : j + 1], (8, LANES))
                        for q in range(4)
                    ]
                    b_third = jnp.where(low, wide[0], wide[1])
                    c_third = jnp.where(low, wide[2], wide[3])
                    x = [xdt[r, g, pl.ds(c, 8, stride=0), :] for g in range(2)]
                    d = [decay[r, g, pl.ds(c, 8, stride=0), :] for g in range(2)]
                    for q, (g, b) in enumerate(((0, wide[0]), (0, wide[1]), (1, b_third))):
                        state[3 * i + q] = d[g] * state[3 * i + q] + x[g] * b
                        cols[q] = d[g] * cols[q] + state[3 * i + q]
                    reads.append(wide[2] * cols[0] + wide[3] * cols[1])
                    reads.append(c_third * cols[2])
                for q in range(3):
                    bottom[cb, j * 24 + 8 * q : j * 24 + 8 * q + 8, :] = cols[q]
                local[rg, :, c, :] = fold_sublanes(reads)
            return tuple(state)

        lax.fori_loop(0, BLOCKS, block, tuple(begin))
        return 0

    lax.fori_loop(0, 4, group, 0)

    def totals(cb, _):
        base = pl.multiple_of(cb * BLOCK, BLOCK)
        for g in range(2):
            product = decay[0, g, pl.ds(base, BLOCK), :]
            for r in range(1, ROWS):
                product = product * decay[r, g, pl.ds(base, BLOCK), :]
            bottom[cb, 384 + 16 * g : 400 + 16 * g, :] = product
        return 0

    lax.fori_loop(0, BLOCKS, totals, 0)


def col_prefix_kernel(parts, out):
    def column(j, _):
        state = [jnp.zeros((8, LANES), f32) for _ in range(3)]
        base = pl.multiple_of(j * 24, 8)
        for s in range(BLOCKS):
            d = [parts[s, pl.ds(384 + 16 * g + j, 8, stride=0), :] for g in range(2)]
            for q in range(3):
                out[s, pl.ds(base + 8 * q, 8), :] = state[q]
                state[q] = d[q // 2] * state[q] + parts[s, pl.ds(base + 8 * q, 8), :]
        return 0

    lax.fori_loop(0, BLOCK, column, 0)


def exit_kernel(states, bct, local, decay, act, gate, vec, weight, out, carried):
    lanes = lane_iota()
    low = lanes < 64

    def group(rg, _):
        def block(cb, _):
            base = cb * BLOCK
            maps = [pltpu.roll(bct[rg * 4 + i, 16:32, :], COLS - base, 1) for i in range(4)]
            for j in range(BLOCK):
                cols = [states[cb, j * 24 + 8 * q : j * 24 + 8 * q + 8, :] for q in range(3)]
                reads = []
                for i in range(4):
                    wide = [
                        jnp.broadcast_to(maps[i][8 * q : 8 * q + 8, j : j + 1], (8, LANES))
                        for q in range(2)
                    ]
                    reads.append(wide[0] * cols[0] + wide[1] * cols[1])
                    reads.append(jnp.where(low, wide[0], wide[1]) * cols[2])
                carried[rg, :, base + j, :] = fold_sublanes(reads)
            return 0

        lax.fori_loop(0, BLOCKS, block, 0)
        return 0

    lax.fori_loop(0, 4, group, 0)

    reach = [jnp.ones((COLS, LANES), f32)] * 2
    for r in range(ROWS):
        gated = []
        for g in range(2):
            s = (r % 4) * 2 + g
            reach[g] = reach[g] * decay[r, g]
            mixed = local[r // 4, s] + reach[g] * carried[r // 4, s]
            if g == 1:
                mixed = mixed + pltpu.roll(mixed, 64, 1)
            mixed = mixed + vec[g, 2:3, :] * act[r, g].astype(f32)
            gated.append(mixed * silu(gate[r, g].astype(f32)))
        total = jnp.sum(gated[0] * gated[0] + gated[1] * gated[1], axis=1, keepdims=True)
        scale = lax.rsqrt(total * (1.0 / 192) + norm_eps)
        normed = [(gated[g] * scale * vec[g, 3:4, :]).astype(bf16) for g in range(2)]
        result = dot(weight[...], jnp.concatenate(normed, axis=1), ((1,), (1,)))
        out[r] = result.astype(bf16)


def call(kernel, shapes, scratch, *operands):
    return pl.pallas_call(
        kernel,
        out_shape=[jax.ShapeDtypeStruct(s, t) for s, t in shapes],
        scratch_shapes=scratch,
        compiler_params=pltpu.CompilerParams(vmem_limit_bytes=VMEM),
    )(*operands)


def steps(axis):
    count = lax.axis_size(axis)
    up = [(i, i + 1) for i in range(count - 1)]
    return up, [(j, i) for i, j in up]


def on_device(
    tokens,
    in_weight,
    conv_weight,
    conv_bias,
    step_bias,
    decay_log,
    skip_gain,
    norm_gain,
    out_weight,
):
    to_right, to_left = steps("gx")
    to_down, to_up = steps("gy")
    left = lax.ppermute(tokens[:, :, COLS - 1], "gx", to_right)
    right = lax.ppermute(tokens[:, :, 0], "gx", to_left)

    def edge(r):
        rest = jnp.stack([left[r], right[r]])
        return jnp.concatenate([tokens[r], jnp.pad(rest, ((0, 14), (0, 32)))], axis=0)

    above = lax.ppermute(edge(ROWS - 1), "gy", to_down)
    below = lax.ppermute(edge(0), "gy", to_up)

    def beside(at, own):
        rows = [above[at : at + 1, :WIDTH], own, below[at : at + 1, :WIDTH]]
        return jnp.pad(jnp.concatenate(rows, axis=0), ((0, 14), (0, 0)))

    def zeros(*shape):
        return jnp.zeros(shape, bf16)

    conv = in_weight[:, 192:416]
    wide = [
        conv[:, :192],
        conv[:, 128:192],
        conv[:, 192:],
        zeros(WIDTH, 96),
        jnp.repeat(in_weight[:, 416:], 64, axis=1),
        jnp.repeat(in_weight[:, 418:], 64, axis=1),
        in_weight[:, :192],
        zeros(WIDTH, 64),
    ]
    weight = jnp.concatenate(wide, axis=1)
    taps = jnp.concatenate([conv_weight.reshape(9, 224), conv_bias[None]], axis=0)
    taps = jnp.concatenate(
        [taps[:, :192], taps[:, 128:192], taps[:, 192:], jnp.zeros((10, 96), f32)], axis=1
    )
    taps = jnp.pad(taps.reshape(10, 3, 128).transpose(1, 0, 2), ((0, 0), (0, 6), (0, 0)))

    def by_head(v):
        return jnp.repeat(jnp.concatenate([v, v[2:]]), 64)

    vec = jnp.stack(
        [
            by_head(step_bias),
            by_head(-jnp.exp(decay_log)),
            by_head(skip_gain),
            jnp.pad(norm_gain, (0, 64)),
        ]
    )
    vec = jnp.pad(vec.reshape(4, 2, 128).transpose(1, 0, 2), ((0, 0), (0, 4), (0, 0)))
    out_turned = jnp.pad(out_weight.T, ((0, 0), (0, 64)))

    plane = (ROWS, 2, COLS, LANES)
    xdt, decay, act, gate, bct, ends = call(
        entry_kernel,
        [
            (plane, f32),
            (plane, f32),
            (plane, bf16),
            (plane, bf16),
            ((ROWS, 32, COLS), f32),
            ((2 * ROWS, 16, LANES), f32),
        ],
        [pltpu.VMEM((ROWS + 2, 3, 144, LANES), f32)],
        tokens,
        above,
        below,
        beside(96, left),
        beside(97, right),
        weight,
        taps,
        vec,
    )
    ends = lax.all_to_all(ends, "gx", 0, 0)
    (carry,) = call(row_prefix_kernel, [((2 * ROWS, 16, LANES), f32)], [], ends)
    carry = lax.all_to_all(carry, "gx", 0, 0)
    local, bottom = call(
        scan_kernel,
        [((4, 8, COLS, LANES), f32), ((BLOCKS, 416, LANES), f32)],
        [],
        xdt,
        decay,
        bct,
        carry,
    )
    bottom = lax.all_to_all(bottom, "gy", 0, 0)
    (states,) = call(col_prefix_kernel, [((BLOCKS, 384, LANES), f32)], [], bottom)
    states = lax.all_to_all(states, "gy", 0, 0)
    (out,) = call(
        exit_kernel,
        [((ROWS, WIDTH, COLS), bf16)],
        [pltpu.VMEM((4, 8, COLS, LANES), f32)],
        states,
        bct,
        local,
        decay,
        act,
        gate,
        vec,
        out_turned,
    )
    return out


def solution(mesh):
    return jax.shard_map(
        on_device,
        mesh=mesh,
        in_specs=(P("gy", None, "gx"), P(), P(), P(), P(), P(), P(), P(), P()),
        out_specs=P("gy", None, "gx"),
        check_vma=False,
    )
```

time: 433 us -> 177 us (0.41)
  the two profiles are of different devices: /device:TPU:27 before, /device:TPU:1 now
where the time goes in v1:
time: 177 us
  blocking collectives  71.1 us (40%)
  Pallas kernels  55.9 us (32%)
  waiting for transfers between devices  20.9 us (12%)
  starting transfers between devices  15.7 us (9%)
  local copies, waits for them, and re-layouts  9.74 us (6%)
  other arithmetic  2.91 us (2%)
    pallas_call x5, Pallas kernels, call(): pl.pallas_call(kernel, out_shape=[jax.ShapeDtypeStruct(s, t) for s, t in...  55.9 us
    all_to_all x1, blocking collectives, on_device(): bottom = lax.all_to_all(bottom, 'gy', 0, 0)  28.7 us
    all_to_all x1, blocking collectives, on_device(): ends = lax.all_to_all(ends, 'gx', 0, 0)  26 us
    all_to_all x1, waiting for transfers between devices, on_device(): states = lax.all_to_all(states, 'gy', 0, 0)  20 us
    all_to_all x1, blocking collectives, on_device(): carry = lax.all_to_all(carry, 'gx', 0, 0)  16.4 us
    all_to_all x1, starting transfers between devices, on_device(): states = lax.all_to_all(states, 'gy', 0, 0)  4.48 us
    ppermute x1, starting transfers between devices, on_device(): left = lax.ppermute(tokens[:, :, COLS - 1], 'gx', to_right)  3.94 us
  transfers between devices with their start and end apart: 5, of which 2 were waited for; matrix products, arithmetic and copies ran while one was open for 5% of the time, Pallas kernels for 0%

profile of v1, /device:TPU:1, one launch (start us, length us, event | category | flops | bytes accessed | tf_op | source)
XLA Modules:
  0.0 176.6 jit_solution(10117770296532437817)
XLA Ops:
  0.0 1.4 fusion.24
  1.4 0.2 copy.19
  1.6 3.9 %collective-permute-start = (bf16[16,96]{1,0:T(8,128)(2,1)S(1)}, bf16[16,96]{1,0:T(8,128)(2,1)S(1)}, u32[]{:S(2)}, u32[]{:S(2)}) collective-permute-start(bf16[16,96]{1,0:T(8,128)(2,1)S(1)} %bitcast.18), channel_id=1, source_target_pairs={{0,1},{1,2},{2,3},{3,4},{4,5},{5,6},{6,7},{7,8},{8,9},{9,10},{10,1... | collective-permute-start | bytes 9224 | tf_op jit(solution)/shard_map/ppermute | solution.py:273
  5.6 0.2 copy.20
  5.8 1.3 collective-permute-start.1
  7.1 0.8 slice_bitcast_fusion
  7.9 0.2 slice_reduce_fusion
  8.1 0.6 slice.97
  8.7 0.7 pad_maximum_fusion.3
  9.7 0.6 slice.96
  10.3 0.7 pad_maximum_fusion.2
  11.2 0.6 slice.98
  11.8 0.7 pad_maximum_fusion.4
  13.2 0.6 pad.34.taps
  13.8 0.6 pad.36.vec
  14.7 0.8 concatenate.36.weight
  15.6 2.9 %collective-permute-start.3 = (bf16[112,128]{1,0:T(8,128)(2,1)S(1)}, bf16[112,128]{1,0:T(8,128)(2,1)S(1)}, u32[]{:S(2)}, u32[]{:S(2)}) collective-permute-start(bf16[112,128]{1,0:T(8,128)(2,1)S(1)} %pad_maximum_fusion.1), channel_id=1, source_target_pairs={{32,0},{64,32},{96,64},{128,96},{160,128},{192,160},{224,192},{33,... | collective-permute-start | bytes 86024 | tf_op jit(solution)/shard_map/ppermute | solution.py:281
  18.5 3.1 %collective-permute-start.2 = (bf16[112,128]{1,0:T(8,128)(2,1)S(1)}, bf16[112,128]{1,0:T(8,128)(2,1)S(1)}, u32[]{:S(2)}, u32[]{:S(2)}) collective-permute-start(bf16[112,128]{1,0:T(8,128)(2,1)S(1)} %pad_maximum_fusion), channel_id=1, source_target_pairs={{0,32},{32,64},{64,96},{96,128},{128,160},{160,192},{192,224},{1,3... | collective-permute-start | bytes 86024 | tf_op jit(solution)/shard_map/ppermute | solution.py:280
  21.6 0.9 collective-permute-done.2.up
  22.6 0.6 fusion.10
  23.2 16.2 %shard_map.91 = (f32[16,2,128,128]{3,2,1,0:T(8,128)}, f32[16,2,128,128]{3,2,1,0:T(8,128)}, bf16[16,2,128,128]{3,2,1,0:T(8,128)(2,1)}, bf16[16,2,128,128]{3,2,1,0...) custom-call(bf16[16,96,128]{2,1,0:T(8,128)(2,1)} %tok.1, bf16[112,128]{1,0:T(8,128)(2,1)} %copy-done.4, ...), custom_call_target="tpu_custom_call" | custom-call | tf_op jit(solution)/shard_map/pallas_call | solution.py:246
  39.4 26.0 %all_to_all.20.parts = f32[32,16,128]{2,1,0:T(8,128)} all-to-all(f32[32,16,128]{2,1,0:T(8,128)} %get-tuple-element.16), channel_id=1, replica_groups=mesh['gy'=8,'gx'=32] {'gx'}, dimensions={0} | all-to-all | bytes 524288 | tf_op jit(solution)/shard_map/all_to_all | solution.py:343
  65.5 1.7 shard_map.92
  67.2 16.4 %all_to_all.21.carry = f32[32,16,128]{2,1,0:T(8,128)} all-to-all(f32[32,16,128]{2,1,0:T(8,128)} %shard_map.92), channel_id=1, replica_groups=mesh['gy'=8,'gx'=32] {'gx'}, dimensions={0} | all-to-all | bytes 524288 | tf_op jit(solution)/shard_map/all_to_all | solution.py:345
  83.6 19.1 %shard_map.93 = (f32[4,8,128,128]{3,2,1,0:T(8,128)}, f32[8,416,128]{2,1,0:T(8,128)}) custom-call(f32[16,2,128,128]{3,2,1,0:T(8,128)} %get-tuple-element.13.xdt, f32[16,2,128,128]{3,2,1,0:T(8,128)} %get-tuple-element.14.decay, f32[16,32,128]{2,1,0:T(8,128)} %get-tuple-element.15.bct, f32[32,16,128]{2,1,0:T(8,128)} %all_to_all.21.carry), custom_call_target="tpu_custom_call" | custom-call | tf_op jit(solution)/shard_map/pallas_call | solution.py:246
  102.6 28.7 %all_to_all.22.parts = f32[8,416,128]{2,1,0:T(8,128)} all-to-all(f32[8,416,128]{2,1,0:T(8,128)} %get-tuple-element.17), channel_id=1, replica_groups=mesh['gy'=8,'gx'=32] {'gy'}, dimensions={0} | all-to-all | bytes 3407872 | tf_op jit(solution)/shard_map/all_to_all | solution.py:355
  131.3 2.9 %shard_map.94 = f32[8,384,128]{2,1,0:T(8,128)} custom-call(f32[8,416,128]{2,1,0:T(8,128)} %all_to_all.22.parts), custom_call_target="tpu_custom_call" | custom-call | tf_op jit(solution)/shard_map/pallas_call | solution.py:246
  134.2 4.5 %all-to-all-start.3 = ((f32[8,384,128]{2,1,0:T(8,128)}), f32[8,384,128]{2,1,0:T(8,128)S(1)}, u32[]{:S(2)}, u32[]{:S(2)}) async-start(f32[8,384,128]{2,1,0:T(8,128)} %shard_map.94), calls=%async_computation.3 | async-start | bytes 3145728 | tf_op jit(solution)/shard_map/all_to_all | solution.py:357
  138.8 0.6 pad.37.weight
  139.5 20.0 %all-to-all-done.3.states = f32[8,384,128]{2,1,0:T(8,128)S(1)} async-done(((f32[8,384,128]{2,1,0:T(8,128)}), f32[8,384,128]{2,1,0:T(8,128)S(1)}, u32[]{:S(2)}, u32[]{:S(2)}) %all-to-all-start.3) | async-done | bytes 1572896 | tf_op jit(solution)/shard_map/all_to_all | solution.py:357
  159.5 1.1 copy-done
  160.6 16.0 %shard_map.95 = bf16[16,96,128]{2,1,0:T(8,128)(2,1)} custom-call(f32[8,384,128]{2,1,0:T(8,128)} %copy-done, f32[16,32,128]{2,1,0:T(8,128)} %get-tuple-element.15.bct, f32[4,8,128,128]{3,2,1,0:T(8,128)} %get-tuple-element.18.local, f32[16,2,128,128]{3,2,1,0:T(8,128)} %get-tuple-element.14.decay, bf16[16,2,128,128]{3,2,1,0:T(8,128)(2,1)} %get-tuple-element.19.act, ...), custom_call_target="tpu_custom_call" | custom-call | tf_op jit(solution)/shard_map/pallas_call | solution.py:246
  (61 shorter events, 1.7 us)
Async XLA Ops:
  0.0 7.8 %copy-start.1 = (bf16[96,419]{1,0:T(8,128)(2,1)S(1)}, bf16[96,419]{1,0:T(8,128)(2,1)}, u32[]{:S(2)}) copy-start(bf16[96,419]{1,0:T(8,128)(2,1)} %param.10) | copy-start | bytes 241348
  0.0 8.1 %copy-start.5 = (f32[3,3,224]{2,1,0:T(4,128)S(1)}, f32[3,3,224]{2,1,0:T(4,128)}, u32[]{:S(2)}) copy-start(f32[3,3,224]{2,1,0:T(4,128)} %param.11) | copy-start | bytes 24196
  0.0 8.1 %copy-start.8 = (f32[3]{0:T(128)S(1)}, f32[3]{0:T(128)}, u32[]{:S(2)}) copy-start(f32[3]{0:T(128)} %param.14) | copy-start | bytes 40
  0.0 9.7 %copy-start.9 = (f32[3]{0:T(128)S(1)}, f32[3]{0:T(128)}, u32[]{:S(2)}) copy-start(f32[3]{0:T(128)} %param.13) | copy-start | bytes 40
  0.0 11.2 %copy-start.10 = (f32[3]{0:T(128)S(1)}, f32[3]{0:T(128)}, u32[]{:S(2)}) copy-start(f32[3]{0:T(128)} %param.15) | copy-start | bytes 40
  0.0 12.8 %copy-start.6 = (f32[224]{0:T(256)S(1)}, f32[224]{0:T(256)}, u32[]{:S(2)}) copy-start(f32[224]{0:T(256)} %param.12) | copy-start | bytes 2692
  0.0 12.8 %copy-start.7 = (f32[192]{0:T(256)S(1)}, f32[192]{0:T(256)}, u32[]{:S(2)}) copy-start(f32[192]{0:T(256)} %param.16) | copy-start | bytes 2308
  1.6 13.9 %collective-permute-start = (bf16[16,96]{1,0:T(8,128)(2,1)S(1)}, bf16[16,96]{1,0:T(8,128)(2,1)S(1)}, u32[]{:S(2)}, u32[]{:S(2)}) collective-permute-start(bf16[16,96]{1,0:T(8,128)(2,1)S(1)} %bitcast.18), channel_id=1, source_target_pairs={{0,1},{1,2},{2,3},{3,4},{4,5},{5,6},{6,7},{7,8},{8,9},{9,10},{10,1... | collective-permute-start | bytes 9224 | tf_op jit(solution)/shard_map/ppermute | solution.py:273
  5.8 9.8 %collective-permute-start.1 = (bf16[16,96]{1,0:T(8,128)(2,1)S(1)}, bf16[16,96]{1,0:T(8,128)(2,1)S(1)}, u32[]{:S(2)}, u32[]{:S(2)}) collective-permute-start(bf16[16,96]{1,0:T(8,128)(2,1)S(1)} %bitcast.19), channel_id=1, source_target_pairs={{1,0},{2,1},{3,2},{4,3},{5,4},{6,5},{7,6},{8,7},{9,8},{10,9},{11,1... | collective-permute-start | bytes 9224 | tf_op jit(solution)/shard_map/ppermute | solution.py:274
  15.6 6.0 %collective-permute-start.3 = (bf16[112,128]{1,0:T(8,128)(2,1)S(1)}, bf16[112,128]{1,0:T(8,128)(2,1)S(1)}, u32[]{:S(2)}, u32[]{:S(2)}) collective-permute-start(bf16[112,128]{1,0:T(8,128)(2,1)S(1)} %pad_maximum_fusion.1), channel_id=1, source_target_pairs={{32,0},{64,32},{96,64},{128,96},{160,128},{192,160},{224,192},{33,... | collective-permute-start | bytes 86024 | tf_op jit(solution)/shard_map/ppermute | solution.py:281
  18.5 4.1 %collective-permute-start.2 = (bf16[112,128]{1,0:T(8,128)(2,1)S(1)}, bf16[112,128]{1,0:T(8,128)(2,1)S(1)}, u32[]{:S(2)}, u32[]{:S(2)}) collective-permute-start(bf16[112,128]{1,0:T(8,128)(2,1)S(1)} %pad_maximum_fusion), channel_id=1, source_target_pairs={{0,32},{32,64},{64,96},{96,128},{128,160},{160,192},{192,224},{1,3... | collective-permute-start | bytes 86024 | tf_op jit(solution)/shard_map/ppermute | solution.py:280
  21.6 1.6 copy-start.3
  22.6 0.6 copy-start.4
  134.2 4.5 %copy-start.2 = (bf16[192,96]{1,0:T(8,128)(2,1)S(1)}, bf16[192,96]{1,0:T(8,128)(2,1)}, u32[]{:S(2)}) copy-start(bf16[192,96]{1,0:T(8,128)(2,1)} %param.17) | copy-start | bytes 110596
  134.2 25.2 %all-to-all-start.3 = ((f32[8,384,128]{2,1,0:T(8,128)}), f32[8,384,128]{2,1,0:T(8,128)S(1)}, u32[]{:S(2)}, u32[]{:S(2)}) async-start(f32[8,384,128]{2,1,0:T(8,128)} %shard_map.94), calls=%async_computation.3 | async-start | bytes 3145728 | tf_op jit(solution)/shard_map/all_to_all | solution.py:357
  159.5 1.1 copy-start

commit v2 on v0

v2 whole, which is shorter than its diff:
```python
import functools

import jax
import jax.numpy as jnp
from jax import lax
from jax.experimental import pallas as pl
from jax.experimental.pallas import tpu as pltpu
from jax.sharding import PartitionSpec as P

f32, bf16 = jnp.float32, jnp.bfloat16
norm_eps = 1e-05
ROWS, COLS, WIDTH, LANES = 16, 128, 96, 128
INNER, STATE, HALF = 192, 16, 64
BLOCK, BLOCKS, GROUP = 16, 8, 4
HALVED, CHIPS = BLOCKS // 2, 4
PIECE, PIECE_OUT = (BLOCK * 26, LANES), (BLOCK * 24, LANES)
PLANE = (ROWS, 2, COLS, LANES)
VMEM = 12 * 1024 * 1024


def silu(v):
    return v / (1.0 + jnp.exp(-v))


def split(v):
    high = v.astype(bf16)
    return high, (v - high.astype(f32)).astype(bf16)


def dot(a, b, dims):
    return lax.dot_general(a, b, (dims, ((), ())), preferred_element_type=f32)


def low_lanes(rows=8):
    return lax.broadcasted_iota(jnp.int32, (rows, LANES), 1) < HALF


def by_head(values, g):
    if g == 1:
        return jnp.full((1, LANES), values[2], f32)
    return jnp.where(low_lanes(1), values[0], values[1])


def fold_sublanes(parts):
    place = lax.broadcasted_iota(jnp.int32, (8, LANES), 0)
    step = 1
    while len(parts) > 1:
        first = (place & step) == 0
        parts = [
            jnp.where(first, a, b) + pltpu.roll(jnp.where(first, b, a), 8 - step, 0)
            for a, b in zip(parts[0::2], parts[1::2])
        ]
        step *= 2
    return parts[0]


def each_row(body, together):
    def some(k, carry):
        for i in range(together):
            body(k * together + i)
        return carry

    lax.fori_loop(0, ROWS // together, some, 0)


def spread(values, q, j):
    return jnp.broadcast_to(values[8 * q : 8 * q + 8, j : j + 1], (8, LANES))


def entry_kernel(
    tok,
    above,
    below,
    left,
    right,
    in_weight,
    conv_weight,
    conv_bias,
    step_bias,
    decay_log,
    xdt,
    decay,
    act,
    gate,
    bct,
    cmap,
    ends,
    proj,
    weight,
    taps,
    compact,
    totals,
):
    source = in_weight[...].astype(f32)
    chan_b, chan_c = source[:, 384:400], source[:, 400:416]
    step_w = [jnp.broadcast_to(source[:, 416 + h : 417 + h], (WIDTH, HALF)) for h in range(3)]
    wide = [
        source[:, 192:384],
        chan_c,
        chan_c,
        chan_b,
        jnp.zeros((WIDTH, 16), f32),
        step_w[0],
        step_w[1],
        step_w[2],
        step_w[2],
        source[:, 0:192],
        jnp.zeros((WIDTH, HALF), f32),
    ]
    weight[...] = jnp.concatenate(wide, axis=1).astype(bf16)
    step_turned = jnp.concatenate([source[:, 416:419], jnp.zeros((WIDTH, 125), f32)], axis=1)
    step_turned = step_turned.T[0:8, :].astype(bf16)
    for ref, at, size in ((conv_weight, 0, 9), (conv_bias, 9, 1)):
        v = ref[...]
        taps[0, at : at + size, :] = v[:, 0:128]
        tail = [v[:, 128:192], v[:, 208:224], v[:, 208:224], v[:, 192:208]]
        taps[1, at : at + size, :] = jnp.concatenate(tail + [jnp.zeros((size, 16), f32)], axis=1)

    def conv_part(tokens, dims):
        return dot(tokens, weight[:, 0:256], dims).astype(bf16).astype(f32)

    def softplus(v):
        return jnp.maximum(v, 0.0) + jnp.log1p(jnp.exp(-jnp.abs(v)))

    for at, ref in ((0, above), (ROWS + 1, below)):
        out = conv_part(ref[0:WIDTH, :], ((0,), (0,)))
        sides = conv_part(ref[WIDTH:, 0:WIDTH], ((1,), (0,)))
        for g in range(2):
            proj[at, g, 8:136, :] = out[:, g * 128 : g * 128 + 128]
            proj[at, g, 7:8, :] = sides[0:1, g * 128 : g * 128 + 128]
            proj[at, g, 136:137, :] = sides[1:2, g * 128 : g * 128 + 128]
    for ref, at in ((left, 7), (right, 136)):
        out = conv_part(ref[...], ((1,), (0,)))
        for g in range(2):
            proj[1 : ROWS + 1, g, at, :] = out[:, g * 128 : g * 128 + 128]

    def own_row(r):
        out = dot(tok[r], weight[...], ((0,), (0,))).astype(bf16)
        compact[r] = dot(step_turned, tok[r], ((1,), (0,))).astype(bf16).astype(f32)
        for g in range(2):
            proj[r + 1, g, 8:136, :] = out[:, g * 128 : g * 128 + 128].astype(f32)
            gate[r, g] = out[:, 512 + g * 128 : 640 + g * 128]
            raw = out[:, 256 + g * 128 : 384 + g * 128].astype(f32) + by_head(step_bias, g)
            xdt[r, g] = softplus(raw)

    each_row(own_row, 4)

    head = lax.broadcasted_iota(jnp.int32, (8, LANES), 0)

    def head_rows(ref):
        return jnp.where(head == 0, ref[0], jnp.where(head == 1, ref[1], ref[2]))

    step = softplus(compact[...] + head_rows(step_bias))
    log_decay = (-jnp.exp(head_rows(decay_log)) * step).reshape(ROWS * 8, LANES)
    log_decay = jnp.concatenate(split(log_decay), axis=1)
    from_at = lax.broadcasted_iota(jnp.int32, (2 * COLS, COLS), 0) & (COLS - 1)
    to_at = lax.broadcasted_iota(jnp.int32, (2 * COLS, COLS), 1)
    later = jnp.where(from_at > to_at, 1.0, 0.0).astype(bf16)
    suffix = dot(log_decay, later, ((1,), (0,)))
    whole = dot(log_decay, jnp.ones((2 * COLS, COLS), bf16), ((1,), (0,)))
    compact[...] = step * jnp.exp(suffix).reshape(ROWS, 8, LANES)
    totals[...] = jnp.exp(whole).reshape(ROWS, 8, LANES)
    rate = [-jnp.exp(by_head(decay_log, g)) for g in range(2)]

    def conv_row(r):
        parts = []
        for g in range(2):
            acc = jnp.broadcast_to(taps[g, 9:10, :], (COLS, LANES))
            for a in range(3):
                for b in range(3):
                    k = a * 3 + b
                    acc = acc + taps[g, k : k + 1, :] * proj[r + a, g, 7 + b : 135 + b, :]
            parts.append(silu(acc).astype(bf16).astype(f32))
        turned = parts[1].T
        chan_b = turned[96:112, :]
        bct[r, 0:16, :] = chan_b
        bct[r, 16:32, :] = turned[64:80, :]
        other = pltpu.roll(parts[1], HALF, 1)
        cmap[:, r, :] = other
        parts[1] = jnp.where(low_lanes(COLS), parts[1], other)
        for g in range(2):
            act[r, g] = parts[g].astype(bf16)
            step = xdt[r, g]
            xdt[r, g] = step * parts[g]
            decay[r, g] = jnp.exp(rate[g] * step)
        weighted = [compact[r, h : h + 1, :] * chan_b for h in range(3)]
        weighted = jnp.concatenate(split(jnp.concatenate(weighted, axis=0)), axis=0)
        inner = jnp.concatenate([act[r, 0], act[r, 1]], axis=1)
        state = dot(weighted, inner, ((1,), (0,)))
        state = state[0:48, :] + state[48:96, :]
        low = low_lanes(16)
        first = jnp.where(low, state[0:16, 0:128], state[16:32, 0:128])
        third = jnp.where(low_lanes(), state[32:40, 128:256], state[40:48, 128:256])
        total = jnp.where(low_lanes(1), totals[r, 0:1, :], totals[r, 1:2, :])
        rest = jnp.concatenate([total, totals[r, 2:3, :], jnp.zeros((2, LANES), f32)], axis=0)
        ends[2 * r] = jnp.concatenate([first[0:8, :], third[0:4, :], rest], axis=0)
        ends[2 * r + 1] = jnp.concatenate([first[8:16, :], third[4:8, :], rest], axis=0)

    each_row(conv_row, 2)


def row_prefix_kernel(parts, out):
    count = parts.shape[0]
    first = jnp.zeros((8, LANES), f32)
    second = jnp.zeros((8, LANES), f32)
    for s in range(count):
        out[s, 0:8, :] = first
        out[s, 8:16, :] = second
        first = parts[s, 12:13, :] * first + parts[s, 0:8, :]
        second = parts[s, 13:14, :] * second + parts[s, 8:16, :]


def starts(carry, r):
    third = jnp.concatenate([carry[2 * r, 8:12, :], carry[2 * r + 1, 8:12, :]], axis=0)
    return [carry[2 * r, 0:8, :], carry[2 * r + 1, 0:8, :], third]


def bottom_kernel(xdt, decay, bct, carry, mine, theirs, hold):
    core = lax.axis_index("gy") % 2
    low = low_lanes()
    begin = []
    for r in range(ROWS):
        begin += starts(carry, r)

    def block(cb, state):
        state = list(state)
        base = pl.multiple_of(cb * BLOCK, BLOCK)
        maps = [pltpu.roll(bct[r, 0:16, :], COLS - base, 1) for r in range(ROWS)]
        for j in range(BLOCK):
            cols = [jnp.zeros((8, LANES), f32)] * 3
            for r in range(ROWS):
                wide = [spread(maps[r], q, j) for q in range(2)]
                wide.append(jnp.where(low, wide[0], wide[1]))
                x = [xdt[r, g, pl.ds(base + j, 8, stride=0), :] for g in range(2)]
                d = [decay[r, g, pl.ds(base + j, 8, stride=0), :] for g in range(2)]
                for q in range(3):
                    g = q // 2
                    state[3 * r + q] = d[g] * state[3 * r + q] + x[g] * wide[q]
                    cols[q] = d[g] * cols[q] + state[3 * r + q]
            for q in range(3):
                hold[j * 24 + 8 * q : j * 24 + 8 * q + 8, :] = cols[q]
        for g in range(2):
            product = decay[0, g, pl.ds(base, BLOCK), :]
            for r in range(1, ROWS):
                product = product * decay[r, g, pl.ds(base, BLOCK), :]
            hold[384 + 16 * g : 400 + 16 * g, :] = product

        @pl.when(cb // HALVED == core)
        def _():
            mine[cb % HALVED] = hold[...]

        @pl.when(cb // HALVED != core)
        def _():
            theirs[cb % HALVED] = hold[...]

        return tuple(state)

    lax.fori_loop(0, BLOCKS, block, tuple(begin))


def local_kernel(begins, xdt, decay, bct, carry, act, gate, skip_gain, *refs):
    if begins:
        track_in, gated_out, reach_out, track, local = refs
        track[...] = track_in[...]
    else:
        gated_out, reach_out, track, local = refs
        track[...] = jnp.zeros_like(track)
    low = low_lanes()

    def group(at, _):
        rg = begins // GROUP + at
        begin = []
        for i in range(GROUP):
            begin += starts(carry, rg * GROUP + i)

        def block(cb, state):
            state = list(state)
            base = cb * BLOCK
            maps = [pltpu.roll(bct[rg * GROUP + i], COLS - base, 1) for i in range(GROUP)]
            for j in range(BLOCK):
                cols = [track[cb, j * 24 + 8 * q : j * 24 + 8 * q + 8, :] for q in range(3)]
                reads = []
                for i in range(GROUP):
                    r = rg * GROUP + i
                    wide = [spread(maps[i], q, j) for q in range(4)]
                    b_all = [wide[0], wide[1], jnp.where(low, wide[0], wide[1])]
                    x = [xdt[r, g, pl.ds(base + j, 8, stride=0), :] for g in range(2)]
                    d = [decay[r, g, pl.ds(base + j, 8, stride=0), :] for g in range(2)]
                    for q in range(3):
                        g = q // 2
                        state[3 * i + q] = d[g] * state[3 * i + q] + x[g] * b_all[q]
                        cols[q] = d[g] * cols[q] + state[3 * i + q]
                    reads.append(wide[2] * cols[0] + wide[3] * cols[1])
                    reads.append(jnp.where(low, wide[2], wide[3]) * cols[2])
                for q in range(3):
                    track[cb, j * 24 + 8 * q : j * 24 + 8 * q + 8, :] = cols[q]
                local[at, :, base + j, :] = fold_sublanes(reads)
            return tuple(state)

        lax.fori_loop(0, BLOCKS, block, tuple(begin))
        return 0

    lax.fori_loop(0, ROWS // 2 // GROUP, group, 0)
    reach = [jnp.ones((COLS, LANES), f32)] * 2
    for r in range(begins):
        for g in range(2):
            reach[g] = reach[g] * decay[r, g]
    for i in range(ROWS // 2):
        r = begins + i
        for g in range(2):
            reach[g] = reach[g] * decay[r, g]
            mixed = local[i // GROUP, (i % GROUP) * 2 + g]
            if g == 1:
                mixed = mixed + pltpu.roll(mixed, HALF, 1)
            mixed = mixed + by_head(skip_gain, g) * act[r, g].astype(f32)
            gating = silu(gate[r, g].astype(f32))
            gated_out[i, g] = mixed * gating
            reach_out[i, g] = reach[g] * gating


def place():
    gy = lax.axis_index("gy")
    return gy % 2, gy // 2


def rows_of(j, q):
    return pl.ds(pl.multiple_of(j * 24 + 8 * q, 8), 8)


def decay_of(j, q):
    return pl.ds(BLOCK * (24 + q // 2) + j, 8, stride=0)


def join_kernel(mine, theirs, *outs):
    core, chip = place()
    for k, out in enumerate(outs):
        piece = (chip + k) % CHIPS

        def column(j, _):
            for q in range(3):
                a, b = mine[piece, rows_of(j, q), :], theirs[piece, rows_of(j, q), :]
                da, db = mine[piece, decay_of(j, q), :], theirs[piece, decay_of(j, q), :]
                out[rows_of(j, q), :] = jnp.where(core == 0, db * a + b, da * b + a)
            return 0

        lax.fori_loop(0, BLOCK, column, 0, unroll=4)
        rest = pl.ds(BLOCK * 24, BLOCK * 2)
        out[rest, :] = mine[piece, rest, :] * theirs[piece, rest, :]


def col_prefix_kernel(*refs):
    parts, outs, held, ready = refs[:CHIPS], refs[CHIPS : 2 * CHIPS], refs[-2], refs[-1]
    _, chip = place()
    for k, part in enumerate(parts):
        held[(chip + CHIPS - k) % CHIPS] = part[...]

    def column(j, _):
        for q in range(3):
            state = jnp.zeros((8, LANES), f32)
            for s in range(CHIPS):
                ready[s, rows_of(j, q), :] = state
                state = held[s, decay_of(j, q), :] * state + held[s, rows_of(j, q), :]
        return 0

    lax.fori_loop(0, BLOCK, column, 0, unroll=4)
    for k, out in enumerate(outs):
        out[...] = ready[(chip + k) % CHIPS]


def share_kernel(*refs):
    parts, (mine, theirs, own, other) = refs[:CHIPS], refs[CHIPS:]
    core, chip = place()
    for k, part in enumerate(parts):
        piece = (chip + CHIPS - k) % CHIPS

        def column(j, _):
            for q in range(3):
                upper = part[rows_of(j, q), :]
                a, b = mine[piece, rows_of(j, q), :], theirs[piece, rows_of(j, q), :]
                da, db = mine[piece, decay_of(j, q), :], theirs[piece, decay_of(j, q), :]
                lower = jnp.where(core == 0, da * upper + a, db * upper + b)
                own[piece, rows_of(j, q), :] = jnp.where(core == 0, upper, lower)
                other[piece, rows_of(j, q), :] = jnp.where(core == 0, lower, upper)
            return 0

        lax.fori_loop(0, BLOCK, column, 0, unroll=4)


def exit_kernel(
    own, other, cmap, gated_a, reach_a, gated_b, reach_b, norm_gain, out_weight, out, carried
):
    low = low_lanes()
    core, _ = place()

    def block(k, _, states, half):
        for j in range(BLOCK):
            first, second, third = [
                states[k, j * 24 + 8 * q : j * 24 + 8 * q + 8, :] for q in range(3)
            ]
            turned = pltpu.roll(third, HALF, 1)
            right = [jnp.where(low, third, turned), jnp.where(low, turned, third)]
            whole = jnp.concatenate(
                [
                    jnp.concatenate([first, second], axis=0),
                    jnp.concatenate(right, axis=0),
                ],
                axis=1,
            )
            c = ((core ^ half) * HALVED + k) * BLOCK + j
            reads = cmap[c][:, 0:32].astype(bf16)
            result = dot(reads, jnp.concatenate(split(whole), axis=0), ((1,), (0,)))
            for g in range(2):
                carried[:, g, c, :] = result[:, g * 128 : g * 128 + 128]
        return 0

    for half, states in enumerate((own, other)):
        lax.fori_loop(0, HALVED, functools.partial(block, states=states, half=half), 0)
    turned = out_weight[...].astype(f32).T
    weight = jnp.concatenate([turned, jnp.zeros((WIDTH, HALF), f32)], axis=1).astype(bf16)
    pad = jnp.zeros((1, HALF), f32)
    gain = [norm_gain[:, 0:128], jnp.concatenate([norm_gain[:, 128:192], pad], axis=1)]

    def row(r, begins, gated, reach):
        i = r - begins
        parts = [gated[i, g] + reach[i, g] * carried[r, g] for g in range(2)]
        total = jnp.sum(parts[0] * parts[0] + parts[1] * parts[1], axis=1, keepdims=True)
        scale = lax.rsqrt(total * (1.0 / INNER) + norm_eps)
        normed = [(parts[g] * scale * gain[g]).astype(bf16) for g in range(2)]
        result = dot(weight, jnp.concatenate(normed, axis=1), ((1,), (1,)))
        out[r] = result.astype(bf16)

    for begins, gated, reach in ((0, gated_a, reach_a), (ROWS // 2, gated_b, reach_b)):

        def some(k, carry):
            for i in range(4):
                row(begins + 4 * k + i, begins, gated, reach)
            return carry

        lax.fori_loop(0, ROWS // 8, some, 0)


def call(kernel, spaces, shapes, scratch, *operands, after=()):
    kinds = {"v": pltpu.VMEM, "s": pltpu.SMEM, "h": pl.ANY}
    first, waits = len(operands), len(after)
    spaces, operands = spaces + "h" * waits, operands + tuple(after)

    def inner(*refs):
        kernel(*refs[:first], *refs[first + waits :])

    return pl.pallas_call(
        inner,
        in_specs=[pl.BlockSpec(memory_space=kinds[k]) for k in spaces],
        out_specs=[pl.BlockSpec(memory_space=kinds[k]) for _, _, k in shapes],
        out_shape=[jax.ShapeDtypeStruct(s, t) for s, t, _ in shapes],
        scratch_shapes=scratch,
        compiler_params=pltpu.CompilerParams(vmem_limit_bytes=VMEM),
    )(*operands)


def steps(axis):
    count = lax.axis_size(axis)
    up = [(i, i + 1) for i in range(count - 1)]
    return up, [(j, i) for i, j in up]


def on_device(
    tokens,
    in_weight,
    conv_weight,
    conv_bias,
    step_bias,
    decay_log,
    skip_gain,
    norm_gain,
    out_weight,
):
    to_right, to_left = steps("gx")
    to_down, to_up = steps("gy")
    left = lax.ppermute(tokens[:, :, COLS - 1], "gx", to_right)
    right = lax.ppermute(tokens[:, :, 0], "gx", to_left)

    def edge(r):
        rest = jnp.pad(jnp.stack([left[r], right[r]]), ((0, 14), (0, LANES - WIDTH)))
        return jnp.concatenate([tokens[r], rest], axis=0)

    above = lax.ppermute(edge(ROWS - 1), "gy", to_down)
    below = lax.ppermute(edge(0), "gy", to_up)
    vmem = pltpu.VMEM
    xdt, decay, act, gate, bct, cmap, ends = call(
        entry_kernel,
        "vvvvvvvvss",
        [
            (PLANE, f32, "v"),
            (PLANE, f32, "v"),
            (PLANE, bf16, "v"),
            (PLANE, bf16, "v"),
            ((ROWS, 32, COLS), f32, "v"),
            ((COLS, ROWS, LANES), f32, "v"),
            ((2 * ROWS, 16, LANES), f32, "v"),
        ],
        [
            vmem((ROWS + 2, 2, 144, LANES), f32),
            vmem((WIDTH, 768), bf16),
            vmem((2, 16, LANES), f32),
            vmem((ROWS, 8, LANES), f32),
            vmem((ROWS, 8, LANES), f32),
        ],
        tokens,
        above,
        below,
        left,
        right,
        in_weight,
        conv_weight.reshape(9, 224),
        conv_bias.reshape(1, 224),
        step_bias,
        decay_log,
    )
    ends = lax.all_to_all(ends, "gx", 0, 0)
    (carry,) = call(row_prefix_kernel, "v", [((2 * ROWS, 16, LANES), f32, "v")], [], ends)
    carry = lax.all_to_all(carry, "gx", 0, 0)
    piece, piece_out = (PIECE, f32, "v"), (PIECE_OUT, f32, "v")
    halves = ((HALVED,) + PIECE, f32, "v")
    mine, theirs = call(
        bottom_kernel, "vvvv", [halves] * 2, [vmem(PIECE, f32)], xdt, decay, bct, carry
    )
    gy_count = lax.axis_size("gy")
    swap = [(i, i ^ 1) for i in range(gy_count)]
    ahead = [[(i, (i + 2 * k) % gy_count) for i in range(gy_count)] for k in range(CHIPS)]

    def rotate(pieces):
        return [pieces[0]] + [lax.ppermute(pieces[k], "gy", ahead[k]) for k in range(1, CHIPS)]

    theirs = lax.ppermute(theirs, "gy", swap)
    joined = call(join_kernel, "vv", [piece] * CHIPS, [], mine, theirs)
    pieces = rotate(joined)
    half = (ROWS // 2,) + PLANE[1:]
    local_scratch = vmem((ROWS // 2 // GROUP, 8, COLS, LANES), f32)
    inner = (xdt, decay, bct, carry, act, gate, skip_gain)
    gated_a, reach_a, track = call(
        functools.partial(local_kernel, 0),
        "vvvvvvs",
        [(half, f32, "v"), (half, f32, "v"), ((BLOCKS,) + PIECE_OUT, f32, "v")],
        [local_scratch],
        *inner,
        after=joined[:1],
    )
    pieces = call(
        col_prefix_kernel,
        "vvvv",
        [piece_out] * CHIPS,
        [vmem((CHIPS,) + PIECE, f32), vmem((CHIPS,) + PIECE_OUT, f32)],
        *pieces,
        after=(track,),
    )
    above_chip = pieces[0]
    pieces = rotate(pieces)
    gated_b, reach_b = call(
        functools.partial(local_kernel, ROWS // 2),
        "vvvvvvsv",
        [(half, f32, "v"), (half, f32, "v")],
        [vmem((BLOCKS,) + PIECE_OUT, f32), local_scratch],
        *inner,
        track,
        after=(above_chip,),
    )
    halves_out = ((HALVED,) + PIECE_OUT, f32, "v")
    own, other = call(
        share_kernel, "vvvvvv", [halves_out] * 2, [], *pieces, mine, theirs, after=(gated_b,)
    )
    other = lax.ppermute(other, "gy", swap)
    (out,) = call(
        exit_kernel,
        "vvvvvvvvv",
        [((ROWS, WIDTH, COLS), bf16, "v")],
        [vmem(PLANE, f32)],
        own,
        other,
        cmap,
        gated_a,
        reach_a,
        gated_b,
        reach_b,
        norm_gain.reshape(1, INNER),
        out_weight,
    )
    return out


def solution(mesh):
    return jax.shard_map(
        on_device,
        mesh=mesh,
        in_specs=(P("gy", None, "gx"), P(), P(), P(), P(), P(), P(), P(), P()),
        out_specs=P("gy", None, "gx"),
        check_vma=False,
    )
```

time: 433 us -> 117 us (0.27)
  the two profiles are of different devices: /device:TPU:27 before, /device:TPU:1 now
where the time goes in v2:
time: 117 us
  blocking collectives  42 us (36%)
  Pallas kernels  38.2 us (33%)
  starting transfers between devices  26.8 us (23%)
  waiting for transfers between devices  7.85 us (7%)
  local copies, waits for them, and re-layouts  1.8 us (2%)
    pallas_call x9, Pallas kernels, call(): pl.pallas_call(inner, in_specs=[pl.BlockSpec(memory_space=kinds[k]) for k...  38.2 us
    all_to_all x1, blocking collectives, on_device(): ends = lax.all_to_all(ends, 'gx', 0, 0)  25.9 us
    all_to_all x1, blocking collectives, on_device(): carry = lax.all_to_all(carry, 'gx', 0, 0)  16.1 us
    ppermute x6, starting transfers between devices, rotate(): lax.ppermute(pieces[k], 'gy', ahead[k])  10.2 us
    ppermute x1, starting transfers between devices, on_device(): above = lax.ppermute(edge(ROWS - 1), 'gy', to_down)  5.14 us
    ppermute x1, starting transfers between devices, on_device(): left = lax.ppermute(tokens[:, :, COLS - 1], 'gx', to_right)  4.57 us
    ppermute x1, waiting for transfers between devices, on_device(): below = lax.ppermute(edge(0), 'gy', to_up)  3.23 us
    ppermute x1, starting transfers between devices, on_device(): other = lax.ppermute(other, 'gy', swap)  2.4 us
  transfers between devices with their start and end apart: 12, of which 4 were waited for; matrix products, arithmetic and copies ran while one was open for 0% of the time, Pallas kernels for 15%

profile of v2, /device:TPU:1, one launch (start us, length us, event | category | flops | bytes accessed | tf_op | source)
XLA Modules:
  0.0 116.9 jit_solution(10940300342674607162)
XLA Ops:
  0.0 1.3 %fusion.11 = (bf16[16,96,1]{2,1,0:T(8,128)(2,1)S(1)}, bf16[16,96,1]{2,1,0:T(8,128)(2,1)S(1)}) fusion(bf16[16,96,128]{2,1,0:T(8,128)(2,1)} %refs_0_.1), kind=kLoop, calls=%fused_computation.17 | loop fusion | bytes 12288 | tf_op jit(solution)/shard_map/slice | solution.py:479
  1.4 0.2 copy.13
  1.6 1.3 %collective-permute-start.1 = (bf16[16,96]{1,0:T(8,128)(2,1)S(1)}, bf16[16,96]{1,0:T(8,128)(2,1)S(1)}, u32[]{:S(2)}, u32[]{:S(2)}) collective-permute-start(bf16[16,96]{1,0:T(8,128)(2,1)S(1)} %bitcast.10), channel_id=1, source_target_pairs={{1,0},{2,1},{3,2},{4,3},{5,4},{6,5},{7,6},{8,7},{9,8},{10,9},{11,1... | collective-permute-start | bytes 9224 | tf_op jit(solution)/shard_map/ppermute | solution.py:480
  2.9 0.2 copy.12
  3.1 4.6 %collective-permute-start = (bf16[16,96]{1,0:T(8,128)(2,1)S(1)}, bf16[16,96]{1,0:T(8,128)(2,1)S(1)}, u32[]{:S(2)}, u32[]{:S(2)}) collective-permute-start(bf16[16,96]{1,0:T(8,128)(2,1)S(1)} %bitcast.11), channel_id=1, source_target_pairs={{0,1},{1,2},{2,3},{3,4},{4,5},{5,6},{6,7},{7,8},{8,9},{9,10},{10,1... | collective-permute-start | bytes 9224 | tf_op jit(solution)/shard_map/ppermute | solution.py:479
  7.7 0.7 collective-permute-done.refs_3_
  8.4 5.1 %collective-permute-start.2 = (bf16[112,128]{1,0:T(8,128)(2,1)S(1)}, bf16[112,128]{1,0:T(8,128)(2,1)S(1)}, u32[]{:S(2)}, u32[]{:S(2)}) collective-permute-start(bf16[112,128]{1,0:T(8,128)(2,1)S(1)} %pad_maximum_fusion), channel_id=1, source_target_pairs={{0,32},{32,64},{64,96},{96,128},{128,160},{160,192},{192,224},{1,3... | collective-permute-start | bytes 86024 | tf_op jit(solution)/shard_map/ppermute | solution.py:486
  13.6 1.9 %collective-permute-start.3 = (bf16[112,128]{1,0:T(8,128)(2,1)S(1)}, bf16[112,128]{1,0:T(8,128)(2,1)S(1)}, u32[]{:S(2)}, u32[]{:S(2)}) collective-permute-start(bf16[112,128]{1,0:T(8,128)(2,1)S(1)} %pad_maximum_fusion.1), channel_id=1, source_target_pairs={{32,0},{64,32},{96,64},{128,96},{160,128},{192,160},{224,192},{33,... | collective-permute-start | bytes 86024 | tf_op jit(solution)/shard_map/ppermute | solution.py:487
  15.6 3.2 %collective-permute-done.3.refs_2_ = bf16[112,128]{1,0:T(8,128)(2,1)S(1)} collective-permute-done((bf16[112,128]{1,0:T(8,128)(2,1)S(1)}, bf16[112,128]{1,0:T(8,128)(2,1)S(1)}, u32[]{:S(2)}, u32[]{:S(2)}) %collective-permute-start.3) | collective-permute-done | bytes 28704 | tf_op jit(solution)/shard_map/ppermute | solution.py:487
  18.8 7.6 %shard_map.91 = (f32[16,2,128,128]{3,2,1,0:T(8,128)S(1)}, f32[16,2,128,128]{3,2,1,0:T(8,128)S(1)}, bf16[16,2,128,128]{3,2,1,0:T(8,128)(2,1)S(1)}, bf16[16,2,128,...) custom-call(bf16[16,96,128]{2,1,0:T(8,128)(2,1)S(1)} %copy-done, ...), custom_call_target="tpu_custom_call" | custom-call | tf_op jit(solution)/shard_map/pallas_call | solution.py:450
  26.4 25.9 %all_to_all.10.refs_0_ = f32[32,16,128]{2,1,0:T(8,128)S(1)} all-to-all(f32[32,16,128]{2,1,0:T(8,128)S(1)} %get-tuple-element.32), channel_id=1, replica_groups=mesh['gy'=8,'gx'=32] {'gx'}, dimensions={0} | all-to-all | bytes 524288 | tf_op jit(solution)/shard_map/all_to_all | solution.py:519
  52.2 0.1 shard_map.92
  52.3 16.1 %all_to_all.11.refs_3_ = f32[32,16,128]{2,1,0:T(8,128)S(1)} all-to-all(f32[32,16,128]{2,1,0:T(8,128)S(1)} %shard_map.92), channel_id=1, replica_groups=mesh['gy'=8,'gx'=32] {'gx'}, dimensions={0} | all-to-all | bytes 524288 | tf_op jit(solution)/shard_map/all_to_all | solution.py:521
  68.4 7.0 %shard_map.93 = (f32[4,416,128]{2,1,0:T(8,128)S(1)}, f32[4,416,128]{2,1,0:T(8,128)S(1)}) custom-call(f32[16,2,128,128]{3,2,1,0:T(8,128)S(1)} %get-tuple-element.29.refs_0_, f32[16,2,128,128]{3,2,1,0:T(8,128)S(1)} %get-tuple-element.30.refs_1_, f32[16,32,128]{2,1,0:T(8,128)S(1)} %get-tuple-element.31.refs_2_, f32[32,16,128]{2,1,0:T(8,128)S(1)} %all_to_all.11.refs_3_), custom_call_target="tpu_custom_call" | custom-call | tf_op jit(solution)/shard_map/pallas_call | solution.py:450
  75.4 1.3 %collective-permute-start.4 = (f32[4,416,128]{2,1,0:T(8,128)S(1)}, f32[4,416,128]{2,1,0:T(8,128)S(1)}, u32[]{:S(2)}, u32[]{:S(2)}) collective-permute-start(f32[4,416,128]{2,1,0:T(8,128)S(1)} %get-tuple-element.34), channel_id=1, source_target_pairs={{0,32},{32,0},{64,96},{96,64},{128,160},{160,128},{192,224},{224,1... | collective-permute-start | bytes 2555912 | tf_op jit(solution)/shard_map/ppermute | solution.py:534
  76.7 2.0 %collective-permute-done.4.refs_1_.refs_5_ = f32[4,416,128]{2,1,0:T(8,128)S(1)} collective-permute-done((f32[4,416,128]{2,1,0:T(8,128)S(1)}, f32[4,416,128]{2,1,0:T(8,128)S(1)}, u32[]{:S(2)}, u32[]{:S(2)}) %collective-permute-start.4) | collective-permute-done | bytes 852000 | tf_op jit(solution)/shard_map/ppermute | solution.py:534
  78.7 0.2 shard_map.94
  78.9 2.6 %collective-permute-start.5 = (f32[416,128]{1,0:T(8,128)S(1)}, f32[416,128]{1,0:T(8,128)S(1)}, u32[]{:S(2)}, u32[]{:S(2)}) collective-permute-start(f32[416,128]{1,0:T(8,128)S(1)} %get-tuple-element.36), channel_id=1, source_target_pairs={{0,64},{32,96},{64,128},{96,160},{128,192},{160,224},{192,0},{224,... | collective-permute-start | bytes 638984 | tf_op jit(solution)/shard_map/ppermute | solution.py:532
  81.5 1.7 %collective-permute-start.6 = (f32[416,128]{1,0:T(8,128)S(1)}, f32[416,128]{1,0:T(8,128)S(1)}, u32[]{:S(2)}, u32[]{:S(2)}) collective-permute-start(f32[416,128]{1,0:T(8,128)S(1)} %get-tuple-element.37), channel_id=1, source_target_pairs={{0,128},{32,160},{64,192},{96,224},{128,0},{160,32},{192,64},{224,... | collective-permute-start | bytes 638984 | tf_op jit(solution)/shard_map/ppermute | solution.py:532
  83.1 2.0 %collective-permute-start.7 = (f32[416,128]{1,0:T(8,128)S(1)}, f32[416,128]{1,0:T(8,128)S(1)}, u32[]{:S(2)}, u32[]{:S(2)}) collective-permute-start(f32[416,128]{1,0:T(8,128)S(1)} %get-tuple-element.38), channel_id=1, source_target_pairs={{0,192},{32,224},{64,0},{96,32},{128,64},{160,96},{192,128},{224,1... | collective-permute-start | bytes 638984 | tf_op jit(solution)/shard_map/ppermute | solution.py:532
  85.1 8.6 %shard_map.95 = (f32[8,2,128,128]{3,2,1,0:T(8,128)S(1)}, f32[8,2,128,128]{3,2,1,0:T(8,128)S(1)}, f32[8,384,128]{2,1,0:T(8,128)S(1)}) custom-call(f32[16,2,128,128]{3,2,1,0:T(8,128)S(1)} %get-tuple-element.29.refs_0_, f32[16,2,128,128]{3,2,1,0:T(8,128)S(1)} %get-tuple-element.30.refs_1_, f32[16,32,128]{2,1,0:T(8,128)S(1)} %get-tuple-element.31.refs_2_, ...), custom_call_target="tpu_custom_call" | custom-call | tf_op jit(solution)/shard_map/pallas_call | solution.py:450
  93.7 0.2 shard_map.96
  94.0 0.1 collective-permute-start.8
  94.1 2.8 %collective-permute-start.9 = (f32[384,128]{1,0:T(8,128)S(1)}, f32[384,128]{1,0:T(8,128)S(1)}, u32[]{:S(2)}, u32[]{:S(2)}) collective-permute-start(f32[384,128]{1,0:T(8,128)S(1)} %get-tuple-element.44), channel_id=1, source_target_pairs={{0,128},{32,160},{64,192},{96,224},{128,0},{160,32},{192,64},{224,... | collective-permute-start | bytes 589832 | tf_op jit(solution)/shard_map/ppermute | solution.py:532
  96.8 1.2 %collective-permute-start.10 = (f32[384,128]{1,0:T(8,128)S(1)}, f32[384,128]{1,0:T(8,128)S(1)}, u32[]{:S(2)}, u32[]{:S(2)}) collective-permute-start(f32[384,128]{1,0:T(8,128)S(1)} %get-tuple-element.45), channel_id=1, source_target_pairs={{0,192},{32,224},{64,0},{96,32},{128,64},{160,96},{192,128},{224,1... | collective-permute-start | bytes 589832 | tf_op jit(solution)/shard_map/ppermute | solution.py:532
  98.0 8.6 %shard_map.97 = (f32[8,2,128,128]{3,2,1,0:T(8,128)S(1)}, f32[8,2,128,128]{3,2,1,0:T(8,128)S(1)}) custom-call(f32[16,2,128,128]{3,2,1,0:T(8,128)S(1)} %get-tuple-element.29.refs_0_, f32[16,2,128,128]{3,2,1,0:T(8,128)S(1)} %get-tuple-element.30.refs_1_, f32[16,32,128]{2,1,0:T(8,128)S(1)} %get-tuple-element.31.refs_2_, f32[32,16,128]{2,1,0:T(8,128)S(1)} %all_to_all.11.refs_3_, ...), custom_call_target="tpu_custom_call" | custom-call | tf_op jit(solution)/shard_map/pallas_call | solution.py:450
  106.6 0.0 copy-start.2
  106.6 0.0 copy-start.5
  106.7 0.3 shard_map.98
  107.0 2.4 %collective-permute-start.11 = (f32[4,384,128]{2,1,0:T(8,128)S(1)}, f32[4,384,128]{2,1,0:T(8,128)S(1)}, u32[]{:S(2)}, u32[]{:S(2)}) collective-permute-start(f32[4,384,128]{2,1,0:T(8,128)S(1)} %get-tuple-element.48), channel_id=1, source_target_pairs={{0,32},{32,0},{64,96},{96,64},{128,160},{160,128},{192,224},{224,1... | collective-permute-start | bytes 2359304 | tf_op jit(solution)/shard_map/ppermute | solution.py:571
  109.4 1.9 %collective-permute-done.11.refs_1_ = f32[4,384,128]{2,1,0:T(8,128)S(1)} collective-permute-done((f32[4,384,128]{2,1,0:T(8,128)S(1)}, f32[4,384,128]{2,1,0:T(8,128)S(1)}, u32[]{:S(2)}, u32[]{:S(2)}) %collective-permute-start.11) | collective-permute-done | bytes 786464 | tf_op jit(solution)/shard_map/ppermute | solution.py:571
  111.4 5.6 %shard_map.99 = bf16[16,96,128]{2,1,0:T(8,128)(2,1)} custom-call(f32[4,384,128]{2,1,0:T(8,128)S(1)} %get-tuple-element.47.refs_0_, f32[4,384,128]{2,1,0:T(8,128)S(1)} %collective-permute-done.11.refs_1_, f32[128,16,128]{2,1,0:T(8,128)S(1)} %get-tuple-element.49.refs_2_, f32[8,2,128,128]{3,2,1,0:T(8,128)S(1)} %get-tuple-element.50.refs_3_, ...), custom_call_target="tpu_custom_call" | custom-call | tf_op jit(solution)/shard_map/pallas_call | solution.py:450
  (32 shorter events, 0.1 us)
Async XLA Ops:
  0.0 7.7 %copy-start = (bf16[16,96,128]{2,1,0:T(8,128)(2,1)S(1)}, bf16[16,96,128]{2,1,0:T(8,128)(2,1)}, u32[]{:S(2)}) copy-start(bf16[16,96,128]{2,1,0:T(8,128)(2,1)} %refs_0_.1) | copy-start | bytes 1179652
  0.0 15.5 %copy-start.8 = (f32[3,3,224]{2,1,0:T(4,128)S(1)}, f32[3,3,224]{2,1,0:T(4,128)}, u32[]{:S(2)}) copy-start(f32[3,3,224]{2,1,0:T(4,128)} %param.11) | copy-start | bytes 24196
  0.0 18.8 %copy-start.7 = (f32[3]{0:T(128)S(1)}, f32[3]{0:T(128)}, u32[]{:S(2)}) copy-start(f32[3]{0:T(128)} %refs_9_.1) | copy-start | bytes 40
  0.0 18.8 %copy-start.6 = (f32[3]{0:T(128)S(1)}, f32[3]{0:T(128)}, u32[]{:S(2)}) copy-start(f32[3]{0:T(128)} %refs_8_.2) | copy-start | bytes 40
  0.0 18.8 %copy-start.4 = (f32[224]{0:T(256)S(1)}, f32[224]{0:T(256)}, u32[]{:S(2)}) copy-start(f32[224]{0:T(256)} %param.12) | copy-start | bytes 2692
  0.0 18.8 %copy-start.1 = (bf16[96,419]{1,0:T(8,128)(2,1)S(1)}, bf16[96,419]{1,0:T(8,128)(2,1)}, u32[]{:S(2)}) copy-start(bf16[96,419]{1,0:T(8,128)(2,1)} %refs_5_.1) | copy-start | bytes 241348
  1.6 6.1 %collective-permute-start.1 = (bf16[16,96]{1,0:T(8,128)(2,1)S(1)}, bf16[16,96]{1,0:T(8,128)(2,1)S(1)}, u32[]{:S(2)}, u32[]{:S(2)}) collective-permute-start(bf16[16,96]{1,0:T(8,128)(2,1)S(1)} %bitcast.10), channel_id=1, source_target_pairs={{1,0},{2,1},{3,2},{4,3},{5,4},{6,5},{7,6},{8,7},{9,8},{10,9},{11,1... | collective-permute-start | bytes 9224 | tf_op jit(solution)/shard_map/ppermute | solution.py:480
  3.1 5.3 %collective-permute-start = (bf16[16,96]{1,0:T(8,128)(2,1)S(1)}, bf16[16,96]{1,0:T(8,128)(2,1)S(1)}, u32[]{:S(2)}, u32[]{:S(2)}) collective-permute-start(bf16[16,96]{1,0:T(8,128)(2,1)S(1)} %bitcast.11), channel_id=1, source_target_pairs={{0,1},{1,2},{2,3},{3,4},{4,5},{5,6},{6,7},{7,8},{8,9},{9,10},{10,1... | collective-permute-start | bytes 9224 | tf_op jit(solution)/shard_map/ppermute | solution.py:479
  8.4 7.1 %collective-permute-start.2 = (bf16[112,128]{1,0:T(8,128)(2,1)S(1)}, bf16[112,128]{1,0:T(8,128)(2,1)S(1)}, u32[]{:S(2)}, u32[]{:S(2)}) collective-permute-start(bf16[112,128]{1,0:T(8,128)(2,1)S(1)} %pad_maximum_fusion), channel_id=1, source_target_pairs={{0,32},{32,64},{64,96},{96,128},{128,160},{160,192},{192,224},{1,3... | collective-permute-start | bytes 86024 | tf_op jit(solution)/shard_map/ppermute | solution.py:486
  13.6 5.2 %collective-permute-start.3 = (bf16[112,128]{1,0:T(8,128)(2,1)S(1)}, bf16[112,128]{1,0:T(8,128)(2,1)S(1)}, u32[]{:S(2)}, u32[]{:S(2)}) collective-permute-start(bf16[112,128]{1,0:T(8,128)(2,1)S(1)} %pad_maximum_fusion.1), channel_id=1, source_target_pairs={{32,0},{64,32},{96,64},{128,96},{160,128},{192,160},{224,192},{33,... | collective-permute-start | bytes 86024 | tf_op jit(solution)/shard_map/ppermute | solution.py:487
  68.4 16.7 %copy-start.3 = (f32[3]{0:T(128)S(1)}, f32[3]{0:T(128)}, u32[]{:S(2)}) copy-start(f32[3]{0:T(128)} %refs_6_.3) | copy-start | bytes 40
  75.4 3.3 %collective-permute-start.4 = (f32[4,416,128]{2,1,0:T(8,128)S(1)}, f32[4,416,128]{2,1,0:T(8,128)S(1)}, u32[]{:S(2)}, u32[]{:S(2)}) collective-permute-start(f32[4,416,128]{2,1,0:T(8,128)S(1)} %get-tuple-element.34), channel_id=1, source_target_pairs={{0,32},{32,0},{64,96},{96,64},{128,160},{160,128},{192,224},{224,1... | collective-permute-start | bytes 2555912 | tf_op jit(solution)/shard_map/ppermute | solution.py:534
  78.9 14.8 %collective-permute-start.5 = (f32[416,128]{1,0:T(8,128)S(1)}, f32[416,128]{1,0:T(8,128)S(1)}, u32[]{:S(2)}, u32[]{:S(2)}) collective-permute-start(f32[416,128]{1,0:T(8,128)S(1)} %get-tuple-element.36), channel_id=1, source_target_pairs={{0,64},{32,96},{64,128},{96,160},{128,192},{160,224},{192,0},{224,... | collective-permute-start | bytes 638984 | tf_op jit(solution)/shard_map/ppermute | solution.py:532
  81.5 12.2 %collective-permute-start.6 = (f32[416,128]{1,0:T(8,128)S(1)}, f32[416,128]{1,0:T(8,128)S(1)}, u32[]{:S(2)}, u32[]{:S(2)}) collective-permute-start(f32[416,128]{1,0:T(8,128)S(1)} %get-tuple-element.37), channel_id=1, source_target_pairs={{0,128},{32,160},{64,192},{96,224},{128,0},{160,32},{192,64},{224,... | collective-permute-start | bytes 638984 | tf_op jit(solution)/shard_map/ppermute | solution.py:532
  83.1 10.6 %collective-permute-start.7 = (f32[416,128]{1,0:T(8,128)S(1)}, f32[416,128]{1,0:T(8,128)S(1)}, u32[]{:S(2)}, u32[]{:S(2)}) collective-permute-start(f32[416,128]{1,0:T(8,128)S(1)} %get-tuple-element.38), channel_id=1, source_target_pairs={{0,192},{32,224},{64,0},{96,32},{128,64},{160,96},{192,128},{224,1... | collective-permute-start | bytes 638984 | tf_op jit(solution)/shard_map/ppermute | solution.py:532
  94.0 12.7 %collective-permute-start.8 = (f32[384,128]{1,0:T(8,128)S(1)}, f32[384,128]{1,0:T(8,128)S(1)}, u32[]{:S(2)}, u32[]{:S(2)}) collective-permute-start(f32[384,128]{1,0:T(8,128)S(1)} %get-tuple-element.43), channel_id=1, source_target_pairs={{0,64},{32,96},{64,128},{96,160},{128,192},{160,224},{192,0},{224,... | collective-permute-start | bytes 589832 | tf_op jit(solution)/shard_map/ppermute | solution.py:532
  94.1 12.6 %collective-permute-start.9 = (f32[384,128]{1,0:T(8,128)S(1)}, f32[384,128]{1,0:T(8,128)S(1)}, u32[]{:S(2)}, u32[]{:S(2)}) collective-permute-start(f32[384,128]{1,0:T(8,128)S(1)} %get-tuple-element.44), channel_id=1, source_target_pairs={{0,128},{32,160},{64,192},{96,224},{128,0},{160,32},{192,64},{224,... | collective-permute-start | bytes 589832 | tf_op jit(solution)/shard_map/ppermute | solution.py:532
  96.8 9.9 %collective-permute-start.10 = (f32[384,128]{1,0:T(8,128)S(1)}, f32[384,128]{1,0:T(8,128)S(1)}, u32[]{:S(2)}, u32[]{:S(2)}) collective-permute-start(f32[384,128]{1,0:T(8,128)S(1)} %get-tuple-element.45), channel_id=1, source_target_pairs={{0,192},{32,224},{64,0},{96,32},{128,64},{160,96},{192,128},{224,1... | collective-permute-start | bytes 589832 | tf_op jit(solution)/shard_map/ppermute | solution.py:532
  106.6 4.7 %copy-start.2 = (bf16[192,96]{1,0:T(8,128)(2,1)S(1)}, bf16[192,96]{1,0:T(8,128)(2,1)}, u32[]{:S(2)}) copy-start(bf16[192,96]{1,0:T(8,128)(2,1)} %refs_8_.3) | copy-start | bytes 110596
  106.6 4.7 %copy-start.5 = (f32[192]{0:T(256)S(1)}, f32[192]{0:T(256)}, u32[]{:S(2)}) copy-start(f32[192]{0:T(256)} %param.16) | copy-start | bytes 2308
  107.0 4.3 %collective-permute-start.11 = (f32[4,384,128]{2,1,0:T(8,128)S(1)}, f32[4,384,128]{2,1,0:T(8,128)S(1)}, u32[]{:S(2)}, u32[]{:S(2)}) collective-permute-start(f32[4,384,128]{2,1,0:T(8,128)S(1)} %get-tuple-element.48), channel_id=1, source_target_pairs={{0,32},{32,0},{64,96},{96,64},{128,160},{160,128},{192,224},{224,1... | collective-permute-start | bytes 2359304 | tf_op jit(solution)/shard_map/ppermute | solution.py:571

commit v3 on v2

--- a/solution.py
+++ b/solution.py
@@ -11,7 +11,7 @@
 norm_eps = 1e-05
 ROWS, COLS, WIDTH, LANES = 16, 128, 96, 128
 INNER, STATE, HALF = 192, 16, 64
-BLOCK, BLOCKS, GROUP = 16, 8, 4
+BLOCK, BLOCKS = 16, 8
 HALVED, CHIPS = BLOCKS // 2, 4
 PIECE, PIECE_OUT = (BLOCK * 26, LANES), (BLOCK * 24, LANES)
 PLANE = (ROWS, 2, COLS, LANES)
@@ -67,29 +67,12 @@
     return jnp.broadcast_to(values[8 * q : 8 * q + 8, j : j + 1], (8, LANES))
 
 
-def entry_kernel(
-    tok,
-    above,
-    below,
-    left,
-    right,
-    in_weight,
-    conv_weight,
-    conv_bias,
-    step_bias,
-    decay_log,
-    xdt,
-    decay,
-    act,
-    gate,
-    bct,
-    cmap,
-    ends,
-    proj,
-    weight,
-    taps,
-    compact,
-    totals,
+def softplus(v):
+    return jnp.maximum(v, 0.0) + jnp.log1p(jnp.exp(-jnp.abs(v)))
+
+
+def project_kernel(
+    tok, in_weight, step_bias, decay_log, inner, gate, steps, compact, totals, conv_w, weight
 ):
     source = in_weight[...].astype(f32)
     chan_b, chan_c = source[:, 384:400], source[:, 400:416]
@@ -108,40 +91,18 @@
         jnp.zeros((WIDTH, HALF), f32),
     ]
     weight[...] = jnp.concatenate(wide, axis=1).astype(bf16)
+    conv_w[...] = weight[:, 0:256]
     step_turned = jnp.concatenate([source[:, 416:419], jnp.zeros((WIDTH, 125), f32)], axis=1)
     step_turned = step_turned.T[0:8, :].astype(bf16)
-    for ref, at, size in ((conv_weight, 0, 9), (conv_bias, 9, 1)):
-        v = ref[...]
-        taps[0, at : at + size, :] = v[:, 0:128]
-        tail = [v[:, 128:192], v[:, 208:224], v[:, 208:224], v[:, 192:208]]
-        taps[1, at : at + size, :] = jnp.concatenate(tail + [jnp.zeros((size, 16), f32)], axis=1)
-
-    def conv_part(tokens, dims):
-        return dot(tokens, weight[:, 0:256], dims).astype(bf16).astype(f32)
-
-    def softplus(v):
-        return jnp.maximum(v, 0.0) + jnp.log1p(jnp.exp(-jnp.abs(v)))
-
-    for at, ref in ((0, above), (ROWS + 1, below)):
-        out = conv_part(ref[0:WIDTH, :], ((0,), (0,)))
-        sides = conv_part(ref[WIDTH:, 0:WIDTH], ((1,), (0,)))
-        for g in range(2):
-            proj[at, g, 8:136, :] = out[:, g * 128 : g * 128 + 128]
-            proj[at, g, 7:8, :] = sides[0:1, g * 128 : g * 128 + 128]
-            proj[at, g, 136:137, :] = sides[1:2, g * 128 : g * 128 + 128]
-    for ref, at in ((left, 7), (right, 136)):
-        out = conv_part(ref[...], ((1,), (0,)))
-        for g in range(2):
-            proj[1 : ROWS + 1, g, at, :] = out[:, g * 128 : g * 128 + 128]
 
     def own_row(r):
         out = dot(tok[r], weight[...], ((0,), (0,))).astype(bf16)
         compact[r] = dot(step_turned, tok[r], ((1,), (0,))).astype(bf16).astype(f32)
         for g in range(2):
-            proj[r + 1, g, 8:136, :] = out[:, g * 128 : g * 128 + 128].astype(f32)
+            inner[r, g] = out[:, g * 128 : g * 128 + 128]
             gate[r, g] = out[:, 512 + g * 128 : 640 + g * 128]
             raw = out[:, 256 + g * 128 : 384 + g * 128].astype(f32) + by_head(step_bias, g)
-            xdt[r, g] = softplus(raw)
+            steps[r, g] = softplus(raw)
 
     each_row(own_row, 4)
 
@@ -160,6 +121,52 @@
     whole = dot(log_decay, jnp.ones((2 * COLS, COLS), bf16), ((1,), (0,)))
     compact[...] = step * jnp.exp(suffix).reshape(ROWS, 8, LANES)
     totals[...] = jnp.exp(whole).reshape(ROWS, 8, LANES)
+
+
+def entry_kernel(
+    inner,
+    above,
+    below,
+    left,
+    right,
+    steps,
+    compact,
+    totals,
+    conv_w,
+    conv_weight,
+    conv_bias,
+    decay_log,
+    xdt,
+    decay,
+    act,
+    bct,
+    cmap,
+    *refs,
+):
+    ends_out, (proj, taps, ends) = refs[:CHIPS], refs[CHIPS:]
+    for ref, at, size in ((conv_weight, 0, 9), (conv_bias, 9, 1)):
+        v = ref[...]
+        taps[0, at : at + size, :] = v[:, 0:128]
+        tail = [v[:, 128:192], v[:, 208:224], v[:, 208:224], v[:, 192:208]]
+        taps[1, at : at + size, :] = jnp.concatenate(tail + [jnp.zeros((size, 16), f32)], axis=1)
+
+    def conv_part(tokens, dims):
+        return dot(tokens, conv_w[...], dims).astype(bf16).astype(f32)
+
+    for at, ref in ((0, above), (ROWS + 1, below)):
+        out = conv_part(ref[...], ((0,), (0,)))
+        for g in range(2):
+            proj[at, g, 8:136, :] = out[:, g * 128 : g * 128 + 128]
+    for ref, at in ((left, 7), (right, 136)):
+        out = conv_part(ref[...], ((1,), (0,)))
+        for g in range(2):
+            proj[:, g, at, :] = out[0 : ROWS + 2, g * 128 : g * 128 + 128]
+
+    def own_row(r):
+        for g in range(2):
+            proj[r + 1, g, 8:136, :] = inner[r, g].astype(f32)
+
+    each_row(own_row, 4)
     rate = [-jnp.exp(by_head(decay_log, g)) for g in range(2)]
 
     def conv_row(r):
@@ -180,34 +187,94 @@
         parts[1] = jnp.where(low_lanes(COLS), parts[1], other)
         for g in range(2):
             act[r, g] = parts[g].astype(bf16)
-            step = xdt[r, g]
+            step = steps[r, g]
             xdt[r, g] = step * parts[g]
             decay[r, g] = jnp.exp(rate[g] * step)
         weighted = [compact[r, h : h + 1, :] * chan_b for h in range(3)]
         weighted = jnp.concatenate(split(jnp.concatenate(weighted, axis=0)), axis=0)
-        inner = jnp.concatenate([act[r, 0], act[r, 1]], axis=1)
-        state = dot(weighted, inner, ((1,), (0,)))
+        inner_x = jnp.concatenate([act[r, 0], act[r, 1]], axis=1)
+        state = dot(weighted, inner_x, ((1,), (0,)))
         state = state[0:48, :] + state[48:96, :]
-        low = low_lanes(16)
-        first = jnp.where(low, state[0:16, 0:128], state[16:32, 0:128])
+        first = jnp.where(low_lanes(16), state[0:16, 0:128], state[16:32, 0:128])
         third = jnp.where(low_lanes(), state[32:40, 128:256], state[40:48, 128:256])
         total = jnp.where(low_lanes(1), totals[r, 0:1, :], totals[r, 1:2, :])
         rest = jnp.concatenate([total, totals[r, 2:3, :], jnp.zeros((2, LANES), f32)], axis=0)
-        ends[2 * r] = jnp.concatenate([first[0:8, :], third[0:4, :], rest], axis=0)
-        ends[2 * r + 1] = jnp.concatenate([first[8:16, :], third[4:8, :], rest], axis=0)
+        quarter, at = r // 4, (r % 4) * 2
+        ends[quarter, at] = jnp.concatenate([first[0:8, :], third[0:4, :], rest], axis=0)
+        ends[quarter, at + 1] = jnp.concatenate([first[8:16, :], third[4:8, :], rest], axis=0)
 
     each_row(conv_row, 2)
-
-
-def row_prefix_kernel(parts, out):
-    count = parts.shape[0]
-    first = jnp.zeros((8, LANES), f32)
-    second = jnp.zeros((8, LANES), f32)
-    for s in range(count):
-        out[s, 0:8, :] = first
-        out[s, 8:16, :] = second
-        first = parts[s, 12:13, :] * first + parts[s, 0:8, :]
-        second = parts[s, 13:14, :] * second + parts[s, 8:16, :]
+    member, _ = line()
+    for k, out in enumerate(ends_out):
+        out[...] = ends[(member + k) % CHIPS]
+
+
+def line():
+    gx = lax.axis_index("gx")
+    return gx % 4, gx // 4
+
+
+def part_of(ref, i, at=None):
+    box = ref if at is None else ref.at[at]
+    return (box[i, 0:8, :], box[i, 8:16, :]), (box[i, 12:13, :], box[i, 13:14, :])
+
+
+def put(ref, i, tiles, decays=None):
+    ref[i, 0:8, :] = tiles[0]
+    ref[i, 8:16, :] = tiles[1]
+    if decays is not None:
+        ref[i, 12:13, :] = decays[0]
+        ref[i, 13:14, :] = decays[1]
+
+
+def chain(tiles, step):
+    return [d * a + b for a, b, d in zip(tiles, *step)]
+
+
+def product(a, b):
+    return [u * v for u, v in zip(a, b)]
+
+
+def members_kernel(*refs):
+    parts, (out, held) = refs[:CHIPS], refs[CHIPS:]
+    member, _ = line()
+    for k, part in enumerate(parts):
+        held[(member + CHIPS - k) % CHIPS] = part[...]
+    for i in range(8):
+        tiles, decays = part_of(held, i, 0)
+        for m in range(1, CHIPS):
+            step = part_of(held, i, m)
+            tiles, decays = chain(tiles, step), product(decays, step[1])
+        put(out, i, tiles, decays)
+
+
+def pair_kernel(mine, theirs, out):
+    _, z = line()
+    odd = z % 2 == 1
+    for i in range(8):
+        a, b = part_of(mine, i), part_of(theirs, i)
+        after, before = chain(b[0], a), chain(a[0], b)
+        tiles = [jnp.where(odd, u, v) for u, v in zip(after, before)]
+        put(out, i, tiles, product(a[1], b[1]))
+
+
+def carry_kernel(near, mid, far, theirs, *refs):
+    parts, outs, held = refs[:CHIPS], refs[CHIPS : 2 * CHIPS], refs[-1]
+    member, z = line()
+    odd = z % 2 == 1
+    for k, part in enumerate(parts):
+        held[(member + CHIPS - k) % CHIPS] = part[...]
+    for i in range(8):
+        tiles = part_of(far, i)[0]
+        for part in (mid, near):
+            tiles = chain(tiles, part_of(part, i))
+        tiles = [jnp.where(odd, u, v) for u, v in zip(chain(tiles, part_of(theirs, i)), tiles)]
+        for m in range(CHIPS):
+            step = part_of(held, i, m)
+            put(held.at[m], i, tiles)
+            tiles = chain(tiles, step)
+    for k, out in enumerate(outs):
+        out[...] = held[(member + k) % CHIPS]
 
 
 def starts(carry, r):
@@ -215,8 +282,12 @@
     return [carry[2 * r, 0:8, :], carry[2 * r + 1, 0:8, :], third]
 
 
-def bottom_kernel(xdt, decay, bct, carry, mine, theirs, hold):
+def bottom_kernel(xdt, decay, bct, *refs):
+    parts, (mine, theirs, carry, hold) = refs[:CHIPS], refs[CHIPS:]
     core = lax.axis_index("gy") % 2
+    member, _ = line()
+    for k, part in enumerate(parts):
+        carry[pl.ds((member + CHIPS - k) % CHIPS * 8, 8)] = part[...]
     low = low_lanes()
     begin = []
     for r in range(ROWS):
@@ -258,64 +329,72 @@
     lax.fori_loop(0, BLOCKS, block, tuple(begin))
 
 
-def local_kernel(begins, xdt, decay, bct, carry, act, gate, skip_gain, *refs):
+def gating_kernel(decay, gate, gating, reach):
+    along = [jnp.ones((COLS, LANES), f32)] * 2
+
+    def some(k, along):
+        along = list(along)
+        for i in range(4):
+            r = k * 4 + i
+            for g in range(2):
+                along[g] = along[g] * decay[r, g]
+                gated = silu(gate[r, g].astype(f32))
+                gating[r, g] = gated
+                reach[r, g] = along[g] * gated
+        return tuple(along)
+
+    lax.fori_loop(0, ROWS // 4, some, tuple(along))
+
+
+def local_kernel(begins, xdt, decay, bct, carry, act, gating, skip_gain, *refs):
     if begins:
-        track_in, gated_out, reach_out, track, local = refs
-        track[...] = track_in[...]
+        track_in, gated, local = refs
     else:
-        gated_out, reach_out, track, local = refs
-        track[...] = jnp.zeros_like(track)
+        gated, track, local = refs
     low = low_lanes()
-
-    def group(at, _):
-        rg = begins // GROUP + at
-        begin = []
-        for i in range(GROUP):
-            begin += starts(carry, rg * GROUP + i)
-
-        def block(cb, state):
-            state = list(state)
-            base = cb * BLOCK
-            maps = [pltpu.roll(bct[rg * GROUP + i], COLS - base, 1) for i in range(GROUP)]
-            for j in range(BLOCK):
-                cols = [track[cb, j * 24 + 8 * q : j * 24 + 8 * q + 8, :] for q in range(3)]
-                reads = []
-                for i in range(GROUP):
-                    r = rg * GROUP + i
-                    wide = [spread(maps[i], q, j) for q in range(4)]
-                    b_all = [wide[0], wide[1], jnp.where(low, wide[0], wide[1])]
-                    x = [xdt[r, g, pl.ds(base + j, 8, stride=0), :] for g in range(2)]
-                    d = [decay[r, g, pl.ds(base + j, 8, stride=0), :] for g in range(2)]
-                    for q in range(3):
-                        g = q // 2
-                        state[3 * i + q] = d[g] * state[3 * i + q] + x[g] * b_all[q]
-                        cols[q] = d[g] * cols[q] + state[3 * i + q]
-                    reads.append(wide[2] * cols[0] + wide[3] * cols[1])
-                    reads.append(jnp.where(low, wide[2], wide[3]) * cols[2])
+    count = ROWS // 2
+    begin = []
+    for i in range(count):
+        begin += starts(carry, begins + i)
+
+    def block(cb, state):
+        state = list(state)
+        base = cb * BLOCK
+        maps = [pltpu.roll(bct[begins + i], COLS - base, 1) for i in range(count)]
+        for j in range(BLOCK):
+            if begins:
+                cols = [track_in[cb, j * 24 + 8 * q : j * 24 + 8 * q + 8, :] for q in range(3)]
+            else:
+                cols = [jnp.zeros((8, LANES), f32)] * 3
+            reads = []
+            for i in range(count):
+                r = begins + i
+                wide = [spread(maps[i], q, j) for q in range(4)]
+                b_all = [wide[0], wide[1], jnp.where(low, wide[0], wide[1])]
+                x = [xdt[r, g, pl.ds(base + j, 8, stride=0), :] for g in range(2)]
+                d = [decay[r, g, pl.ds(base + j, 8, stride=0), :] for g in range(2)]
+                for q in range(3):
+                    g = q // 2
+                    state[3 * i + q] = d[g] * state[3 * i + q] + x[g] * b_all[q]
+                    cols[q] = d[g] * cols[q] + state[3 * i + q]
+                reads.append(wide[2] * cols[0] + wide[3] * cols[1])
+                reads.append(jnp.where(low, wide[2], wide[3]) * cols[2])
+            if not begins:
                 for q in range(3):
                     track[cb, j * 24 + 8 * q : j * 24 + 8 * q + 8, :] = cols[q]
-                local[at, :, base + j, :] = fold_sublanes(reads)
-            return tuple(state)
-
-        lax.fori_loop(0, BLOCKS, block, tuple(begin))
-        return 0
-
-    lax.fori_loop(0, ROWS // 2 // GROUP, group, 0)
-    reach = [jnp.ones((COLS, LANES), f32)] * 2
-    for r in range(begins):
-        for g in range(2):
-            reach[g] = reach[g] * decay[r, g]
-    for i in range(ROWS // 2):
+            for k in range(2):
+                local[k, :, base + j, :] = fold_sublanes(reads[8 * k : 8 * k + 8])
+        return tuple(state)
+
+    lax.fori_loop(0, BLOCKS, block, tuple(begin))
+    for i in range(count):
         r = begins + i
         for g in range(2):
-            reach[g] = reach[g] * decay[r, g]
-            mixed = local[i // GROUP, (i % GROUP) * 2 + g]
+            mixed = local[i // 4, (i % 4) * 2 + g]
             if g == 1:
                 mixed = mixed + pltpu.roll(mixed, HALF, 1)
             mixed = mixed + by_head(skip_gain, g) * act[r, g].astype(f32)
-            gating = silu(gate[r, g].astype(f32))
-            gated_out[i, g] = mixed * gating
-            reach_out[i, g] = reach[g] * gating
+            gated[i, g] = mixed * gating[r, g]
 
 
 def place():
@@ -386,13 +465,11 @@
         lax.fori_loop(0, BLOCK, column, 0, unroll=4)
 
 
-def exit_kernel(
-    own, other, cmap, gated_a, reach_a, gated_b, reach_b, norm_gain, out_weight, out, carried
-):
+def reads_kernel(states, cmap, carried, *, half):
     low = low_lanes()
     core, _ = place()
 
-    def block(k, _, states, half):
+    def block(k, _):
         for j in range(BLOCK):
             first, second, third = [
                 states[k, j * 24 + 8 * q : j * 24 + 8 * q + 8, :] for q in range(3)
@@ -406,34 +483,44 @@
                 ],
                 axis=1,
             )
-            c = ((core ^ half) * HALVED + k) * BLOCK + j
-            reads = cmap[c][:, 0:32].astype(bf16)
+            at = k * BLOCK + j
+            reads = cmap[(core ^ half) * HALF + at][:, 0:32].astype(bf16)
             result = dot(reads, jnp.concatenate(split(whole), axis=0), ((1,), (0,)))
             for g in range(2):
-                carried[:, g, c, :] = result[:, g * 128 : g * 128 + 128]
+                carried[:, g, at, :] = result[:, g * 128 : g * 128 + 128]
         return 0
 
-    for half, states in enumerate((own, other)):
-        lax.fori_loop(0, HALVED, functools.partial(block, states=states, half=half), 0)
+    lax.fori_loop(0, HALVED, block, 0)
+
+
+def exit_kernel(
+    own, other, cmap, gated_a, gated_b, reach, norm_gain, out_weight, out, carried
+):
+    core, _ = place()
+    reads_kernel(other, cmap, carried, half=1)
     turned = out_weight[...].astype(f32).T
     weight = jnp.concatenate([turned, jnp.zeros((WIDTH, HALF), f32)], axis=1).astype(bf16)
     pad = jnp.zeros((1, HALF), f32)
     gain = [norm_gain[:, 0:128], jnp.concatenate([norm_gain[:, 128:192], pad], axis=1)]
 
-    def row(r, begins, gated, reach):
+    def row(r, begins, gated):
         i = r - begins
-        parts = [gated[i, g] + reach[i, g] * carried[r, g] for g in range(2)]
+        parts = []
+        for g in range(2):
+            a, b = own[r, g], carried[r, g]
+            both = [jnp.where(core == 0, a, b), jnp.where(core == 0, b, a)]
+            parts.append(gated[i, g] + reach[r, g] * jnp.concatenate(both, axis=0))
         total = jnp.sum(parts[0] * parts[0] + parts[1] * parts[1], axis=1, keepdims=True)
         scale = lax.rsqrt(total * (1.0 / INNER) + norm_eps)
         normed = [(parts[g] * scale * gain[g]).astype(bf16) for g in range(2)]
         result = dot(weight, jnp.concatenate(normed, axis=1), ((1,), (1,)))
         out[r] = result.astype(bf16)
 
-    for begins, gated, reach in ((0, gated_a, reach_a), (ROWS // 2, gated_b, reach_b)):
+    for begins, gated in ((0, gated_a), (ROWS // 2, gated_b)):
 
         def some(k, carry):
             for i in range(4):
-                row(begins + 4 * k + i, begins, gated, reach)
+                row(begins + 4 * k + i, begins, gated)
             return carry
 
         lax.fori_loop(0, ROWS // 8, some, 0)
@@ -476,71 +563,113 @@
 ):
     to_right, to_left = steps("gx")
     to_down, to_up = steps("gy")
-    left = lax.ppermute(tokens[:, :, COLS - 1], "gx", to_right)
-    right = lax.ppermute(tokens[:, :, 0], "gx", to_left)
-
-    def edge(r):
-        rest = jnp.pad(jnp.stack([left[r], right[r]]), ((0, 14), (0, LANES - WIDTH)))
-        return jnp.concatenate([tokens[r], rest], axis=0)
-
-    above = lax.ppermute(edge(ROWS - 1), "gy", to_down)
-    below = lax.ppermute(edge(0), "gy", to_up)
+    above = lax.ppermute(tokens[ROWS - 1], "gy", to_down)
+    below = lax.ppermute(tokens[0], "gy", to_up)
+
+    def edge(c):
+        column = [above[None, :, c], tokens[:, :, c], below[None, :, c]]
+        return jnp.concatenate(column, axis=0)
+
+    last, first = edge(COLS - 1), edge(0)
+    left = lax.ppermute(last, "gx", to_right)
+    right = lax.ppermute(first, "gx", to_left)
     vmem = pltpu.VMEM
-    xdt, decay, act, gate, bct, cmap, ends = call(
+    rows8 = ((ROWS, 8, LANES), f32, "v")
+    inner, gate, step, compact, totals, conv_w = call(
+        project_kernel,
+        "vvss",
+        [(PLANE, bf16, "v"), (PLANE, bf16, "v"), (PLANE, f32, "v"), rows8, rows8]
+        + [((WIDTH, 256), bf16, "v")],
+        [vmem((WIDTH, 768), bf16)],
+        tokens,
+        in_weight,
+        step_bias,
+        decay_log,
+        after=(last,),
+    )
+    packet = ((8, 16, LANES), f32, "v")
+    quarters = vmem((CHIPS,) + packet[0], f32)
+    xdt, decay, act, bct, cmap, *ends = call(
         entry_kernel,
-        "vvvvvvvvss",
+        "vvvvvvvvvvvs",
         [
             (PLANE, f32, "v"),
             (PLANE, f32, "v"),
             (PLANE, bf16, "v"),
-            (PLANE, bf16, "v"),
             ((ROWS, 32, COLS), f32, "v"),
             ((COLS, ROWS, LANES), f32, "v"),
-            ((2 * ROWS, 16, LANES), f32, "v"),
-        ],
-        [
-            vmem((ROWS + 2, 2, 144, LANES), f32),
-            vmem((WIDTH, 768), bf16),
-            vmem((2, 16, LANES), f32),
-            vmem((ROWS, 8, LANES), f32),
-            vmem((ROWS, 8, LANES), f32),
-        ],
-        tokens,
+        ]
+        + [packet] * CHIPS,
+        [vmem((ROWS + 2, 2, 144, LANES), f32), vmem((2, 16, LANES), f32), quarters],
+        inner,
         above,
         below,
         left,
         right,
-        in_weight,
+        step,
+        compact,
+        totals,
+        conv_w,
         conv_weight.reshape(9, 224),
         conv_bias.reshape(1, 224),
-        step_bias,
         decay_log,
     )
-    ends = lax.all_to_all(ends, "gx", 0, 0)
-    (carry,) = call(row_prefix_kernel, "v", [((2 * ROWS, 16, LANES), f32, "v")], [], ends)
-    carry = lax.all_to_all(carry, "gx", 0, 0)
+    gx_count = lax.axis_size("gx")
+
+    def members(pieces):
+        moved = [pieces[0]] * CHIPS
+        for k in (2, 1, 3):
+            pairs = [(i, i // 4 * 4 + (i + k) % 4) for i in range(gx_count)]
+            moved[k] = lax.ppermute(pieces[k], "gx", pairs)
+        return moved
+
+    gating, reach = call(
+        gating_kernel, "vv", [(PLANE, f32, "v")] * 2, [], decay, gate, after=ends[:1]
+    )
+    ends = members(ends)
+    (whole,) = call(members_kernel, "vvvv", [packet], [quarters], *ends, after=(reach,))
+    beside = lax.ppermute(whole, "gx", [(i, i ^ 4) for i in range(gx_count)])
+    (both,) = call(pair_kernel, "vv", [packet], [], whole, beside)
+    mid, near, far = [
+        lax.ppermute(both, "gx", [(i, i + 8 * k) for i in range(gx_count - 8 * k)])
+        for k in (2, 1, 3)
+    ]
+    carries = call(
+        carry_kernel, "v" * 8, [packet] * CHIPS, [quarters], near, mid, far, beside, *ends
+    )
+    carries = members(carries)
     piece, piece_out = (PIECE, f32, "v"), (PIECE_OUT, f32, "v")
     halves = ((HALVED,) + PIECE, f32, "v")
-    mine, theirs = call(
-        bottom_kernel, "vvvv", [halves] * 2, [vmem(PIECE, f32)], xdt, decay, bct, carry
+    mine, theirs, carry = call(
+        bottom_kernel,
+        "v" * 7,
+        [halves, halves, ((2 * ROWS, 16, LANES), f32, "v")],
+        [vmem(PIECE, f32)],
+        xdt,
+        decay,
+        bct,
+        *carries,
     )
     gy_count = lax.axis_size("gy")
     swap = [(i, i ^ 1) for i in range(gy_count)]
     ahead = [[(i, (i + 2 * k) % gy_count) for i in range(gy_count)] for k in range(CHIPS)]
 
     def rotate(pieces):
-        return [pieces[0]] + [lax.ppermute(pieces[k], "gy", ahead[k]) for k in range(1, CHIPS)]
+        moved = [pieces[0]] * CHIPS
+        for k in (2, 1, 3):
+            moved[k] = lax.ppermute(pieces[k], "gy", ahead[k])
+        return moved
 
     theirs = lax.ppermute(theirs, "gy", swap)
     joined = call(join_kernel, "vv", [piece] * CHIPS, [], mine, theirs)
     pieces = rotate(joined)
-    half = (ROWS // 2,) + PLANE[1:]
-    local_scratch = vmem((ROWS // 2 // GROUP, 8, COLS, LANES), f32)
-    inner = (xdt, decay, bct, carry, act, gate, skip_gain)
-    gated_a, reach_a, track = call(
+    half = ((ROWS // 2,) + PLANE[1:], f32, "v")
+    local_scratch = vmem((2, 8, COLS, LANES), f32)
+    inner = (xdt, decay, bct, carry, act, gating, skip_gain)
+    gated_a, track = call(
         functools.partial(local_kernel, 0),
         "vvvvvvs",
-        [(half, f32, "v"), (half, f32, "v"), ((BLOCKS,) + PIECE_OUT, f32, "v")],
+        [half, ((BLOCKS,) + PIECE_OUT, f32, "v")],
         [local_scratch],
         *inner,
         after=joined[:1],
@@ -555,11 +684,11 @@
     )
     above_chip = pieces[0]
     pieces = rotate(pieces)
-    gated_b, reach_b = call(
+    (gated_b,) = call(
         functools.partial(local_kernel, ROWS // 2),
         "vvvvvvsv",
-        [(half, f32, "v"), (half, f32, "v")],
-        [vmem((BLOCKS,) + PIECE_OUT, f32), local_scratch],
+        [half],
+        [local_scratch],
         *inner,
         track,
         after=(above_chip,),
@@ -568,19 +697,29 @@
     own, other = call(
         share_kernel, "vvvvvv", [halves_out] * 2, [], *pieces, mine, theirs, after=(gated_b,)
     )
-    other = lax.ppermute(other, "gy", swap)
+    sent = other
+    other = lax.ppermute(sent, "gy", swap)
+    half_plane = (ROWS, 2, HALF, LANES)
+    (own,) = call(
+        functools.partial(reads_kernel, half=0),
+        "vv",
+        [(half_plane, f32, "v")],
+        [],
+        own,
+        cmap,
+        after=(sent,),
+    )
     (out,) = call(
         exit_kernel,
-        "vvvvvvvvv",
+        "vvvvvvvv",
         [((ROWS, WIDTH, COLS), bf16, "v")],
-        [vmem(PLANE, f32)],
+        [vmem(half_plane, f32)],
         own,
         other,
         cmap,
         gated_a,
-        reach_a,
         gated_b,
-        reach_b,
+        reach,
         norm_gain.reshape(1, INNER),
         out_weight,
     )

time: 117 us -> 106 us (0.906)
  blocking collectives: 42 us -> 0 us
  starting transfers between devices: 26.8 us -> 50.8 us
  waiting for transfers between devices: 7.85 us -> 15.2 us
  Pallas kernels: 38.2 us -> 36.4 us
    all_to_all x2 -> x0, blocking collectives: 42 us -> none  [the longest x1 25.9 us: on_device(): ends = lax.all_to_all(ends, 'gx', 0, 0)]
    ppermute x11 -> x21, starting transfers between devices: 25.5 us -> 46.3 us  [the longest x3 12.7 us: on_device(): lax.ppermute(both, 'gx', [(i, i + 8 * k) for i in range(gx_count - 8 * k)])]
    ppermute x11 -> x21, waiting for transfers between devices: 5.85 us -> 13.2 us  [the longest x6 6.18 us: members(): moved[k] = lax.ppermute(pieces[k], 'gx', pairs)]
    ppermute x1, starting transfers between devices: 1.26 us -> 4.47 us  [on_device(): theirs = lax.ppermute(theirs, 'gy', swap)]
    pallas_call x9 -> x14, Pallas kernels: 38.2 us -> 36.4 us  [call(): pl.pallas_call(inner, in_specs=[pl.BlockSpec(memory_space=kinds[k]) for k...]
  transfers between devices with their start and end apart: 12 -> 22, of which waited for: 4 -> 12; matrix products, arithmetic and copies ran while one was open for 0% -> 2% of each run, Pallas kernels for 15% -> 18%
where the time goes in v3:
time: 106 us
  starting transfers between devices  50.8 us (48%)
  Pallas kernels  36.4 us (34%)
  waiting for transfers between devices  15.2 us (14%)
  local copies, waits for them, and re-layouts  2.92 us (3%)
    pallas_call x14, Pallas kernels, call(): pl.pallas_call(inner, in_specs=[pl.BlockSpec(memory_space=kinds[k]) for k...  36.4 us
    ppermute x3, starting transfers between devices, on_device(): lax.ppermute(both, 'gx', [(i, i + 8 * k) for i in range(gx_count - 8 * k)])  12.7 us
    ppermute x6, starting transfers between devices, rotate(): moved[k] = lax.ppermute(pieces[k], 'gy', ahead[k])  9.79 us
    ppermute x6, starting transfers between devices, members(): moved[k] = lax.ppermute(pieces[k], 'gx', pairs)  9.73 us
    ppermute x6, waiting for transfers between devices, members(): moved[k] = lax.ppermute(pieces[k], 'gx', pairs)  6.18 us
    ppermute x1, starting transfers between devices, on_device(): above = lax.ppermute(tokens[ROWS - 1], 'gy', to_down)  4.58 us
    ppermute x1, starting transfers between devices, on_device(): theirs = lax.ppermute(theirs, 'gy', swap)  4.47 us
    ppermute x1, starting transfers between devices, on_device(): left = lax.ppermute(last, 'gx', to_right)  3.12 us
  transfers between devices with their start and end apart: 22, of which 12 were waited for; matrix products, arithmetic and copies ran while one was open for 2% of the time, Pallas kernels for 18%

profile of v3, /device:TPU:1, one launch (start us, length us, event | category | flops | bytes accessed | tf_op | source)
XLA Modules:
  0.0 105.7 jit_solution(7787846155316888575)
XLA Ops:
  0.8 4.6 %collective-permute-start = (bf16[96,128]{1,0:T(8,128)(2,1)S(1)}, bf16[96,128]{1,0:T(8,128)(2,1)S(1)}, u32[]{:S(2)}, u32[]{:S(2)}) collective-permute-start(bf16[96,128]{1,0:T(8,128)(2,1)S(1)} %get-tuple-element.83), channel_id=1, source_target_pairs={{0,32},{32,64},{64,96},{96,128},{128,160},{160,192},{192,224},{1,3... | collective-permute-start | bytes 73736 | tf_op jit(solution)/shard_map/ppermute | solution.py:566
  5.4 1.9 %collective-permute-start.1 = (bf16[96,128]{1,0:T(8,128)(2,1)S(1)}, bf16[96,128]{1,0:T(8,128)(2,1)S(1)}, u32[]{:S(2)}, u32[]{:S(2)}) collective-permute-start(bf16[96,128]{1,0:T(8,128)(2,1)S(1)} %get-tuple-element.84), channel_id=1, source_target_pairs={{32,0},{64,32},{96,64},{128,96},{160,128},{192,160},{224,192},{33,... | collective-permute-start | bytes 73736 | tf_op jit(solution)/shard_map/ppermute | solution.py:567
  7.4 1.3 %fusion = (bf16[16,96,1]{2,1,0:T(8,128)(2,1)S(1)}, bf16[16,96,1]{2,1,0:T(8,128)(2,1)S(1)}) fusion(bf16[16,96,128]{2,1,0:T(8,128)(2,1)} %refs_0_.1), kind=kLoop, calls=%fused_computation.8 | loop fusion | bytes 12288 | tf_op jit(solution)/shard_map/slice | solution.py:570
  9.3 1.3 %collective-permute-done.1.refs_2_ = bf16[96,128]{1,0:T(8,128)(2,1)S(1)} collective-permute-done((bf16[96,128]{1,0:T(8,128)(2,1)S(1)}, bf16[96,128]{1,0:T(8,128)(2,1)S(1)}, u32[]{:S(2)}, u32[]{:S(2)}) %collective-permute-start.1) | collective-permute-done | bytes 24608 | tf_op jit(solution)/shard_map/ppermute | solution.py:567
  10.8 3.1 %collective-permute-start.2 = (bf16[18,96]{1,0:T(8,128)(2,1)S(1)}, bf16[18,96]{1,0:T(8,128)(2,1)S(1)}, u32[]{:S(2)}, u32[]{:S(2)}) collective-permute-start(bf16[18,96]{1,0:T(8,128)(2,1)S(1)} %pad_maximum_fusion.refs_4_), channel_id=1, source_target_pairs={{0,1},{1,2},{2,3},{3,4},{4,5},{5,6},{6,7},{7,8},{8,9},{9,10},{10,1... | collective-permute-start | bytes 10376 | tf_op jit(solution)/shard_map/ppermute | solution.py:574
  13.9 1.3 %collective-permute-start.3 = (bf16[18,96]{1,0:T(8,128)(2,1)S(1)}, bf16[18,96]{1,0:T(8,128)(2,1)S(1)}, u32[]{:S(2)}, u32[]{:S(2)}) collective-permute-start(bf16[18,96]{1,0:T(8,128)(2,1)S(1)} %pad_maximum_fusion.1), channel_id=1, source_target_pairs={{1,0},{2,1},{3,2},{4,3},{5,4},{6,5},{7,6},{8,7},{9,8},{10,9},{11,1... | collective-permute-start | bytes 10376 | tf_op jit(solution)/shard_map/ppermute | solution.py:575
  15.3 3.0 %shard_map.91 = (bf16[16,2,128,128]{3,2,1,0:T(8,128)(2,1)S(1)}, bf16[16,2,128,128]{3,2,1,0:T(8,128)(2,1)S(1)}, f32[16,2,128,128]{3,2,1,0:T(8,128)S(1)}, f32[16,8...) custom-call(bf16[16,96,128]{2,1,0:T(8,128)(2,1)S(1)} %copy-done, ...), custom_call_target="tpu_custom_call" | custom-call | tf_op jit(solution)/shard_map/pallas_call | solution.py:537
  18.4 5.3 %shard_map.92 = (f32[16,2,128,128]{3,2,1,0:T(8,128)S(1)}, f32[16,2,128,128]{3,2,1,0:T(8,128)S(1)}, bf16[16,2,128,128]{3,2,1,0:T(8,128)(2,1)S(1)}, f32[16,32,128]...) custom-call(bf16[16,2,128,128]{3,2,1,0:T(8,128)(2,1)S(1)} %get-tuple, ...), custom_call_target="tpu_custom_call" | custom-call | tf_op jit(solution)/shard_map/pallas_call | solution.py:537
  23.7 2.2 %collective-permute-start.4 = (f32[8,16,128]{2,1,0:T(8,128)S(1)}, f32[8,16,128]{2,1,0:T(8,128)S(1)}, u32[]{:S(2)}, u32[]{:S(2)}) collective-permute-start(f32[8,16,128]{2,1,0:T(8,128)S(1)} %get-tuple-element.50), channel_id=1, source_target_pairs={{0,1},{1,2},{2,3},{3,0},{4,5},{5,6},{6,7},{7,4},{8,9},{9,10},{10,1... | collective-permute-start | bytes 196616 | tf_op jit(solution)/shard_map/ppermute | solution.py:623
  25.8 4.0 %collective-permute-start.5 = (f32[8,16,128]{2,1,0:T(8,128)S(1)}, f32[8,16,128]{2,1,0:T(8,128)S(1)}, u32[]{:S(2)}, u32[]{:S(2)}) collective-permute-start(f32[8,16,128]{2,1,0:T(8,128)S(1)} %get-tuple-element.51), channel_id=1, source_target_pairs={{0,2},{1,3},{2,0},{3,1},{4,6},{5,7},{6,4},{7,5},{8,10},{9,11},{10,... | collective-permute-start | bytes 196616 | tf_op jit(solution)/shard_map/ppermute | solution.py:623
  30.5 3.0 %collective-permute-done.5.refs_2_.refs_6_ = f32[8,16,128]{2,1,0:T(8,128)S(1)} collective-permute-done((f32[8,16,128]{2,1,0:T(8,128)S(1)}, f32[8,16,128]{2,1,0:T(8,128)S(1)}, u32[]{:S(2)}, u32[]{:S(2)}) %collective-permute-start.5) | collective-permute-done | bytes 65568 | tf_op jit(solution)/shard_map/ppermute | solution.py:623
  33.7 1.7 %collective-permute-start.7 = (f32[8,16,128]{2,1,0:T(8,128)S(1)}, f32[8,16,128]{2,1,0:T(8,128)S(1)}, u32[]{:S(2)}, u32[]{:S(2)}) collective-permute-start(f32[8,16,128]{2,1,0:T(8,128)S(1)} %shard_map.94.refs_0_), channel_id=1, source_target_pairs={{0,4},{1,5},{2,6},{3,7},{4,0},{5,1},{6,2},{7,3},{8,12},{9,13},{10,... | collective-permute-start | bytes 196616 | tf_op jit(solution)/shard_map/ppermute | solution.py:631
  35.4 1.7 %collective-permute-done.7.refs_1_.refs_3_ = f32[8,16,128]{2,1,0:T(8,128)S(1)} collective-permute-done((f32[8,16,128]{2,1,0:T(8,128)S(1)}, f32[8,16,128]{2,1,0:T(8,128)S(1)}, u32[]{:S(2)}, u32[]{:S(2)}) %collective-permute-start.7) | collective-permute-done | bytes 65568 | tf_op jit(solution)/shard_map/ppermute | solution.py:631
  37.1 7.5 %collective-permute-start.10 = (f32[8,16,128]{2,1,0:T(8,128)S(1)}, f32[8,16,128]{2,1,0:T(8,128)S(1)}, u32[]{:S(2)}, u32[]{:S(2)}) collective-permute-start(f32[8,16,128]{2,1,0:T(8,128)S(1)} %shard_map.95), channel_id=1, source_target_pairs={{0,24},{1,25},{2,26},{3,27},{4,28},{5,29},{6,30},{7,31},{32,56},{3... | collective-permute-start | bytes 196616 | tf_op jit(solution)/shard_map/ppermute | solution.py:634
  44.6 3.1 %collective-permute-start.9 = (f32[8,16,128]{2,1,0:T(8,128)S(1)}, f32[8,16,128]{2,1,0:T(8,128)S(1)}, u32[]{:S(2)}, u32[]{:S(2)}) collective-permute-start(f32[8,16,128]{2,1,0:T(8,128)S(1)} %shard_map.95), channel_id=1, source_target_pairs={{0,16},{1,17},{2,18},{3,19},{4,20},{5,21},{6,22},{7,23},{8,24},{9,... | collective-permute-start | bytes 196616 | tf_op jit(solution)/shard_map/ppermute | solution.py:634
  47.7 2.2 %collective-permute-start.8 = (f32[8,16,128]{2,1,0:T(8,128)S(1)}, f32[8,16,128]{2,1,0:T(8,128)S(1)}, u32[]{:S(2)}, u32[]{:S(2)}) collective-permute-start(f32[8,16,128]{2,1,0:T(8,128)S(1)} %shard_map.95), channel_id=1, source_target_pairs={{0,8},{1,9},{2,10},{3,11},{4,12},{5,13},{6,14},{7,15},{8,16},{9,17... | collective-permute-start | bytes 196616 | tf_op jit(solution)/shard_map/ppermute | solution.py:634
  49.9 1.3 %collective-permute-done.8.refs_0_ = f32[8,16,128]{2,1,0:T(8,128)S(1)} collective-permute-done((f32[8,16,128]{2,1,0:T(8,128)S(1)}, f32[8,16,128]{2,1,0:T(8,128)S(1)}, u32[]{:S(2)}, u32[]{:S(2)}) %collective-permute-start.8) | collective-permute-done | bytes 65568 | tf_op jit(solution)/shard_map/ppermute | solution.py:634
  51.7 3.2 %collective-permute-start.12 = (f32[8,16,128]{2,1,0:T(8,128)S(1)}, f32[8,16,128]{2,1,0:T(8,128)S(1)}, u32[]{:S(2)}, u32[]{:S(2)}) collective-permute-start(f32[8,16,128]{2,1,0:T(8,128)S(1)} %get-tuple-element.57), channel_id=1, source_target_pairs={{0,2},{1,3},{2,0},{3,1},{4,6},{5,7},{6,4},{7,5},{8,10},{9,11},{10,... | collective-permute-start | bytes 196616 | tf_op jit(solution)/shard_map/ppermute | solution.py:623
  55.7 1.6 %collective-permute-done.12.refs_5_ = f32[8,16,128]{2,1,0:T(8,128)S(1)} collective-permute-done((f32[8,16,128]{2,1,0:T(8,128)S(1)}, f32[8,16,128]{2,1,0:T(8,128)S(1)}, u32[]{:S(2)}, u32[]{:S(2)}) %collective-permute-start.12) | collective-permute-done | bytes 65568 | tf_op jit(solution)/shard_map/ppermute | solution.py:623
  58.0 7.0 %shard_map.97 = (f32[4,416,128]{2,1,0:T(8,128)S(1)}, f32[4,416,128]{2,1,0:T(8,128)S(1)}, f32[32,16,128]{2,1,0:T(8,128)S(1)}) custom-call(f32[16,2,128,128]{3,2,1,0:T(8,128)S(1)} %get-tuple-element.46.refs_0_, f32[16,2,128,128]{3,2,1,0:T(8,128)S(1)} %get-tuple-element.47.refs_0_.refs_1_, f32[16,32,128]{2,1,0:T(8,128)S(1)} %get-tuple-element.48.refs_2_, ...), custom_call_target="tpu_custom_call" | custom-call | tf_op jit(solution)/shard_map/pallas_call | solution.py:537
  65.0 4.5 %collective-permute-start.14 = (f32[4,416,128]{2,1,0:T(8,128)S(1)}, f32[4,416,128]{2,1,0:T(8,128)S(1)}, u32[]{:S(2)}, u32[]{:S(2)}) collective-permute-start(f32[4,416,128]{2,1,0:T(8,128)S(1)} %get-tuple-element.60), channel_id=1, source_target_pairs={{0,32},{32,0},{64,96},{96,64},{128,160},{160,128},{192,224},{224,1... | collective-permute-start | bytes 2555912 | tf_op jit(solution)/shard_map/ppermute | solution.py:663
  69.5 2.0 %collective-permute-done.14.refs_1_.refs_5_ = f32[4,416,128]{2,1,0:T(8,128)S(1)} collective-permute-done((f32[4,416,128]{2,1,0:T(8,128)S(1)}, f32[4,416,128]{2,1,0:T(8,128)S(1)}, u32[]{:S(2)}, u32[]{:S(2)}) %collective-permute-start.14) | collective-permute-done | bytes 852000 | tf_op jit(solution)/shard_map/ppermute | solution.py:663
  71.7 1.9 %collective-permute-start.15 = (f32[416,128]{1,0:T(8,128)S(1)}, f32[416,128]{1,0:T(8,128)S(1)}, u32[]{:S(2)}, u32[]{:S(2)}) collective-permute-start(f32[416,128]{1,0:T(8,128)S(1)} %get-tuple-element.62), channel_id=1, source_target_pairs={{0,64},{32,96},{64,128},{96,160},{128,192},{160,224},{192,0},{224,... | collective-permute-start | bytes 638984 | tf_op jit(solution)/shard_map/ppermute | solution.py:660
  73.6 2.0 %collective-permute-start.16 = (f32[416,128]{1,0:T(8,128)S(1)}, f32[416,128]{1,0:T(8,128)S(1)}, u32[]{:S(2)}, u32[]{:S(2)}) collective-permute-start(f32[416,128]{1,0:T(8,128)S(1)} %get-tuple-element.63), channel_id=1, source_target_pairs={{0,128},{32,160},{64,192},{96,224},{128,0},{160,32},{192,64},{224,... | collective-permute-start | bytes 638984 | tf_op jit(solution)/shard_map/ppermute | solution.py:660
  75.7 1.4 %collective-permute-start.17 = (f32[416,128]{1,0:T(8,128)S(1)}, f32[416,128]{1,0:T(8,128)S(1)}, u32[]{:S(2)}, u32[]{:S(2)}) collective-permute-start(f32[416,128]{1,0:T(8,128)S(1)} %get-tuple-element.64), channel_id=1, source_target_pairs={{0,192},{32,224},{64,0},{96,32},{128,64},{160,96},{192,128},{224,1... | collective-permute-start | bytes 638984 | tf_op jit(solution)/shard_map/ppermute | solution.py:660
  77.1 6.9 %shard_map.99 = (f32[8,2,128,128]{3,2,1,0:T(8,128)S(1)}, f32[8,384,128]{2,1,0:T(8,128)S(1)}) custom-call(f32[16,2,128,128]{3,2,1,0:T(8,128)S(1)} %get-tuple-element.46.refs_0_, f32[16,2,128,128]{3,2,1,0:T(8,128)S(1)} %get-tuple-element.47.refs_0_.refs_1_, f32[16,32,128]{2,1,0:T(8,128)S(1)} %get-tuple-element.48.refs_2_, ...), custom_call_target="tpu_custom_call" | custom-call | tf_op jit(solution)/shard_map/pallas_call | solution.py:537
  83.9 1.3 %collective-permute-done.16.refs_2_ = f32[416,128]{1,0:T(8,128)S(1)} collective-permute-done((f32[416,128]{1,0:T(8,128)S(1)}, f32[416,128]{1,0:T(8,128)S(1)}, u32[]{:S(2)}, u32[]{:S(2)}) %collective-permute-start.16) | collective-permute-done | bytes 213024 | tf_op jit(solution)/shard_map/ppermute | solution.py:660
  86.1 3.2 %collective-permute-start.19 = (f32[384,128]{1,0:T(8,128)S(1)}, f32[384,128]{1,0:T(8,128)S(1)}, u32[]{:S(2)}, u32[]{:S(2)}) collective-permute-start(f32[384,128]{1,0:T(8,128)S(1)} %get-tuple-element.71), channel_id=1, source_target_pairs={{0,128},{32,160},{64,192},{96,224},{128,0},{160,32},{192,64},{224,... | collective-permute-start | bytes 589832 | tf_op jit(solution)/shard_map/ppermute | solution.py:660
  89.9 6.9 %shard_map.101.refs_6_.refs_4_ = f32[8,2,128,128]{3,2,1,0:T(8,128)S(1)} custom-call(f32[16,2,128,128]{3,2,1,0:T(8,128)S(1)} %get-tuple-element.46.refs_0_, f32[16,2,128,128]{3,2,1,0:T(8,128)S(1)} %get-tuple-element.47.refs_0_.refs_1_, f32[16,32,128]{2,1,0:T(8,128)S(1)} %get-tuple-element.48.refs_2_, f32[32,16,128]{2,1,0:T(8,128)S(1)} %get-tuple-element.65.refs_3_, ...), custom_call_target="tpu_custom_call" | custom-call | tf_op jit(solution)/shard_map/pallas_call | solution.py:537
  98.4 1.4 %collective-permute-start.21 = (f32[4,384,128]{2,1,0:T(8,128)S(1)}, f32[4,384,128]{2,1,0:T(8,128)S(1)}, u32[]{:S(2)}, u32[]{:S(2)}) collective-permute-start(f32[4,384,128]{2,1,0:T(8,128)S(1)} %get-tuple-element.75.refs_2_), channel_id=1, source_target_pairs={{0,32},{32,0},{64,96},{96,64},{128,160},{160,128},{192,224},{224,1... | collective-permute-start | bytes 2359304 | tf_op jit(solution)/shard_map/ppermute | solution.py:701
  99.8 1.6 %shard_map.103.refs_0_ = f32[16,2,64,128]{3,2,1,0:T(8,128)S(1)} custom-call(f32[4,384,128]{2,1,0:T(8,128)S(1)} %get-tuple-element.73.refs_0_, f32[128,16,128]{2,1,0:T(8,128)S(1)} %get-tuple-element.74.refs_1_.refs_2_, f32[4,384,128]{2,1,0:T(8,128)S(1)} %get-tuple-element.75.refs_2_), custom_call_target="tpu_custom_call" | custom-call | tf_op jit(solution)/shard_map/pallas_call | solution.py:537
  101.7 4.0 %shard_map.104 = bf16[16,96,128]{2,1,0:T(8,128)(2,1)} custom-call(f32[16,2,64,128]{3,2,1,0:T(8,128)S(1)} %shard_map.103.refs_0_, f32[4,384,128]{2,1,0:T(8,128)S(1)} %collective-permute-done.21.refs_1_, f32[128,16,128]{2,1,0:T(8,128)S(1)} %get-tuple-element.74.refs_1_.refs_2_, f32[8,2,128,128]{3,2,1,0:T(8,128)S(1)} %get-tuple-element.76.refs_3_, ...), custom_call_target="tpu_custom_call" | custom-call | tf_op jit(solution)/shard_map/pallas_call | solution.py:537
  (53 shorter events, 8.2 us)
Async XLA Ops:
  0.0 15.3 %copy-start = (bf16[16,96,128]{2,1,0:T(8,128)(2,1)S(1)}, bf16[16,96,128]{2,1,0:T(8,128)(2,1)}, u32[]{:S(2)}) copy-start(bf16[16,96,128]{2,1,0:T(8,128)(2,1)} %refs_0_.1) | copy-start | bytes 1179652
  0.0 15.2 %copy-start.8 = (f32[3,3,224]{2,1,0:T(4,128)S(1)}, f32[3,3,224]{2,1,0:T(4,128)}, u32[]{:S(2)}) copy-start(f32[3,3,224]{2,1,0:T(4,128)} %param.11) | copy-start | bytes 24196
  0.0 15.3 %copy-start.4 = (f32[3]{0:T(128)S(1)}, f32[3]{0:T(128)}, u32[]{:S(2)}) copy-start(f32[3]{0:T(128)} %refs_11_.1) | copy-start | bytes 40
  0.0 15.3 %copy-start.7 = (f32[3]{0:T(128)S(1)}, f32[3]{0:T(128)}, u32[]{:S(2)}) copy-start(f32[3]{0:T(128)} %refs_2_.1) | copy-start | bytes 40
  0.0 15.3 %copy-start.1 = (bf16[96,419]{1,0:T(8,128)(2,1)S(1)}, bf16[96,419]{1,0:T(8,128)(2,1)}, u32[]{:S(2)}) copy-start(bf16[96,419]{1,0:T(8,128)(2,1)} %refs_1_.1) | copy-start | bytes 241348
  0.0 18.3 %copy-start.5 = (f32[224]{0:T(256)S(1)}, f32[224]{0:T(256)}, u32[]{:S(2)}) copy-start(f32[224]{0:T(256)} %param.12) | copy-start | bytes 2692
  0.8 8.2 %collective-permute-start = (bf16[96,128]{1,0:T(8,128)(2,1)S(1)}, bf16[96,128]{1,0:T(8,128)(2,1)S(1)}, u32[]{:S(2)}, u32[]{:S(2)}) collective-permute-start(bf16[96,128]{1,0:T(8,128)(2,1)S(1)} %get-tuple-element.83), channel_id=1, source_target_pairs={{0,32},{32,64},{64,96},{96,128},{128,160},{160,192},{192,224},{1,3... | collective-permute-start | bytes 73736 | tf_op jit(solution)/shard_map/ppermute | solution.py:566
  5.4 5.1 %collective-permute-start.1 = (bf16[96,128]{1,0:T(8,128)(2,1)S(1)}, bf16[96,128]{1,0:T(8,128)(2,1)S(1)}, u32[]{:S(2)}, u32[]{:S(2)}) collective-permute-start(bf16[96,128]{1,0:T(8,128)(2,1)S(1)} %get-tuple-element.84), channel_id=1, source_target_pairs={{32,0},{64,32},{96,64},{128,96},{160,128},{192,160},{224,192},{33,... | collective-permute-start | bytes 73736 | tf_op jit(solution)/shard_map/ppermute | solution.py:567
  10.8 7.6 %collective-permute-start.2 = (bf16[18,96]{1,0:T(8,128)(2,1)S(1)}, bf16[18,96]{1,0:T(8,128)(2,1)S(1)}, u32[]{:S(2)}, u32[]{:S(2)}) collective-permute-start(bf16[18,96]{1,0:T(8,128)(2,1)S(1)} %pad_maximum_fusion.refs_4_), channel_id=1, source_target_pairs={{0,1},{1,2},{2,3},{3,4},{4,5},{5,6},{6,7},{7,8},{8,9},{9,10},{10,1... | collective-permute-start | bytes 10376 | tf_op jit(solution)/shard_map/ppermute | solution.py:574
  13.9 4.4 %collective-permute-start.3 = (bf16[18,96]{1,0:T(8,128)(2,1)S(1)}, bf16[18,96]{1,0:T(8,128)(2,1)S(1)}, u32[]{:S(2)}, u32[]{:S(2)}) collective-permute-start(bf16[18,96]{1,0:T(8,128)(2,1)S(1)} %pad_maximum_fusion.1), channel_id=1, source_target_pairs={{1,0},{2,1},{3,2},{4,3},{5,4},{6,5},{7,6},{8,7},{9,8},{10,9},{11,1... | collective-permute-start | bytes 10376 | tf_op jit(solution)/shard_map/ppermute | solution.py:575
  23.7 6.9 %collective-permute-start.4 = (f32[8,16,128]{2,1,0:T(8,128)S(1)}, f32[8,16,128]{2,1,0:T(8,128)S(1)}, u32[]{:S(2)}, u32[]{:S(2)}) collective-permute-start(f32[8,16,128]{2,1,0:T(8,128)S(1)} %get-tuple-element.50), channel_id=1, source_target_pairs={{0,1},{1,2},{2,3},{3,0},{4,5},{5,6},{6,7},{7,4},{8,9},{9,10},{10,1... | collective-permute-start | bytes 196616 | tf_op jit(solution)/shard_map/ppermute | solution.py:623
  25.8 7.7 %collective-permute-start.5 = (f32[8,16,128]{2,1,0:T(8,128)S(1)}, f32[8,16,128]{2,1,0:T(8,128)S(1)}, u32[]{:S(2)}, u32[]{:S(2)}) collective-permute-start(f32[8,16,128]{2,1,0:T(8,128)S(1)} %get-tuple-element.51), channel_id=1, source_target_pairs={{0,2},{1,3},{2,0},{3,1},{4,6},{5,7},{6,4},{7,5},{8,10},{9,11},{10,... | collective-permute-start | bytes 196616 | tf_op jit(solution)/shard_map/ppermute | solution.py:623
  29.8 3.8 %collective-permute-start.6 = (f32[8,16,128]{2,1,0:T(8,128)S(1)}, f32[8,16,128]{2,1,0:T(8,128)S(1)}, u32[]{:S(2)}, u32[]{:S(2)}) collective-permute-start(f32[8,16,128]{2,1,0:T(8,128)S(1)} %get-tuple-element.52), channel_id=1, source_target_pairs={{0,3},{1,0},{2,1},{3,2},{4,7},{5,4},{6,5},{7,6},{8,11},{9,8},{10,9... | collective-permute-start | bytes 196616 | tf_op jit(solution)/shard_map/ppermute | solution.py:623
  33.7 3.4 %collective-permute-start.7 = (f32[8,16,128]{2,1,0:T(8,128)S(1)}, f32[8,16,128]{2,1,0:T(8,128)S(1)}, u32[]{:S(2)}, u32[]{:S(2)}) collective-permute-start(f32[8,16,128]{2,1,0:T(8,128)S(1)} %shard_map.94.refs_0_), channel_id=1, source_target_pairs={{0,4},{1,5},{2,6},{3,7},{4,0},{5,1},{6,2},{7,3},{8,12},{9,13},{10,... | collective-permute-start | bytes 196616 | tf_op jit(solution)/shard_map/ppermute | solution.py:631
  37.1 12.8 %collective-permute-start.10 = (f32[8,16,128]{2,1,0:T(8,128)S(1)}, f32[8,16,128]{2,1,0:T(8,128)S(1)}, u32[]{:S(2)}, u32[]{:S(2)}) collective-permute-start(f32[8,16,128]{2,1,0:T(8,128)S(1)} %shard_map.95), channel_id=1, source_target_pairs={{0,24},{1,25},{2,26},{3,27},{4,28},{5,29},{6,30},{7,31},{32,56},{3... | collective-permute-start | bytes 196616 | tf_op jit(solution)/shard_map/ppermute | solution.py:634
  44.6 5.3 %collective-permute-start.9 = (f32[8,16,128]{2,1,0:T(8,128)S(1)}, f32[8,16,128]{2,1,0:T(8,128)S(1)}, u32[]{:S(2)}, u32[]{:S(2)}) collective-permute-start(f32[8,16,128]{2,1,0:T(8,128)S(1)} %shard_map.95), channel_id=1, source_target_pairs={{0,16},{1,17},{2,18},{3,19},{4,20},{5,21},{6,22},{7,23},{8,24},{9,... | collective-permute-start | bytes 196616 | tf_op jit(solution)/shard_map/ppermute | solution.py:634
  47.7 3.5 %collective-permute-start.8 = (f32[8,16,128]{2,1,0:T(8,128)S(1)}, f32[8,16,128]{2,1,0:T(8,128)S(1)}, u32[]{:S(2)}, u32[]{:S(2)}) collective-permute-start(f32[8,16,128]{2,1,0:T(8,128)S(1)} %shard_map.95), channel_id=1, source_target_pairs={{0,8},{1,9},{2,10},{3,11},{4,12},{5,13},{6,14},{7,15},{8,16},{9,17... | collective-permute-start | bytes 196616 | tf_op jit(solution)/shard_map/ppermute | solution.py:634
  51.3 4.4 %collective-permute-start.11 = (f32[8,16,128]{2,1,0:T(8,128)S(1)}, f32[8,16,128]{2,1,0:T(8,128)S(1)}, u32[]{:S(2)}, u32[]{:S(2)}) collective-permute-start(f32[8,16,128]{2,1,0:T(8,128)S(1)} %get-tuple-element.56), channel_id=1, source_target_pairs={{0,1},{1,2},{2,3},{3,0},{4,5},{5,6},{6,7},{7,4},{8,9},{9,10},{10,1... | collective-permute-start | bytes 196616 | tf_op jit(solution)/shard_map/ppermute | solution.py:623
  51.7 5.5 %collective-permute-start.12 = (f32[8,16,128]{2,1,0:T(8,128)S(1)}, f32[8,16,128]{2,1,0:T(8,128)S(1)}, u32[]{:S(2)}, u32[]{:S(2)}) collective-permute-start(f32[8,16,128]{2,1,0:T(8,128)S(1)} %get-tuple-element.57), channel_id=1, source_target_pairs={{0,2},{1,3},{2,0},{3,1},{4,6},{5,7},{6,4},{7,5},{8,10},{9,11},{10,... | collective-permute-start | bytes 196616 | tf_op jit(solution)/shard_map/ppermute | solution.py:623
  54.9 3.1 %collective-permute-start.13 = (f32[8,16,128]{2,1,0:T(8,128)S(1)}, f32[8,16,128]{2,1,0:T(8,128)S(1)}, u32[]{:S(2)}, u32[]{:S(2)}) collective-permute-start(f32[8,16,128]{2,1,0:T(8,128)S(1)} %get-tuple-element.58), channel_id=1, source_target_pairs={{0,3},{1,0},{2,1},{3,2},{4,7},{5,4},{6,5},{7,6},{8,11},{9,8},{10,9... | collective-permute-start | bytes 196616 | tf_op jit(solution)/shard_map/ppermute | solution.py:623
  58.0 19.1 %copy-start.3 = (f32[3]{0:T(128)S(1)}, f32[3]{0:T(128)}, u32[]{:S(2)}) copy-start(f32[3]{0:T(128)} %refs_6_.3) | copy-start | bytes 40
  65.0 6.5 %collective-permute-start.14 = (f32[4,416,128]{2,1,0:T(8,128)S(1)}, f32[4,416,128]{2,1,0:T(8,128)S(1)}, u32[]{:S(2)}, u32[]{:S(2)}) collective-permute-start(f32[4,416,128]{2,1,0:T(8,128)S(1)} %get-tuple-element.60), channel_id=1, source_target_pairs={{0,32},{32,0},{64,96},{96,64},{128,160},{160,128},{192,224},{224,1... | collective-permute-start | bytes 2555912 | tf_op jit(solution)/shard_map/ppermute | solution.py:663
  71.7 12.2 %collective-permute-start.15 = (f32[416,128]{1,0:T(8,128)S(1)}, f32[416,128]{1,0:T(8,128)S(1)}, u32[]{:S(2)}, u32[]{:S(2)}) collective-permute-start(f32[416,128]{1,0:T(8,128)S(1)} %get-tuple-element.62), channel_id=1, source_target_pairs={{0,64},{32,96},{64,128},{96,160},{128,192},{160,224},{192,0},{224,... | collective-permute-start | bytes 638984 | tf_op jit(solution)/shard_map/ppermute | solution.py:660
  73.6 11.6 %collective-permute-start.16 = (f32[416,128]{1,0:T(8,128)S(1)}, f32[416,128]{1,0:T(8,128)S(1)}, u32[]{:S(2)}, u32[]{:S(2)}) collective-permute-start(f32[416,128]{1,0:T(8,128)S(1)} %get-tuple-element.63), channel_id=1, source_target_pairs={{0,128},{32,160},{64,192},{96,224},{128,0},{160,32},{192,64},{224,... | collective-permute-start | bytes 638984 | tf_op jit(solution)/shard_map/ppermute | solution.py:660
  75.7 9.6 %collective-permute-start.17 = (f32[416,128]{1,0:T(8,128)S(1)}, f32[416,128]{1,0:T(8,128)S(1)}, u32[]{:S(2)}, u32[]{:S(2)}) collective-permute-start(f32[416,128]{1,0:T(8,128)S(1)} %get-tuple-element.64), channel_id=1, source_target_pairs={{0,192},{32,224},{64,0},{96,32},{128,64},{160,96},{192,128},{224,1... | collective-permute-start | bytes 638984 | tf_op jit(solution)/shard_map/ppermute | solution.py:660
  85.5 11.4 %collective-permute-start.18 = (f32[384,128]{1,0:T(8,128)S(1)}, f32[384,128]{1,0:T(8,128)S(1)}, u32[]{:S(2)}, u32[]{:S(2)}) collective-permute-start(f32[384,128]{1,0:T(8,128)S(1)} %get-tuple-element.70), channel_id=1, source_target_pairs={{0,64},{32,96},{64,128},{96,160},{128,192},{160,224},{192,0},{224,... | collective-permute-start | bytes 589832 | tf_op jit(solution)/shard_map/ppermute | solution.py:660
  86.1 11.9 %collective-permute-start.19 = (f32[384,128]{1,0:T(8,128)S(1)}, f32[384,128]{1,0:T(8,128)S(1)}, u32[]{:S(2)}, u32[]{:S(2)}) collective-permute-start(f32[384,128]{1,0:T(8,128)S(1)} %get-tuple-element.71), channel_id=1, source_target_pairs={{0,128},{32,160},{64,192},{96,224},{128,0},{160,32},{192,64},{224,... | collective-permute-start | bytes 589832 | tf_op jit(solution)/shard_map/ppermute | solution.py:660
  89.3 8.7 %collective-permute-start.20 = (f32[384,128]{1,0:T(8,128)S(1)}, f32[384,128]{1,0:T(8,128)S(1)}, u32[]{:S(2)}, u32[]{:S(2)}) collective-permute-start(f32[384,128]{1,0:T(8,128)S(1)} %get-tuple-element.72), channel_id=1, source_target_pairs={{0,192},{32,224},{64,0},{96,32},{128,64},{160,96},{192,128},{224,1... | collective-permute-start | bytes 589832 | tf_op jit(solution)/shard_map/ppermute | solution.py:660
  98.3 3.4 %copy-start.2 = (bf16[192,96]{1,0:T(8,128)(2,1)S(1)}, bf16[192,96]{1,0:T(8,128)(2,1)}, u32[]{:S(2)}) copy-start(bf16[192,96]{1,0:T(8,128)(2,1)} %refs_7_.1) | copy-start | bytes 110596
  98.4 3.4 %copy-start.6 = (f32[192]{0:T(256)S(1)}, f32[192]{0:T(256)}, u32[]{:S(2)}) copy-start(f32[192]{0:T(256)} %param.16) | copy-start | bytes 2308
  98.4 3.3 %collective-permute-start.21 = (f32[4,384,128]{2,1,0:T(8,128)S(1)}, f32[4,384,128]{2,1,0:T(8,128)S(1)}, u32[]{:S(2)}, u32[]{:S(2)}) collective-permute-start(f32[4,384,128]{2,1,0:T(8,128)S(1)} %get-tuple-element.75.refs_2_), channel_id=1, source_target_pairs={{0,32},{32,0},{64,96},{96,64},{128,160},{160,128},{192,224},{224,1... | collective-permute-start | bytes 2359304 | tf_op jit(solution)/shard_map/ppermute | solution.py:701

commit v4 on v3

--- a/solution.py
+++ b/solution.py
@@ -72,8 +72,22 @@
 
 
 def project_kernel(
-    tok, in_weight, step_bias, decay_log, inner, gate, steps, compact, totals, conv_w, weight
+    tok,
+    in_weight,
+    conv_weight,
+    conv_bias,
+    step_bias,
+    decay_log,
+    inner,
+    gate,
+    steps,
+    compact,
+    totals,
+    conv_w,
+    taps,
+    weight,
 ):
+    load_taps(conv_weight, conv_bias, taps)
     source = in_weight[...].astype(f32)
     chan_b, chan_c = source[:, 384:400], source[:, 400:416]
     step_w = [jnp.broadcast_to(source[:, 416 + h : 417 + h], (WIDTH, HALF)) for h in range(3)]
@@ -123,7 +137,112 @@
     totals[...] = jnp.exp(whole).reshape(ROWS, 8, LANES)
 
 
-def entry_kernel(
+def pack_kernel(tok, left, right, *outs):
+    for out, r in zip(outs, (ROWS - 1, 0)):
+        sides = [left[r : r + 1, :].astype(f32), right[r : r + 1, :].astype(f32)]
+        sides = jnp.concatenate(sides + [jnp.zeros((14, WIDTH), f32)], axis=0)
+        sides = jnp.concatenate([sides, jnp.zeros((16, LANES - WIDTH), f32)], axis=1)
+        out[0:WIDTH, :] = tok[r]
+        out[WIDTH:, :] = sides.astype(bf16)
+
+
+def load_taps(conv_weight, conv_bias, taps):
+    for k in range(10):
+        v = conv_bias[...] if k == 9 else conv_weight[k // 3, k % 3 : k % 3 + 1, :]
+        taps[0, k : k + 1, :] = v[:, 0:128]
+        tail = [v[:, 128:192], v[:, 208:224], v[:, 208:224], v[:, 192:208]]
+        taps[1, k : k + 1, :] = jnp.concatenate(tail + [jnp.zeros((1, 16), f32)], axis=1)
+
+
+def conv_part(tokens, conv_w, dims):
+    return dot(tokens, conv_w[...], dims).astype(bf16).astype(f32)
+
+
+def put_sides(left, right, conv_w, proj, begins, first, count):
+    for ref, at in ((left, 7), (right, 136)):
+        out = conv_part(ref[...], conv_w, ((1,), (0,)))
+        for g in range(2):
+            proj[first : first + count, g, at, :] = out[
+                begins : begins + count, g * 128 : g * 128 + 128
+            ]
+
+
+def conv_row(proj, taps, at):
+    parts = []
+    for g in range(2):
+        acc = jnp.broadcast_to(taps[g, 9:10, :], (COLS, LANES))
+        for a in range(3):
+            for b in range(3):
+                k = a * 3 + b
+                acc = acc + taps[g, k : k + 1, :] * proj[at + a, g, 7 + b : 135 + b, :]
+        parts.append(silu(acc).astype(bf16).astype(f32))
+    return parts
+
+
+def finish_row(parts, steps, compact, totals, xdt, act, bct, ends):
+    turned = parts[1].T
+    chan_b = turned[96:112, :]
+    bct[0:16, :] = chan_b
+    bct[16:32, :] = turned[64:80, :]
+    other = pltpu.roll(parts[1], HALF, 1)
+    whole = [parts[0], jnp.where(low_lanes(COLS), parts[1], other)]
+    for g in range(2):
+        act[g] = whole[g].astype(bf16)
+        xdt[g] = steps[g] * whole[g]
+    weighted = [compact[h : h + 1, :] * chan_b for h in range(3)]
+    weighted = jnp.concatenate(split(jnp.concatenate(weighted, axis=0)), axis=0)
+    inner_x = jnp.concatenate(whole, axis=1).astype(bf16)
+    state = dot(weighted, inner_x, ((1,), (0,)))
+    state = state[0:48, :] + state[48:96, :]
+    first = jnp.where(low_lanes(16), state[0:16, 0:128], state[16:32, 0:128])
+    third = jnp.where(low_lanes(), state[32:40, 128:256], state[40:48, 128:256])
+    total = jnp.where(low_lanes(1), totals[0:1, :], totals[1:2, :])
+    rest = jnp.concatenate([total, totals[2:3, :], jnp.zeros((2, LANES), f32)], axis=0)
+    ends[0] = jnp.concatenate([first[0:8, :], third[0:4, :], rest], axis=0)
+    ends[1] = jnp.concatenate([first[8:16, :], third[4:8, :], rest], axis=0)
+    return other
+
+
+def inside_kernel(
+    inner,
+    left,
+    right,
+    steps,
+    compact,
+    totals,
+    conv_w,
+    taps,
+    decay_log,
+    xdt,
+    decay,
+    act,
+    bct,
+    cmap,
+    ends,
+    proj,
+):
+    put_sides(left, right, conv_w, proj, 0, 0, ROWS)
+    rate = [-jnp.exp(by_head(decay_log, g)) for g in range(2)]
+
+    def own_row(r):
+        for g in range(2):
+            proj[r, g, 8:136, :] = inner[r, g].astype(f32)
+            decay[r, g] = jnp.exp(rate[g] * steps[r, g])
+
+    each_row(own_row, 4)
+
+    def some(k, carry):
+        for i in range(2):
+            r = 1 + 2 * k + i
+            parts = conv_row(proj, taps, r - 1)
+            refs = [ref.at[r] for ref in (steps, compact, totals, xdt, act, bct)]
+            cmap[:, r, :] = finish_row(parts, *refs, ends.at[pl.ds(2 * r, 2)])
+        return carry
+
+    lax.fori_loop(0, ROWS // 2 - 1, some, 0)
+
+
+def edge_kernel(
     inner,
     above,
     below,
@@ -133,80 +252,45 @@
     compact,
     totals,
     conv_w,
-    conv_weight,
-    conv_bias,
-    decay_log,
+    taps,
+    cmap_in,
+    ends,
     xdt,
-    decay,
     act,
     bct,
     cmap,
     *refs,
 ):
-    ends_out, (proj, taps, ends) = refs[:CHIPS], refs[CHIPS:]
-    for ref, at, size in ((conv_weight, 0, 9), (conv_bias, 9, 1)):
-        v = ref[...]
-        taps[0, at : at + size, :] = v[:, 0:128]
-        tail = [v[:, 128:192], v[:, 208:224], v[:, 208:224], v[:, 192:208]]
-        taps[1, at : at + size, :] = jnp.concatenate(tail + [jnp.zeros((size, 16), f32)], axis=1)
-
-    def conv_part(tokens, dims):
-        return dot(tokens, conv_w[...], dims).astype(bf16).astype(f32)
-
-    for at, ref in ((0, above), (ROWS + 1, below)):
-        out = conv_part(ref[...], ((0,), (0,)))
+    ends_out, (proj, held) = refs[:CHIPS], refs[CHIPS:]
+    put_sides(left, right, conv_w, proj, 0, 1, 2)
+    put_sides(left, right, conv_w, proj, ROWS - 2, 3, 2)
+    for at, ref in ((0, above), (5, below)):
+        out = conv_part(ref[0:WIDTH, :], conv_w, ((0,), (0,)))
+        sides = conv_part(ref[WIDTH:, 0:WIDTH], conv_w, ((1,), (0,)))
         for g in range(2):
             proj[at, g, 8:136, :] = out[:, g * 128 : g * 128 + 128]
-    for ref, at in ((left, 7), (right, 136)):
-        out = conv_part(ref[...], ((1,), (0,)))
+            proj[at, g, 7:8, :] = sides[0:1, g * 128 : g * 128 + 128]
+            proj[at, g, 136:137, :] = sides[1:2, g * 128 : g * 128 + 128]
+    for at, r in ((1, 0), (2, 1), (3, ROWS - 2), (4, ROWS - 1)):
         for g in range(2):
-            proj[:, g, at, :] = out[0 : ROWS + 2, g * 128 : g * 128 + 128]
-
-    def own_row(r):
-        for g in range(2):
-            proj[r + 1, g, 8:136, :] = inner[r, g].astype(f32)
-
-    each_row(own_row, 4)
-    rate = [-jnp.exp(by_head(decay_log, g)) for g in range(2)]
-
-    def conv_row(r):
-        parts = []
-        for g in range(2):
-            acc = jnp.broadcast_to(taps[g, 9:10, :], (COLS, LANES))
-            for a in range(3):
-                for b in range(3):
-                    k = a * 3 + b
-                    acc = acc + taps[g, k : k + 1, :] * proj[r + a, g, 7 + b : 135 + b, :]
-            parts.append(silu(acc).astype(bf16).astype(f32))
-        turned = parts[1].T
-        chan_b = turned[96:112, :]
-        bct[r, 0:16, :] = chan_b
-        bct[r, 16:32, :] = turned[64:80, :]
-        other = pltpu.roll(parts[1], HALF, 1)
-        cmap[:, r, :] = other
-        parts[1] = jnp.where(low_lanes(COLS), parts[1], other)
-        for g in range(2):
-            act[r, g] = parts[g].astype(bf16)
-            step = steps[r, g]
-            xdt[r, g] = step * parts[g]
-            decay[r, g] = jnp.exp(rate[g] * step)
-        weighted = [compact[r, h : h + 1, :] * chan_b for h in range(3)]
-        weighted = jnp.concatenate(split(jnp.concatenate(weighted, axis=0)), axis=0)
-        inner_x = jnp.concatenate([act[r, 0], act[r, 1]], axis=1)
-        state = dot(weighted, inner_x, ((1,), (0,)))
-        state = state[0:48, :] + state[48:96, :]
-        first = jnp.where(low_lanes(16), state[0:16, 0:128], state[16:32, 0:128])
-        third = jnp.where(low_lanes(), state[32:40, 128:256], state[40:48, 128:256])
-        total = jnp.where(low_lanes(1), totals[r, 0:1, :], totals[r, 1:2, :])
-        rest = jnp.concatenate([total, totals[r, 2:3, :], jnp.zeros((2, LANES), f32)], axis=0)
-        quarter, at = r // 4, (r % 4) * 2
-        ends[quarter, at] = jnp.concatenate([first[0:8, :], third[0:4, :], rest], axis=0)
-        ends[quarter, at + 1] = jnp.concatenate([first[8:16, :], third[4:8, :], rest], axis=0)
-
-    each_row(conv_row, 2)
+            proj[at, g, 8:136, :] = inner[r, g].astype(f32)
+    held[...] = ends[...]
+    cmap[...] = cmap_in[...]
+    for e, r in enumerate((0, ROWS - 1)):
+        parts = conv_row(proj, taps, 3 * e)
+        own = [ref.at[r] for ref in (steps, compact, totals)]
+        mine = [ref.at[e] for ref in (xdt, act, bct)]
+        cmap[:, r, :] = finish_row(parts, *own, *mine, held.at[pl.ds(2 * r, 2)])
     member, _ = line()
     for k, out in enumerate(ends_out):
-        out[...] = ends[(member + k) % CHIPS]
+        out[...] = held[pl.ds((member + k) % CHIPS * 8, 8)]
+
+
+def row_of(pair, r):
+    inside, edge = pair
+    if r in (0, ROWS - 1):
+        return edge.at[0 if r == 0 else 1]
+    return inside.at[r]
 
 
 def line():
@@ -282,51 +366,111 @@
     return [carry[2 * r, 0:8, :], carry[2 * r + 1, 0:8, :], third]
 
 
-def bottom_kernel(xdt, decay, bct, *refs):
-    parts, (mine, theirs, carry, hold) = refs[:CHIPS], refs[CHIPS:]
-    core = lax.axis_index("gy") % 2
-    member, _ = line()
-    for k, part in enumerate(parts):
-        carry[pl.ds((member + CHIPS - k) % CHIPS * 8, 8)] = part[...]
+def bottom_kernel(xdt_in, xdt_edge, decay, bct_in, bct_edge, *refs, half):
+    if half:
+        state_in, bottom = refs
+        begin = [state_in[i] for i in range(3 * ROWS)]
+    else:
+        bottom, state_out = refs
+        begin = [jnp.zeros((8, LANES), f32)] * (3 * ROWS)
     low = low_lanes()
-    begin = []
-    for r in range(ROWS):
-        begin += starts(carry, r)
-
-    def block(cb, state):
+    xdt = [row_of((xdt_in, xdt_edge), r) for r in range(ROWS)]
+    bct = [row_of((bct_in, bct_edge), r) for r in range(ROWS)]
+
+    def block(k, state):
         state = list(state)
-        base = pl.multiple_of(cb * BLOCK, BLOCK)
-        maps = [pltpu.roll(bct[r, 0:16, :], COLS - base, 1) for r in range(ROWS)]
+        base = pl.multiple_of((half * HALVED + k) * BLOCK, BLOCK)
+        maps = [pltpu.roll(bct[r][0:16, :], COLS - base, 1) for r in range(ROWS)]
         for j in range(BLOCK):
             cols = [jnp.zeros((8, LANES), f32)] * 3
             for r in range(ROWS):
                 wide = [spread(maps[r], q, j) for q in range(2)]
                 wide.append(jnp.where(low, wide[0], wide[1]))
-                x = [xdt[r, g, pl.ds(base + j, 8, stride=0), :] for g in range(2)]
+                x = [xdt[r][g, pl.ds(base + j, 8, stride=0), :] for g in range(2)]
                 d = [decay[r, g, pl.ds(base + j, 8, stride=0), :] for g in range(2)]
                 for q in range(3):
                     g = q // 2
                     state[3 * r + q] = d[g] * state[3 * r + q] + x[g] * wide[q]
                     cols[q] = d[g] * cols[q] + state[3 * r + q]
             for q in range(3):
-                hold[j * 24 + 8 * q : j * 24 + 8 * q + 8, :] = cols[q]
+                bottom[k, j * 24 + 8 * q : j * 24 + 8 * q + 8, :] = cols[q]
         for g in range(2):
-            product = decay[0, g, pl.ds(base, BLOCK), :]
+            whole = decay[0, g, pl.ds(base, BLOCK), :]
             for r in range(1, ROWS):
-                product = product * decay[r, g, pl.ds(base, BLOCK), :]
-            hold[384 + 16 * g : 400 + 16 * g, :] = product
-
-        @pl.when(cb // HALVED == core)
-        def _():
-            mine[cb % HALVED] = hold[...]
-
-        @pl.when(cb // HALVED != core)
-        def _():
-            theirs[cb % HALVED] = hold[...]
-
+                whole = whole * decay[r, g, pl.ds(base, BLOCK), :]
+            bottom[k, 384 + 16 * g : 400 + 16 * g, :] = whole
         return tuple(state)
 
-    lax.fori_loop(0, BLOCKS, block, tuple(begin))
+    state = lax.fori_loop(0, HALVED, block, tuple(begin))
+    if not half:
+        for i in range(3 * ROWS):
+            state_out[i] = state[i]
+
+
+def weight_kernel(steps, decay, decay_log, coef):
+    row_at = lax.broadcasted_iota(jnp.int32, (COLS, 2 * COLS), 0)
+    col_at = lax.broadcasted_iota(jnp.int32, (COLS, 2 * COLS), 1) & (COLS - 1)
+    upto = jnp.where(col_at <= row_at, 1.0, 0.0).astype(bf16)
+    rate = [-jnp.exp(by_head(decay_log, g)) for g in range(2)]
+    rate = jnp.concatenate(rate, axis=1)
+
+    def some(k, below):
+        below = list(below)
+        for i in range(4):
+            r = ROWS - 1 - (k * 4 + i)
+            along = rate * jnp.concatenate([steps[r, 0], steps[r, 1]], axis=1)
+            along = dot(upto, jnp.concatenate(split(along), axis=0), ((1,), (0,)))
+            along = jnp.exp(along)
+            for g in range(2):
+                coef[r, g] = along[:, g * 128 : g * 128 + 128] * below[g]
+                below[g] = below[g] * decay[r, g]
+        return tuple(below)
+
+    lax.fori_loop(0, ROWS // 4, some, (jnp.ones((COLS, LANES), f32),) * 2)
+
+
+def add_kernel(coef, left_half, right_half, *refs):
+    parts, (mine, theirs, carry, hold) = refs[:CHIPS], refs[CHIPS:]
+    core, _ = place()
+    member, _ = line()
+    for k, part in enumerate(parts):
+        carry[pl.ds((member + CHIPS - k) % CHIPS * 8, 8)] = part[...]
+    for r in range(ROWS):
+        hold[3 * r], hold[3 * r + 1], hold[3 * r + 2] = starts(carry, r)
+
+    def block(k, _, source, out, base):
+        for at in range(0, BLOCK, 4):
+            sums = [
+                source[k, 24 * j + 8 * q : 24 * j + 8 * q + 8, :]
+                for j in range(at, at + 4)
+                for q in range(3)
+            ]
+            for r in range(ROWS):
+                tiles = [hold[3 * r + q] for q in range(3)]
+                for j in range(4):
+                    c = base + k * BLOCK + at + j
+                    w = [coef[r, g, pl.ds(c, 8, stride=0), :] for g in range(2)]
+                    for q in range(3):
+                        sums[3 * j + q] = sums[3 * j + q] + w[q // 2] * tiles[q]
+            for j in range(4):
+                for q in range(3):
+                    row = 24 * (at + j) + 8 * q
+                    out[k, row : row + 8, :] = sums[3 * j + q]
+        out[k, 384:416, :] = source[k, 384:416, :]
+        return 0
+
+    def both(outs):
+        for half, source in enumerate((left_half, right_half)):
+            run = functools.partial(block, source=source, out=outs[half], base=half * HALF)
+            lax.fori_loop(0, HALVED, run, 0)
+
+    @pl.when(core == 0)
+    def _():
+        both((mine, theirs))
+
+    @pl.when(core != 0)
+    def _():
+        both((theirs, mine))
 
 
 def gating_kernel(decay, gate, gating, reach):
@@ -346,12 +490,28 @@
     lax.fori_loop(0, ROWS // 4, some, tuple(along))
 
 
-def local_kernel(begins, xdt, decay, bct, carry, act, gating, skip_gain, *refs):
+def local_kernel(
+    begins,
+    xdt_in,
+    xdt_edge,
+    decay,
+    bct_in,
+    bct_edge,
+    carry,
+    act_in,
+    act_edge,
+    gating,
+    skip_gain,
+    *refs,
+):
     if begins:
         track_in, gated, local = refs
     else:
         gated, track, local = refs
     low = low_lanes()
+    xdt = [row_of((xdt_in, xdt_edge), r) for r in range(ROWS)]
+    bct = [row_of((bct_in, bct_edge), r) for r in range(ROWS)]
+    act = [row_of((act_in, act_edge), r) for r in range(ROWS)]
     count = ROWS // 2
     begin = []
     for i in range(count):
@@ -360,7 +520,7 @@
     def block(cb, state):
         state = list(state)
         base = cb * BLOCK
-        maps = [pltpu.roll(bct[begins + i], COLS - base, 1) for i in range(count)]
+        maps = [pltpu.roll(bct[begins + i][...], COLS - base, 1) for i in range(count)]
         for j in range(BLOCK):
             if begins:
                 cols = [track_in[cb, j * 24 + 8 * q : j * 24 + 8 * q + 8, :] for q in range(3)]
@@ -371,7 +531,7 @@
                 r = begins + i
                 wide = [spread(maps[i], q, j) for q in range(4)]
                 b_all = [wide[0], wide[1], jnp.where(low, wide[0], wide[1])]
-                x = [xdt[r, g, pl.ds(base + j, 8, stride=0), :] for g in range(2)]
+                x = [xdt[r][g, pl.ds(base + j, 8, stride=0), :] for g in range(2)]
                 d = [decay[r, g, pl.ds(base + j, 8, stride=0), :] for g in range(2)]
                 for q in range(3):
                     g = q // 2
@@ -393,7 +553,7 @@
             mixed = local[i // 4, (i % 4) * 2 + g]
             if g == 1:
                 mixed = mixed + pltpu.roll(mixed, HALF, 1)
-            mixed = mixed + by_head(skip_gain, g) * act[r, g].astype(f32)
+            mixed = mixed + by_head(skip_gain, g) * act[r][g].astype(f32)
             gated[i, g] = mixed * gating[r, g]
 
 
@@ -563,44 +723,65 @@
 ):
     to_right, to_left = steps("gx")
     to_down, to_up = steps("gy")
-    above = lax.ppermute(tokens[ROWS - 1], "gy", to_down)
-    below = lax.ppermute(tokens[0], "gy", to_up)
-
-    def edge(c):
-        column = [above[None, :, c], tokens[:, :, c], below[None, :, c]]
-        return jnp.concatenate(column, axis=0)
-
-    last, first = edge(COLS - 1), edge(0)
+    last, first = tokens[:, :, COLS - 1], tokens[:, :, 0]
     left = lax.ppermute(last, "gx", to_right)
     right = lax.ppermute(first, "gx", to_left)
     vmem = pltpu.VMEM
     rows8 = ((ROWS, 8, LANES), f32, "v")
-    inner, gate, step, compact, totals, conv_w = call(
+    inner, gate, step, compact, totals, conv_w, taps = call(
         project_kernel,
-        "vvss",
+        "vvvvss",
         [(PLANE, bf16, "v"), (PLANE, bf16, "v"), (PLANE, f32, "v"), rows8, rows8]
-        + [((WIDTH, 256), bf16, "v")],
+        + [((WIDTH, 256), bf16, "v"), ((2, 16, LANES), f32, "v")],
         [vmem((WIDTH, 768), bf16)],
         tokens,
         in_weight,
+        conv_weight,
+        conv_bias.reshape(1, 224),
         step_bias,
         decay_log,
-        after=(last,),
-    )
+        after=(last, first),
+    )
+    edge_row = ((WIDTH + 16, LANES), bf16, "v")
+    down_row, up_row = call(
+        pack_kernel, "vvv", [edge_row] * 2, [], tokens, left, right, after=(conv_w,)
+    )
+    above = lax.ppermute(down_row, "gy", to_down)
+    below = lax.ppermute(up_row, "gy", to_up)
     packet = ((8, 16, LANES), f32, "v")
     quarters = vmem((CHIPS,) + packet[0], f32)
-    xdt, decay, act, bct, cmap, *ends = call(
-        entry_kernel,
-        "vvvvvvvvvvvs",
+    all_ends = ((2 * ROWS, 16, LANES), f32, "v")
+    cells = ((COLS, ROWS, LANES), f32, "v")
+    xdt, decay, act, bct, cmap, ends = call(
+        inside_kernel,
+        "v" * 8 + "s",
         [
             (PLANE, f32, "v"),
             (PLANE, f32, "v"),
             (PLANE, bf16, "v"),
             ((ROWS, 32, COLS), f32, "v"),
-            ((COLS, ROWS, LANES), f32, "v"),
-        ]
+            cells,
+            all_ends,
+        ],
+        [vmem((ROWS, 2, 144, LANES), f32)],
+        inner,
+        left,
+        right,
+        step,
+        compact,
+        totals,
+        conv_w,
+        taps,
+        decay_log,
+        after=(up_row, down_row),
+    )
+    two = (2,) + PLANE[1:]
+    xdt_edge, act_edge, bct_edge, cmap, *ends = call(
+        edge_kernel,
+        "v" * 12,
+        [(two, f32, "v"), (two, bf16, "v"), ((2, 32, COLS), f32, "v"), cells]
         + [packet] * CHIPS,
-        [vmem((ROWS + 2, 2, 144, LANES), f32), vmem((2, 16, LANES), f32), quarters],
+        [vmem((6, 2, 144, LANES), f32), vmem(all_ends[0], f32)],
         inner,
         above,
         below,
@@ -610,10 +791,11 @@
         compact,
         totals,
         conv_w,
-        conv_weight.reshape(9, 224),
-        conv_bias.reshape(1, 224),
-        decay_log,
-    )
+        taps,
+        cmap,
+        ends,
+    )
+    scanned = (xdt, xdt_edge, decay, bct, bct_edge)
     gx_count = lax.axis_size("gx")
 
     def members(pieces):
@@ -623,31 +805,54 @@
             moved[k] = lax.ppermute(pieces[k], "gx", pairs)
         return moved
 
+    piece, piece_out = (PIECE, f32, "v"), (PIECE_OUT, f32, "v")
+    halves = ((HALVED,) + PIECE, f32, "v")
+    tiles = ((3 * ROWS, 8, LANES), f32, "v")
+    sent = ends[:1]
+    left_half, middle = call(
+        functools.partial(bottom_kernel, half=0),
+        "vvvvv",
+        [halves, tiles],
+        [],
+        *scanned,
+        after=sent,
+    )
+    ends = members(ends)
+    (whole,) = call(members_kernel, "vvvv", [packet], [quarters], *ends, after=(middle,))
+    beside = lax.ppermute(whole, "gx", [(i, i ^ 4) for i in range(gx_count)])
     gating, reach = call(
-        gating_kernel, "vv", [(PLANE, f32, "v")] * 2, [], decay, gate, after=ends[:1]
-    )
-    ends = members(ends)
-    (whole,) = call(members_kernel, "vvvv", [packet], [quarters], *ends, after=(reach,))
-    beside = lax.ppermute(whole, "gx", [(i, i ^ 4) for i in range(gx_count)])
-    (both,) = call(pair_kernel, "vv", [packet], [], whole, beside)
+        gating_kernel, "vv", [(PLANE, f32, "v")] * 2, [], decay, gate, after=(whole,)
+    )
+    (both,) = call(pair_kernel, "vv", [packet], [], whole, beside, after=(reach,))
+    (right_half,) = call(
+        functools.partial(bottom_kernel, half=1),
+        "vvvvvv",
+        [halves],
+        [],
+        *scanned,
+        middle,
+        after=(both,),
+    )
     mid, near, far = [
         lax.ppermute(both, "gx", [(i, i + 8 * k) for i in range(gx_count - 8 * k)])
         for k in (2, 1, 3)
     ]
     carries = call(
-        carry_kernel, "v" * 8, [packet] * CHIPS, [quarters], near, mid, far, beside, *ends
+        carry_kernel, "v" * 8, [packet] * CHIPS, [quarters], near, mid, far, beside, *ends,
+        after=(right_half,),
+    )
+    (coef,) = call(
+        weight_kernel, "vvs", [(PLANE, f32, "v")], [], step, decay, decay_log, after=carries[:1]
     )
     carries = members(carries)
-    piece, piece_out = (PIECE, f32, "v"), (PIECE_OUT, f32, "v")
-    halves = ((HALVED,) + PIECE, f32, "v")
     mine, theirs, carry = call(
-        bottom_kernel,
+        add_kernel,
         "v" * 7,
         [halves, halves, ((2 * ROWS, 16, LANES), f32, "v")],
-        [vmem(PIECE, f32)],
-        xdt,
-        decay,
-        bct,
+        [vmem(tiles[0], f32)],
+        coef,
+        left_half,
+        right_half,
         *carries,
     )
     gy_count = lax.axis_size("gy")
@@ -665,10 +870,10 @@
     pieces = rotate(joined)
     half = ((ROWS // 2,) + PLANE[1:], f32, "v")
     local_scratch = vmem((2, 8, COLS, LANES), f32)
-    inner = (xdt, decay, bct, carry, act, gating, skip_gain)
+    inner = (*scanned, carry, act, act_edge, gating, skip_gain)
     gated_a, track = call(
         functools.partial(local_kernel, 0),
-        "vvvvvvs",
+        "v" * 9 + "s",
         [half, ((BLOCKS,) + PIECE_OUT, f32, "v")],
         [local_scratch],
         *inner,
@@ -686,7 +891,7 @@
     pieces = rotate(pieces)
     (gated_b,) = call(
         functools.partial(local_kernel, ROWS // 2),
-        "vvvvvvsv",
+        "v" * 9 + "sv",
         [half],
         [local_scratch],
         *inner,

time: 106 us -> 102 us (0.962)
  waiting for transfers between devices: 15.2 us -> 7.79 us
  Pallas kernels: 36.4 us -> 40 us
  local copies, waits for them, and re-layouts: 2.92 us -> 1.77 us
    ppermute x6, waiting for transfers between devices: 6.18 us -> 1.99 us  [members(): moved[k] = lax.ppermute(pieces[k], 'gx', pairs)]
    pallas_call x14 -> x19, Pallas kernels: 36.4 us -> 40 us  [call(): pl.pallas_call(inner, in_specs=[pl.BlockSpec(memory_space=kinds[k]) for k...]
    ppermute x2, waiting for transfers between devices: 1.32 us -> 0.01 us  [the longest x1 0.01 us: on_device(): below = lax.ppermute(up_row, 'gy', to_up)]
    ppermute x3, waiting for transfers between devices: 1.3 us -> 0.01 us  [on_device(): lax.ppermute(both, 'gx', [(i, i + 8 * k) for i in range(gx_count - 8 * k)])]
  transfers between devices with their start and end apart: 22 -> 22, of which waited for: 12 -> 10; matrix products, arithmetic and copies ran while one was open for 2% -> 0% of each run, Pallas kernels for 18% -> 32%
where the time goes in v4:
time: 102 us; the launch traced here: 101 us
  starting transfers between devices  51.3 us (50%)
  Pallas kernels  40 us (39%)
  waiting for transfers between devices  7.79 us (8%)
  local copies, waits for them, and re-layouts  1.77 us (2%)
    pallas_call x19, Pallas kernels, call(): pl.pallas_call(inner, in_specs=[pl.BlockSpec(memory_space=kinds[k]) for k...  40 us
    ppermute x3, starting transfers between devices, on_device(): lax.ppermute(both, 'gx', [(i, i + 8 * k) for i in range(gx_count - 8 * k)])  12.4 us
    ppermute x6, starting transfers between devices, members(): moved[k] = lax.ppermute(pieces[k], 'gx', pairs)  10.1 us
    ppermute x6, starting transfers between devices, rotate(): moved[k] = lax.ppermute(pieces[k], 'gy', ahead[k])  9.8 us
    ppermute x1, starting transfers between devices, on_device(): left = lax.ppermute(last, 'gx', to_right)  3.94 us
    ppermute x1, starting transfers between devices, on_device(): below = lax.ppermute(up_row, 'gy', to_up)  3.91 us
    ppermute x1, starting transfers between devices, on_device(): theirs = lax.ppermute(theirs, 'gy', swap)  3.61 us
    ppermute x1, starting transfers between devices, on_device(): above = lax.ppermute(down_row, 'gy', to_down)  3.1 us
  transfers between devices with their start and end apart: 22, of which 10 were waited for; matrix products, arithmetic and copies ran while one was open for 0% of the time, Pallas kernels for 32%

profile of v4, /device:TPU:1, one launch (start us, length us, event | category | flops | bytes accessed | tf_op | source)
XLA Modules:
  0.0 101.3 jit_solution(15772063402622726169)
XLA Ops:
  0.0 1.3 %fusion = (bf16[16,96,1]{2,1,0:T(8,128)(2,1)S(1)}, bf16[16,96,1]{2,1,0:T(8,128)(2,1)S(1)}) fusion(bf16[16,96,128]{2,1,0:T(8,128)(2,1)} %refs_0_.3), kind=kLoop, calls=%fused_computation | loop fusion | bytes 12288 | tf_op jit(solution)/shard_map/slice | solution.py:726
  1.6 3.9 %collective-permute-start = (bf16[16,96]{1,0:T(8,128)(2,1)S(1)}, bf16[16,96]{1,0:T(8,128)(2,1)S(1)}, u32[]{:S(2)}, u32[]{:S(2)}) collective-permute-start(bf16[16,96]{1,0:T(8,128)(2,1)S(1)} %bitcast.4), channel_id=1, source_target_pairs={{0,1},{1,2},{2,3},{3,4},{4,5},{5,6},{6,7},{7,8},{8,9},{9,10},{10,1... | collective-permute-start | bytes 9224 | tf_op jit(solution)/shard_map/ppermute | solution.py:727
  5.7 1.3 %collective-permute-start.1 = (bf16[16,96]{1,0:T(8,128)(2,1)S(1)}, bf16[16,96]{1,0:T(8,128)(2,1)S(1)}, u32[]{:S(2)}, u32[]{:S(2)}) collective-permute-start(bf16[16,96]{1,0:T(8,128)(2,1)S(1)} %bitcast.6), channel_id=1, source_target_pairs={{1,0},{2,1},{3,2},{4,3},{5,4},{6,5},{7,6},{8,7},{9,8},{10,9},{11,1... | collective-permute-start | bytes 9224 | tf_op jit(solution)/shard_map/ppermute | solution.py:728
  7.1 3.1 %shard_map.91 = (bf16[16,2,128,128]{3,2,1,0:T(8,128)(2,1)S(1)}, bf16[16,2,128,128]{3,2,1,0:T(8,128)(2,1)S(1)}, f32[16,2,128,128]{3,2,1,0:T(8,128)S(1)}, f32[16,8...) custom-call(bf16[16,96,128]{2,1,0:T(8,128)(2,1)S(1)} %copy-done, ...), custom_call_target="tpu_custom_call" | custom-call | tf_op jit(solution)/shard_map/pallas_call | solution.py:697
  10.2 3.9 %collective-permute-start.3 = (bf16[112,128]{1,0:T(8,128)(2,1)S(1)}, bf16[112,128]{1,0:T(8,128)(2,1)S(1)}, u32[]{:S(2)}, u32[]{:S(2)}) collective-permute-start(bf16[112,128]{1,0:T(8,128)(2,1)S(1)} %get-tuple-element.57.refs_9_), channel_id=1, source_target_pairs={{32,0},{64,32},{96,64},{128,96},{160,128},{192,160},{224,192},{33,... | collective-permute-start | bytes 86024 | tf_op jit(solution)/shard_map/ppermute | solution.py:750
  14.1 3.1 %collective-permute-start.2 = (bf16[112,128]{1,0:T(8,128)(2,1)S(1)}, bf16[112,128]{1,0:T(8,128)(2,1)S(1)}, u32[]{:S(2)}, u32[]{:S(2)}) collective-permute-start(bf16[112,128]{1,0:T(8,128)(2,1)S(1)} %get-tuple-element.58.refs_10_), channel_id=1, source_target_pairs={{0,32},{32,64},{64,96},{96,128},{128,160},{160,192},{192,224},{1,3... | collective-permute-start | bytes 86024 | tf_op jit(solution)/shard_map/ppermute | solution.py:749
  17.2 4.4 %shard_map.93 = (f32[16,2,128,128]{3,2,1,0:T(8,128)S(1)}, f32[16,2,128,128]{3,2,1,0:T(8,128)S(1)}, bf16[16,2,128,128]{3,2,1,0:T(8,128)(2,1)S(1)}, f32[16,32,128]...) custom-call(bf16[16,2,128,128]{3,2,1,0:T(8,128)(2,1)S(1)} %get-tuple-element.52.refs_0_, ...), custom_call_target="tpu_custom_call" | custom-call | tf_op jit(solution)/shard_map/pallas_call | solution.py:697
  22.4 1.4 %collective-permute-start.4 = (f32[8,16,128]{2,1,0:T(8,128)S(1)}, f32[8,16,128]{2,1,0:T(8,128)S(1)}, u32[]{:S(2)}, u32[]{:S(2)}) collective-permute-start(f32[8,16,128]{2,1,0:T(8,128)S(1)} %get-tuple-element.63), channel_id=1, source_target_pairs={{0,1},{1,2},{2,3},{3,0},{4,5},{5,6},{6,7},{7,4},{8,9},{9,10},{10,1... | collective-permute-start | bytes 196616 | tf_op jit(solution)/shard_map/ppermute | solution.py:805
  23.8 4.8 %collective-permute-start.5 = (f32[8,16,128]{2,1,0:T(8,128)S(1)}, f32[8,16,128]{2,1,0:T(8,128)S(1)}, u32[]{:S(2)}, u32[]{:S(2)}) collective-permute-start(f32[8,16,128]{2,1,0:T(8,128)S(1)} %get-tuple-element.64), channel_id=1, source_target_pairs={{0,2},{1,3},{2,0},{3,1},{4,6},{5,7},{6,4},{7,5},{8,10},{9,11},{10,... | collective-permute-start | bytes 196616 | tf_op jit(solution)/shard_map/ppermute | solution.py:805
  28.6 3.4 %shard_map.95 = (f32[4,416,128]{2,1,0:T(8,128)S(1)}, f32[48,8,128]{2,1,0:T(8,128)S(1)}) custom-call(f32[16,2,128,128]{3,2,1,0:T(8,128)S(1)} %get-tuple-element.66.refs_0_, f32[2,2,128,128]{3,2,1,0:T(8,128)S(1)} %get-tuple-element.67.refs_1_, f32[16,2,128,128]{3,2,1,0:T(8,128)S(1)} %get-tuple-element.59.refs_2_.refs_0_.refs_1_, ...), custom_call_target="tpu_custom_call" | custom-call | tf_op jit(solution)/shard_map/pallas_call | solution.py:697
  32.4 1.7 %collective-permute-start.7 = (f32[8,16,128]{2,1,0:T(8,128)S(1)}, f32[8,16,128]{2,1,0:T(8,128)S(1)}, u32[]{:S(2)}, u32[]{:S(2)}) collective-permute-start(f32[8,16,128]{2,1,0:T(8,128)S(1)} %shard_map.96.refs_2_.refs_0_), channel_id=1, source_target_pairs={{0,4},{1,5},{2,6},{3,7},{4,0},{5,1},{6,2},{7,3},{8,12},{9,13},{10,... | collective-permute-start | bytes 196616 | tf_op jit(solution)/shard_map/ppermute | solution.py:822
  35.8 7.2 %collective-permute-start.10 = (f32[8,16,128]{2,1,0:T(8,128)S(1)}, f32[8,16,128]{2,1,0:T(8,128)S(1)}, u32[]{:S(2)}, u32[]{:S(2)}) collective-permute-start(f32[8,16,128]{2,1,0:T(8,128)S(1)} %shard_map.98.refs_6_), channel_id=1, source_target_pairs={{0,24},{1,25},{2,26},{3,27},{4,28},{5,29},{6,30},{7,31},{32,56},{3... | collective-permute-start | bytes 196616 | tf_op jit(solution)/shard_map/ppermute | solution.py:837
  43.0 3.0 %collective-permute-start.9 = (f32[8,16,128]{2,1,0:T(8,128)S(1)}, f32[8,16,128]{2,1,0:T(8,128)S(1)}, u32[]{:S(2)}, u32[]{:S(2)}) collective-permute-start(f32[8,16,128]{2,1,0:T(8,128)S(1)} %shard_map.98.refs_6_), channel_id=1, source_target_pairs={{0,16},{1,17},{2,18},{3,19},{4,20},{5,21},{6,22},{7,23},{8,24},{9,... | collective-permute-start | bytes 196616 | tf_op jit(solution)/shard_map/ppermute | solution.py:837
  46.0 2.3 %collective-permute-start.8 = (f32[8,16,128]{2,1,0:T(8,128)S(1)}, f32[8,16,128]{2,1,0:T(8,128)S(1)}, u32[]{:S(2)}, u32[]{:S(2)}) collective-permute-start(f32[8,16,128]{2,1,0:T(8,128)S(1)} %shard_map.98.refs_6_), channel_id=1, source_target_pairs={{0,8},{1,9},{2,10},{3,11},{4,12},{5,13},{6,14},{7,15},{8,16},{9,17... | collective-permute-start | bytes 196616 | tf_op jit(solution)/shard_map/ppermute | solution.py:837
  48.3 3.4 %shard_map.99.refs_8_.refs_2_ = f32[4,416,128]{2,1,0:T(8,128)S(1)} custom-call(f32[16,2,128,128]{3,2,1,0:T(8,128)S(1)} %get-tuple-element.66.refs_0_, f32[2,2,128,128]{3,2,1,0:T(8,128)S(1)} %get-tuple-element.67.refs_1_, f32[16,2,128,128]{3,2,1,0:T(8,128)S(1)} %get-tuple-element.59.refs_2_.refs_0_.refs_1_, f32[16,32,128]{2,1,0:T(8,128)S(1)} %get-tuple-element.68.refs_3_, ...), custom_call_target="tpu_custom_call" | custom-call | tf_op jit(solution)/shard_map/pallas_call | solution.py:697
  51.9 1.4 %collective-permute-start.11 = (f32[8,16,128]{2,1,0:T(8,128)S(1)}, f32[8,16,128]{2,1,0:T(8,128)S(1)}, u32[]{:S(2)}, u32[]{:S(2)}) collective-permute-start(f32[8,16,128]{2,1,0:T(8,128)S(1)} %get-tuple-element.75), channel_id=1, source_target_pairs={{0,1},{1,2},{2,3},{3,0},{4,5},{5,6},{6,7},{7,4},{8,9},{9,10},{10,1... | collective-permute-start | bytes 196616 | tf_op jit(solution)/shard_map/ppermute | solution.py:805
  53.3 2.5 %collective-permute-start.12 = (f32[8,16,128]{2,1,0:T(8,128)S(1)}, f32[8,16,128]{2,1,0:T(8,128)S(1)}, u32[]{:S(2)}, u32[]{:S(2)}) collective-permute-start(f32[8,16,128]{2,1,0:T(8,128)S(1)} %get-tuple-element.76), channel_id=1, source_target_pairs={{0,2},{1,3},{2,0},{3,1},{4,6},{5,7},{6,4},{7,5},{8,10},{9,11},{10,... | collective-permute-start | bytes 196616 | tf_op jit(solution)/shard_map/ppermute | solution.py:805
  55.8 1.7 %shard_map.101.refs_0_ = f32[16,2,128,128]{3,2,1,0:T(8,128)S(1)} custom-call(f32[16,2,128,128]{3,2,1,0:T(8,128)S(1)} %get-tuple-element.51.refs_3_.refs_5_.refs_0_, f32[16,2,128,128]{3,2,1,0:T(8,128)S(1)} %get-tuple-element.59.refs_2_.refs_0_.refs_1_, f32[3]{0:T(128)S(1)} %copy-done.4, f32[8,16,128]{2,1,0:T(8,128)S(1)} %get-tuple-element.73.refs_3_), custom_call_target="tpu_custom_call" | custom-call | tf_op jit(solution)/shard_map/pallas_call | solution.py:697
  59.2 2.2 %shard_map.102 = (f32[4,416,128]{2,1,0:T(8,128)S(1)}, f32[4,416,128]{2,1,0:T(8,128)S(1)}, f32[32,16,128]{2,1,0:T(8,128)S(1)}) custom-call(f32[16,2,128,128]{3,2,1,0:T(8,128)S(1)} %shard_map.101.refs_0_, f32[4,416,128]{2,1,0:T(8,128)S(1)} %get-tuple-element.74.refs_1_, f32[4,416,128]{2,1,0:T(8,128)S(1)} %shard_map.99.refs_8_.refs_2_, ...), custom_call_target="tpu_custom_call" | custom-call | tf_op jit(solution)/shard_map/pallas_call | solution.py:697
  61.3 3.6 %collective-permute-start.14 = (f32[4,416,128]{2,1,0:T(8,128)S(1)}, f32[4,416,128]{2,1,0:T(8,128)S(1)}, u32[]{:S(2)}, u32[]{:S(2)}) collective-permute-start(f32[4,416,128]{2,1,0:T(8,128)S(1)} %get-tuple-element.79), channel_id=1, source_target_pairs={{0,32},{32,0},{64,96},{96,64},{128,160},{160,128},{192,224},{224,1... | collective-permute-start | bytes 2555912 | tf_op jit(solution)/shard_map/ppermute | solution.py:868
  65.0 2.0 %collective-permute-done.14.refs_1_.refs_5_ = f32[4,416,128]{2,1,0:T(8,128)S(1)} collective-permute-done((f32[4,416,128]{2,1,0:T(8,128)S(1)}, f32[4,416,128]{2,1,0:T(8,128)S(1)}, u32[]{:S(2)}, u32[]{:S(2)}) %collective-permute-start.14) | collective-permute-done | bytes 852000 | tf_op jit(solution)/shard_map/ppermute | solution.py:868
  67.2 1.6 %collective-permute-start.15 = (f32[416,128]{1,0:T(8,128)S(1)}, f32[416,128]{1,0:T(8,128)S(1)}, u32[]{:S(2)}, u32[]{:S(2)}) collective-permute-start(f32[416,128]{1,0:T(8,128)S(1)} %get-tuple-element.81), channel_id=1, source_target_pairs={{0,64},{32,96},{64,128},{96,160},{128,192},{160,224},{192,0},{224,... | collective-permute-start | bytes 638984 | tf_op jit(solution)/shard_map/ppermute | solution.py:865
  68.8 1.4 %collective-permute-start.16 = (f32[416,128]{1,0:T(8,128)S(1)}, f32[416,128]{1,0:T(8,128)S(1)}, u32[]{:S(2)}, u32[]{:S(2)}) collective-permute-start(f32[416,128]{1,0:T(8,128)S(1)} %get-tuple-element.82), channel_id=1, source_target_pairs={{0,128},{32,160},{64,192},{96,224},{128,0},{160,32},{192,64},{224,... | collective-permute-start | bytes 638984 | tf_op jit(solution)/shard_map/ppermute | solution.py:865
  70.2 2.0 %collective-permute-start.17 = (f32[416,128]{1,0:T(8,128)S(1)}, f32[416,128]{1,0:T(8,128)S(1)}, u32[]{:S(2)}, u32[]{:S(2)}) collective-permute-start(f32[416,128]{1,0:T(8,128)S(1)} %get-tuple-element.83), channel_id=1, source_target_pairs={{0,192},{32,224},{64,0},{96,32},{128,64},{160,96},{192,128},{224,1... | collective-permute-start | bytes 638984 | tf_op jit(solution)/shard_map/ppermute | solution.py:865
  72.2 6.9 %shard_map.104 = (f32[8,2,128,128]{3,2,1,0:T(8,128)S(1)}, f32[8,384,128]{2,1,0:T(8,128)S(1)}) custom-call(f32[16,2,128,128]{3,2,1,0:T(8,128)S(1)} %get-tuple-element.66.refs_0_, f32[2,2,128,128]{3,2,1,0:T(8,128)S(1)} %get-tuple-element.67.refs_1_, f32[16,2,128,128]{3,2,1,0:T(8,128)S(1)} %get-tuple-element.59.refs_2_.refs_0_.refs_1_, ...), custom_call_target="tpu_custom_call" | custom-call | tf_op jit(solution)/shard_map/pallas_call | solution.py:697
  80.2 1.9 %collective-permute-start.18 = (f32[384,128]{1,0:T(8,128)S(1)}, f32[384,128]{1,0:T(8,128)S(1)}, u32[]{:S(2)}, u32[]{:S(2)}) collective-permute-start(f32[384,128]{1,0:T(8,128)S(1)} %get-tuple-element.90), channel_id=1, source_target_pairs={{0,64},{32,96},{64,128},{96,160},{128,192},{160,224},{192,0},{224,... | collective-permute-start | bytes 589832 | tf_op jit(solution)/shard_map/ppermute | solution.py:865
  82.1 2.7 %collective-permute-start.19 = (f32[384,128]{1,0:T(8,128)S(1)}, f32[384,128]{1,0:T(8,128)S(1)}, u32[]{:S(2)}, u32[]{:S(2)}) collective-permute-start(f32[384,128]{1,0:T(8,128)S(1)} %get-tuple-element.91), channel_id=1, source_target_pairs={{0,128},{32,160},{64,192},{96,224},{128,0},{160,32},{192,64},{224,... | collective-permute-start | bytes 589832 | tf_op jit(solution)/shard_map/ppermute | solution.py:865
  85.0 6.9 %shard_map.106.refs_6_.refs_4_ = f32[8,2,128,128]{3,2,1,0:T(8,128)S(1)} custom-call(f32[16,2,128,128]{3,2,1,0:T(8,128)S(1)} %get-tuple-element.66.refs_0_, f32[2,2,128,128]{3,2,1,0:T(8,128)S(1)} %get-tuple-element.67.refs_1_, f32[16,2,128,128]{3,2,1,0:T(8,128)S(1)} %get-tuple-element.59.refs_2_.refs_0_.refs_1_, ...), custom_call_target="tpu_custom_call" | custom-call | tf_op jit(solution)/shard_map/pallas_call | solution.py:697
  91.9 1.6 %collective-permute-done.19.refs_2_ = f32[384,128]{1,0:T(8,128)S(1)} collective-permute-done((f32[384,128]{1,0:T(8,128)S(1)}, f32[384,128]{1,0:T(8,128)S(1)}, u32[]{:S(2)}, u32[]{:S(2)}) %collective-permute-start.19) | collective-permute-done | bytes 196640 | tf_op jit(solution)/shard_map/ppermute | solution.py:865
  93.9 1.4 %collective-permute-start.21 = (f32[4,384,128]{2,1,0:T(8,128)S(1)}, f32[4,384,128]{2,1,0:T(8,128)S(1)}, u32[]{:S(2)}, u32[]{:S(2)}) collective-permute-start(f32[4,384,128]{2,1,0:T(8,128)S(1)} %get-tuple-element.95.refs_2_), channel_id=1, source_target_pairs={{0,32},{32,0},{64,96},{96,64},{128,160},{160,128},{192,224},{224,1... | collective-permute-start | bytes 2359304 | tf_op jit(solution)/shard_map/ppermute | solution.py:906
  95.3 1.6 %shard_map.108.refs_0_ = f32[16,2,64,128]{3,2,1,0:T(8,128)S(1)} custom-call(f32[4,384,128]{2,1,0:T(8,128)S(1)} %get-tuple-element.93.refs_0_, f32[128,16,128]{2,1,0:T(8,128)S(1)} %get-tuple-element.94.refs_1_.refs_2_, f32[4,384,128]{2,1,0:T(8,128)S(1)} %get-tuple-element.95.refs_2_), custom_call_target="tpu_custom_call" | custom-call | tf_op jit(solution)/shard_map/pallas_call | solution.py:697
  97.3 4.0 %shard_map.109 = bf16[16,96,128]{2,1,0:T(8,128)(2,1)} custom-call(f32[16,2,64,128]{3,2,1,0:T(8,128)S(1)} %shard_map.108.refs_0_, f32[4,384,128]{2,1,0:T(8,128)S(1)} %collective-permute-done.21.refs_1_, f32[128,16,128]{2,1,0:T(8,128)S(1)} %get-tuple-element.94.refs_1_.refs_2_, f32[8,2,128,128]{3,2,1,0:T(8,128)S(1)} %get-tuple-element.96.refs_3_, ...), custom_call_target="tpu_custom_call" | custom-call | tf_op jit(solution)/shard_map/pallas_call | solution.py:697
  (52 shorter events, 7.2 us)
Async XLA Ops:
  0.0 7.0 %copy-start = (bf16[16,96,128]{2,1,0:T(8,128)(2,1)S(1)}, bf16[16,96,128]{2,1,0:T(8,128)(2,1)}, u32[]{:S(2)}) copy-start(bf16[16,96,128]{2,1,0:T(8,128)(2,1)} %refs_0_.3) | copy-start | bytes 1179652
  0.0 7.0 %copy-start.4 = (f32[3]{0:T(128)S(1)}, f32[3]{0:T(128)}, u32[]{:S(2)}) copy-start(f32[3]{0:T(128)} %refs_2_.3) | copy-start | bytes 40
  0.0 7.0 %copy-start.8 = (f32[3]{0:T(128)S(1)}, f32[3]{0:T(128)}, u32[]{:S(2)}) copy-start(f32[3]{0:T(128)} %refs_4_.1) | copy-start | bytes 40
  0.0 7.0 %copy-start.6 = (f32[224]{0:T(256)S(1)}, f32[224]{0:T(256)}, u32[]{:S(2)}) copy-start(f32[224]{0:T(256)} %param.12) | copy-start | bytes 2692
  0.0 7.0 %copy-start.3 = (f32[3,3,224]{2,1,0:T(4,128)S(1)}, f32[3,3,224]{2,1,0:T(4,128)}, u32[]{:S(2)}) copy-start(f32[3,3,224]{2,1,0:T(4,128)} %refs_2_.2) | copy-start | bytes 24196
  0.0 7.0 %copy-start.1 = (bf16[96,419]{1,0:T(8,128)(2,1)S(1)}, bf16[96,419]{1,0:T(8,128)(2,1)}, u32[]{:S(2)}) copy-start(bf16[96,419]{1,0:T(8,128)(2,1)} %refs_1_.1) | copy-start | bytes 241348
  1.6 8.6 %collective-permute-start = (bf16[16,96]{1,0:T(8,128)(2,1)S(1)}, bf16[16,96]{1,0:T(8,128)(2,1)S(1)}, u32[]{:S(2)}, u32[]{:S(2)}) collective-permute-start(bf16[16,96]{1,0:T(8,128)(2,1)S(1)} %bitcast.4), channel_id=1, source_target_pairs={{0,1},{1,2},{2,3},{3,4},{4,5},{5,6},{6,7},{7,8},{8,9},{9,10},{10,1... | collective-permute-start | bytes 9224 | tf_op jit(solution)/shard_map/ppermute | solution.py:727
  5.7 4.4 %collective-permute-start.1 = (bf16[16,96]{1,0:T(8,128)(2,1)S(1)}, bf16[16,96]{1,0:T(8,128)(2,1)S(1)}, u32[]{:S(2)}, u32[]{:S(2)}) collective-permute-start(bf16[16,96]{1,0:T(8,128)(2,1)S(1)} %bitcast.6), channel_id=1, source_target_pairs={{1,0},{2,1},{3,2},{4,3},{5,4},{6,5},{7,6},{8,7},{9,8},{10,9},{11,1... | collective-permute-start | bytes 9224 | tf_op jit(solution)/shard_map/ppermute | solution.py:728
  10.2 11.4 %collective-permute-start.3 = (bf16[112,128]{1,0:T(8,128)(2,1)S(1)}, bf16[112,128]{1,0:T(8,128)(2,1)S(1)}, u32[]{:S(2)}, u32[]{:S(2)}) collective-permute-start(bf16[112,128]{1,0:T(8,128)(2,1)S(1)} %get-tuple-element.57.refs_9_), channel_id=1, source_target_pairs={{32,0},{64,32},{96,64},{128,96},{160,128},{192,160},{224,192},{33,... | collective-permute-start | bytes 86024 | tf_op jit(solution)/shard_map/ppermute | solution.py:750
  14.1 7.5 %collective-permute-start.2 = (bf16[112,128]{1,0:T(8,128)(2,1)S(1)}, bf16[112,128]{1,0:T(8,128)(2,1)S(1)}, u32[]{:S(2)}, u32[]{:S(2)}) collective-permute-start(bf16[112,128]{1,0:T(8,128)(2,1)S(1)} %get-tuple-element.58.refs_10_), channel_id=1, source_target_pairs={{0,32},{32,64},{64,96},{96,128},{128,160},{160,192},{192,224},{1,3... | collective-permute-start | bytes 86024 | tf_op jit(solution)/shard_map/ppermute | solution.py:749
  22.4 9.7 %collective-permute-start.4 = (f32[8,16,128]{2,1,0:T(8,128)S(1)}, f32[8,16,128]{2,1,0:T(8,128)S(1)}, u32[]{:S(2)}, u32[]{:S(2)}) collective-permute-start(f32[8,16,128]{2,1,0:T(8,128)S(1)} %get-tuple-element.63), channel_id=1, source_target_pairs={{0,1},{1,2},{2,3},{3,0},{4,5},{5,6},{6,7},{7,4},{8,9},{9,10},{10,1... | collective-permute-start | bytes 196616 | tf_op jit(solution)/shard_map/ppermute | solution.py:805
  23.8 8.4 %collective-permute-start.5 = (f32[8,16,128]{2,1,0:T(8,128)S(1)}, f32[8,16,128]{2,1,0:T(8,128)S(1)}, u32[]{:S(2)}, u32[]{:S(2)}) collective-permute-start(f32[8,16,128]{2,1,0:T(8,128)S(1)} %get-tuple-element.64), channel_id=1, source_target_pairs={{0,2},{1,3},{2,0},{3,1},{4,6},{5,7},{6,4},{7,5},{8,10},{9,11},{10,... | collective-permute-start | bytes 196616 | tf_op jit(solution)/shard_map/ppermute | solution.py:805
  28.6 3.8 %collective-permute-start.6 = (f32[8,16,128]{2,1,0:T(8,128)S(1)}, f32[8,16,128]{2,1,0:T(8,128)S(1)}, u32[]{:S(2)}, u32[]{:S(2)}) collective-permute-start(f32[8,16,128]{2,1,0:T(8,128)S(1)} %get-tuple-element.65), channel_id=1, source_target_pairs={{0,3},{1,0},{2,1},{3,2},{4,7},{5,4},{6,5},{7,6},{8,11},{9,8},{10,9... | collective-permute-start | bytes 196616 | tf_op jit(solution)/shard_map/ppermute | solution.py:805
  32.4 3.4 %collective-permute-start.7 = (f32[8,16,128]{2,1,0:T(8,128)S(1)}, f32[8,16,128]{2,1,0:T(8,128)S(1)}, u32[]{:S(2)}, u32[]{:S(2)}) collective-permute-start(f32[8,16,128]{2,1,0:T(8,128)S(1)} %shard_map.96.refs_2_.refs_0_), channel_id=1, source_target_pairs={{0,4},{1,5},{2,6},{3,7},{4,0},{5,1},{6,2},{7,3},{8,12},{9,13},{10,... | collective-permute-start | bytes 196616 | tf_op jit(solution)/shard_map/ppermute | solution.py:822
  35.8 15.9 %collective-permute-start.10 = (f32[8,16,128]{2,1,0:T(8,128)S(1)}, f32[8,16,128]{2,1,0:T(8,128)S(1)}, u32[]{:S(2)}, u32[]{:S(2)}) collective-permute-start(f32[8,16,128]{2,1,0:T(8,128)S(1)} %shard_map.98.refs_6_), channel_id=1, source_target_pairs={{0,24},{1,25},{2,26},{3,27},{4,28},{5,29},{6,30},{7,31},{32,56},{3... | collective-permute-start | bytes 196616 | tf_op jit(solution)/shard_map/ppermute | solution.py:837
  43.0 8.8 %collective-permute-start.9 = (f32[8,16,128]{2,1,0:T(8,128)S(1)}, f32[8,16,128]{2,1,0:T(8,128)S(1)}, u32[]{:S(2)}, u32[]{:S(2)}) collective-permute-start(f32[8,16,128]{2,1,0:T(8,128)S(1)} %shard_map.98.refs_6_), channel_id=1, source_target_pairs={{0,16},{1,17},{2,18},{3,19},{4,20},{5,21},{6,22},{7,23},{8,24},{9,... | collective-permute-start | bytes 196616 | tf_op jit(solution)/shard_map/ppermute | solution.py:837
  46.0 5.8 %collective-permute-start.8 = (f32[8,16,128]{2,1,0:T(8,128)S(1)}, f32[8,16,128]{2,1,0:T(8,128)S(1)}, u32[]{:S(2)}, u32[]{:S(2)}) collective-permute-start(f32[8,16,128]{2,1,0:T(8,128)S(1)} %shard_map.98.refs_6_), channel_id=1, source_target_pairs={{0,8},{1,9},{2,10},{3,11},{4,12},{5,13},{6,14},{7,15},{8,16},{9,17... | collective-permute-start | bytes 196616 | tf_op jit(solution)/shard_map/ppermute | solution.py:837
  51.9 5.6 %collective-permute-start.11 = (f32[8,16,128]{2,1,0:T(8,128)S(1)}, f32[8,16,128]{2,1,0:T(8,128)S(1)}, u32[]{:S(2)}, u32[]{:S(2)}) collective-permute-start(f32[8,16,128]{2,1,0:T(8,128)S(1)} %get-tuple-element.75), channel_id=1, source_target_pairs={{0,1},{1,2},{2,3},{3,0},{4,5},{5,6},{6,7},{7,4},{8,9},{9,10},{10,1... | collective-permute-start | bytes 196616 | tf_op jit(solution)/shard_map/ppermute | solution.py:805
  53.3 4.8 %collective-permute-start.12 = (f32[8,16,128]{2,1,0:T(8,128)S(1)}, f32[8,16,128]{2,1,0:T(8,128)S(1)}, u32[]{:S(2)}, u32[]{:S(2)}) collective-permute-start(f32[8,16,128]{2,1,0:T(8,128)S(1)} %get-tuple-element.76), channel_id=1, source_target_pairs={{0,2},{1,3},{2,0},{3,1},{4,6},{5,7},{6,4},{7,5},{8,10},{9,11},{10,... | collective-permute-start | bytes 196616 | tf_op jit(solution)/shard_map/ppermute | solution.py:805
  55.7 3.4 %collective-permute-start.13 = (f32[8,16,128]{2,1,0:T(8,128)S(1)}, f32[8,16,128]{2,1,0:T(8,128)S(1)}, u32[]{:S(2)}, u32[]{:S(2)}) collective-permute-start(f32[8,16,128]{2,1,0:T(8,128)S(1)} %get-tuple-element.77), channel_id=1, source_target_pairs={{0,3},{1,0},{2,1},{3,2},{4,7},{5,4},{6,5},{7,6},{8,11},{9,8},{10,9... | collective-permute-start | bytes 196616 | tf_op jit(solution)/shard_map/ppermute | solution.py:805
  59.2 13.0 %copy-start.5 = (f32[3]{0:T(128)S(1)}, f32[3]{0:T(128)}, u32[]{:S(2)}) copy-start(f32[3]{0:T(128)} %refs_9_.3) | copy-start | bytes 40
  61.3 5.6 %collective-permute-start.14 = (f32[4,416,128]{2,1,0:T(8,128)S(1)}, f32[4,416,128]{2,1,0:T(8,128)S(1)}, u32[]{:S(2)}, u32[]{:S(2)}) collective-permute-start(f32[4,416,128]{2,1,0:T(8,128)S(1)} %get-tuple-element.79), channel_id=1, source_target_pairs={{0,32},{32,0},{64,96},{96,64},{128,160},{160,128},{192,224},{224,1... | collective-permute-start | bytes 2555912 | tf_op jit(solution)/shard_map/ppermute | solution.py:868
  67.2 11.8 %collective-permute-start.15 = (f32[416,128]{1,0:T(8,128)S(1)}, f32[416,128]{1,0:T(8,128)S(1)}, u32[]{:S(2)}, u32[]{:S(2)}) collective-permute-start(f32[416,128]{1,0:T(8,128)S(1)} %get-tuple-element.81), channel_id=1, source_target_pairs={{0,64},{32,96},{64,128},{96,160},{128,192},{160,224},{192,0},{224,... | collective-permute-start | bytes 638984 | tf_op jit(solution)/shard_map/ppermute | solution.py:865
  68.8 11.0 %collective-permute-start.16 = (f32[416,128]{1,0:T(8,128)S(1)}, f32[416,128]{1,0:T(8,128)S(1)}, u32[]{:S(2)}, u32[]{:S(2)}) collective-permute-start(f32[416,128]{1,0:T(8,128)S(1)} %get-tuple-element.82), channel_id=1, source_target_pairs={{0,128},{32,160},{64,192},{96,224},{128,0},{160,32},{192,64},{224,... | collective-permute-start | bytes 638984 | tf_op jit(solution)/shard_map/ppermute | solution.py:865
  70.2 9.8 %collective-permute-start.17 = (f32[416,128]{1,0:T(8,128)S(1)}, f32[416,128]{1,0:T(8,128)S(1)}, u32[]{:S(2)}, u32[]{:S(2)}) collective-permute-start(f32[416,128]{1,0:T(8,128)S(1)} %get-tuple-element.83), channel_id=1, source_target_pairs={{0,192},{32,224},{64,0},{96,32},{128,64},{160,96},{192,128},{224,1... | collective-permute-start | bytes 638984 | tf_op jit(solution)/shard_map/ppermute | solution.py:865
  80.2 11.7 %collective-permute-start.18 = (f32[384,128]{1,0:T(8,128)S(1)}, f32[384,128]{1,0:T(8,128)S(1)}, u32[]{:S(2)}, u32[]{:S(2)}) collective-permute-start(f32[384,128]{1,0:T(8,128)S(1)} %get-tuple-element.90), channel_id=1, source_target_pairs={{0,64},{32,96},{64,128},{96,160},{128,192},{160,224},{192,0},{224,... | collective-permute-start | bytes 589832 | tf_op jit(solution)/shard_map/ppermute | solution.py:865
  82.1 11.4 %collective-permute-start.19 = (f32[384,128]{1,0:T(8,128)S(1)}, f32[384,128]{1,0:T(8,128)S(1)}, u32[]{:S(2)}, u32[]{:S(2)}) collective-permute-start(f32[384,128]{1,0:T(8,128)S(1)} %get-tuple-element.91), channel_id=1, source_target_pairs={{0,128},{32,160},{64,192},{96,224},{128,0},{160,32},{192,64},{224,... | collective-permute-start | bytes 589832 | tf_op jit(solution)/shard_map/ppermute | solution.py:865
  84.9 8.7 %collective-permute-start.20 = (f32[384,128]{1,0:T(8,128)S(1)}, f32[384,128]{1,0:T(8,128)S(1)}, u32[]{:S(2)}, u32[]{:S(2)}) collective-permute-start(f32[384,128]{1,0:T(8,128)S(1)} %get-tuple-element.92), channel_id=1, source_target_pairs={{0,192},{32,224},{64,0},{96,32},{128,64},{160,96},{192,128},{224,1... | collective-permute-start | bytes 589832 | tf_op jit(solution)/shard_map/ppermute | solution.py:865
  93.9 3.4 %copy-start.2 = (bf16[192,96]{1,0:T(8,128)(2,1)S(1)}, bf16[192,96]{1,0:T(8,128)(2,1)}, u32[]{:S(2)}) copy-start(bf16[192,96]{1,0:T(8,128)(2,1)} %refs_7_.1) | copy-start | bytes 110596
  93.9 3.4 %copy-start.7 = (f32[192]{0:T(256)S(1)}, f32[192]{0:T(256)}, u32[]{:S(2)}) copy-start(f32[192]{0:T(256)} %param.16) | copy-start | bytes 2308
  93.9 3.3 %collective-permute-start.21 = (f32[4,384,128]{2,1,0:T(8,128)S(1)}, f32[4,384,128]{2,1,0:T(8,128)S(1)}, u32[]{:S(2)}, u32[]{:S(2)}) collective-permute-start(f32[4,384,128]{2,1,0:T(8,128)S(1)} %get-tuple-element.95.refs_2_), channel_id=1, source_target_pairs={{0,32},{32,0},{64,96},{96,64},{128,160},{160,128},{192,224},{224,1... | collective-permute-start | bytes 2359304 | tf_op jit(solution)/shard_map/ppermute | solution.py:906

commit v5 on v4

--- a/solution.py
+++ b/solution.py
@@ -79,7 +79,6 @@
     step_bias,
     decay_log,
     inner,
-    gate,
     steps,
     compact,
     totals,
@@ -101,8 +100,6 @@
         step_w[1],
         step_w[2],
         step_w[2],
-        source[:, 0:192],
-        jnp.zeros((WIDTH, HALF), f32),
     ]
     weight[...] = jnp.concatenate(wide, axis=1).astype(bf16)
     conv_w[...] = weight[:, 0:256]
@@ -114,11 +111,10 @@
         compact[r] = dot(step_turned, tok[r], ((1,), (0,))).astype(bf16).astype(f32)
         for g in range(2):
             inner[r, g] = out[:, g * 128 : g * 128 + 128]
-            gate[r, g] = out[:, 512 + g * 128 : 640 + g * 128]
             raw = out[:, 256 + g * 128 : 384 + g * 128].astype(f32) + by_head(step_bias, g)
             steps[r, g] = softplus(raw)
 
-    each_row(own_row, 4)
+    each_row(own_row, 8)
 
     head = lax.broadcasted_iota(jnp.int32, (8, LANES), 0)
 
@@ -179,7 +175,8 @@
     return parts
 
 
-def finish_row(parts, steps, compact, totals, xdt, act, bct, ends):
+def finish_row(parts, steps, compact, totals, xdt, act, bct, maps, ends):
+    maps[...] = parts[1].astype(bf16)
     turned = parts[1].T
     chan_b = turned[96:112, :]
     bct[0:16, :] = chan_b
@@ -200,7 +197,6 @@
     rest = jnp.concatenate([total, totals[2:3, :], jnp.zeros((2, LANES), f32)], axis=0)
     ends[0] = jnp.concatenate([first[0:8, :], third[0:4, :], rest], axis=0)
     ends[1] = jnp.concatenate([first[8:16, :], third[4:8, :], rest], axis=0)
-    return other
 
 
 def inside_kernel(
@@ -217,7 +213,7 @@
     decay,
     act,
     bct,
-    cmap,
+    maps,
     ends,
     proj,
 ):
@@ -232,14 +228,14 @@
     each_row(own_row, 4)
 
     def some(k, carry):
-        for i in range(2):
-            r = 1 + 2 * k + i
+        for i in range(7):
+            r = 1 + 7 * k + i
             parts = conv_row(proj, taps, r - 1)
-            refs = [ref.at[r] for ref in (steps, compact, totals, xdt, act, bct)]
-            cmap[:, r, :] = finish_row(parts, *refs, ends.at[pl.ds(2 * r, 2)])
+            refs = [ref.at[r] for ref in (steps, compact, totals, xdt, act, bct, maps)]
+            finish_row(parts, *refs, ends.at[pl.ds(2 * r, 2)])
         return carry
 
-    lax.fori_loop(0, ROWS // 2 - 1, some, 0)
+    lax.fori_loop(0, 2, some, 0)
 
 
 def edge_kernel(
@@ -253,12 +249,11 @@
     totals,
     conv_w,
     taps,
-    cmap_in,
     ends,
     xdt,
     act,
     bct,
-    cmap,
+    maps,
     *refs,
 ):
     ends_out, (proj, held) = refs[:CHIPS], refs[CHIPS:]
@@ -275,15 +270,19 @@
         for g in range(2):
             proj[at, g, 8:136, :] = inner[r, g].astype(f32)
     held[...] = ends[...]
-    cmap[...] = cmap_in[...]
     for e, r in enumerate((0, ROWS - 1)):
         parts = conv_row(proj, taps, 3 * e)
         own = [ref.at[r] for ref in (steps, compact, totals)]
-        mine = [ref.at[e] for ref in (xdt, act, bct)]
-        cmap[:, r, :] = finish_row(parts, *own, *mine, held.at[pl.ds(2 * r, 2)])
+        mine = [ref.at[e] for ref in (xdt, act, bct, maps)]
+        finish_row(parts, *own, *mine, held.at[pl.ds(2 * r, 2)])
     member, _ = line()
     for k, out in enumerate(ends_out):
         out[...] = held[pl.ds((member + k) % CHIPS * 8, 8)]
+
+
+def cells_kernel(maps_in, maps_edge, cmap):
+    for r in range(ROWS):
+        cmap[:, r, :] = pltpu.roll(row_of((maps_in, maps_edge), r)[...].astype(f32), HALF, 1)
 
 
 def row_of(pair, r):
@@ -473,21 +472,24 @@
         both((theirs, mine))
 
 
-def gating_kernel(decay, gate, gating, reach):
-    along = [jnp.ones((COLS, LANES), f32)] * 2
+def gating_kernel(decay, tok, in_weight, gating, reach, weight):
+    source = in_weight[...].astype(f32)
+    wide = [source[:, 0:INNER], jnp.zeros((WIDTH, HALF), f32)]
+    weight[...] = jnp.concatenate(wide, axis=1).astype(bf16)
 
     def some(k, along):
         along = list(along)
         for i in range(4):
             r = k * 4 + i
+            gate = dot(tok[r], weight[...], ((0,), (0,))).astype(bf16).astype(f32)
             for g in range(2):
                 along[g] = along[g] * decay[r, g]
-                gated = silu(gate[r, g].astype(f32))
+                gated = silu(gate[:, g * 128 : g * 128 + 128])
                 gating[r, g] = gated
                 reach[r, g] = along[g] * gated
         return tuple(along)
 
-    lax.fori_loop(0, ROWS // 4, some, tuple(along))
+    lax.fori_loop(0, ROWS // 4, some, (jnp.ones((COLS, LANES), f32),) * 2)
 
 
 def local_kernel(
@@ -723,17 +725,17 @@
 ):
     to_right, to_left = steps("gx")
     to_down, to_up = steps("gy")
+    vmem = pltpu.VMEM
     last, first = tokens[:, :, COLS - 1], tokens[:, :, 0]
     left = lax.ppermute(last, "gx", to_right)
     right = lax.ppermute(first, "gx", to_left)
-    vmem = pltpu.VMEM
     rows8 = ((ROWS, 8, LANES), f32, "v")
-    inner, gate, step, compact, totals, conv_w, taps = call(
+    inner, step, compact, totals, conv_w, taps = call(
         project_kernel,
         "vvvvss",
-        [(PLANE, bf16, "v"), (PLANE, bf16, "v"), (PLANE, f32, "v"), rows8, rows8]
+        [(PLANE, bf16, "v"), (PLANE, f32, "v"), rows8, rows8]
         + [((WIDTH, 256), bf16, "v"), ((2, 16, LANES), f32, "v")],
-        [vmem((WIDTH, 768), bf16)],
+        [vmem((WIDTH, 512), bf16)],
         tokens,
         in_weight,
         conv_weight,
@@ -752,7 +754,7 @@
     quarters = vmem((CHIPS,) + packet[0], f32)
     all_ends = ((2 * ROWS, 16, LANES), f32, "v")
     cells = ((COLS, ROWS, LANES), f32, "v")
-    xdt, decay, act, bct, cmap, ends = call(
+    xdt, decay, act, bct, maps, ends = call(
         inside_kernel,
         "v" * 8 + "s",
         [
@@ -760,7 +762,7 @@
             (PLANE, f32, "v"),
             (PLANE, bf16, "v"),
             ((ROWS, 32, COLS), f32, "v"),
-            cells,
+            ((ROWS, COLS, LANES), bf16, "v"),
             all_ends,
         ],
         [vmem((ROWS, 2, 144, LANES), f32)],
@@ -776,10 +778,11 @@
         after=(up_row, down_row),
     )
     two = (2,) + PLANE[1:]
-    xdt_edge, act_edge, bct_edge, cmap, *ends = call(
+    xdt_edge, act_edge, bct_edge, maps_edge, *ends = call(
         edge_kernel,
-        "v" * 12,
-        [(two, f32, "v"), (two, bf16, "v"), ((2, 32, COLS), f32, "v"), cells]
+        "v" * 11,
+        [(two, f32, "v"), (two, bf16, "v"), ((2, 32, COLS), f32, "v")]
+        + [((2, COLS, LANES), bf16, "v")]
         + [packet] * CHIPS,
         [vmem((6, 2, 144, LANES), f32), vmem(all_ends[0], f32)],
         inner,
@@ -792,7 +795,6 @@
         totals,
         conv_w,
         taps,
-        cmap,
         ends,
     )
     scanned = (xdt, xdt_edge, decay, bct, bct_edge)
@@ -821,7 +823,14 @@
     (whole,) = call(members_kernel, "vvvv", [packet], [quarters], *ends, after=(middle,))
     beside = lax.ppermute(whole, "gx", [(i, i ^ 4) for i in range(gx_count)])
     gating, reach = call(
-        gating_kernel, "vv", [(PLANE, f32, "v")] * 2, [], decay, gate, after=(whole,)
+        gating_kernel,
+        "vvv",
+        [(PLANE, f32, "v")] * 2,
+        [vmem((WIDTH, 256), bf16)],
+        decay,
+        tokens,
+        in_weight,
+        after=(whole,),
     )
     (both,) = call(pair_kernel, "vv", [packet], [], whole, beside, after=(reach,))
     (right_half,) = call(
@@ -879,13 +888,14 @@
         *inner,
         after=joined[:1],
     )
+    (cmap,) = call(cells_kernel, "vv", [cells], [], maps, maps_edge, after=joined[:1])
     pieces = call(
         col_prefix_kernel,
         "vvvv",
         [piece_out] * CHIPS,
         [vmem((CHIPS,) + PIECE, f32), vmem((CHIPS,) + PIECE_OUT, f32)],
         *pieces,
-        after=(track,),
+        after=(track, cmap),
     )
     above_chip = pieces[0]
     pieces = rotate(pieces)

time: 102 us -> 99.8 us (0.978)
  waiting for transfers between devices: 7.79 us -> 6.19 us
    pallas_call x19 -> x20, Pallas kernels: 40 us -> 39.8 us  [call(): pl.pallas_call(inner, in_specs=[pl.BlockSpec(memory_space=kinds[k]) for k...]
where the time goes in v5:
time: 99.8 us; the launch traced here: 99.6 us
  starting transfers between devices  51.4 us (52%)
  Pallas kernels  39.8 us (40%)
  waiting for transfers between devices  6.19 us (6%)
  local copies, waits for them, and re-layouts  1.77 us (2%)
    pallas_call x20, Pallas kernels, call(): pl.pallas_call(inner, in_specs=[pl.BlockSpec(memory_space=kinds[k]) for k...  39.8 us
    ppermute x3, starting transfers between devices, on_device(): lax.ppermute(both, 'gx', [(i, i + 8 * k) for i in range(gx_count - 8 * k)])  12.1 us
    ppermute x6, starting transfers between devices, members(): moved[k] = lax.ppermute(pieces[k], 'gx', pairs)  10.4 us
    ppermute x6, starting transfers between devices, rotate(): moved[k] = lax.ppermute(pieces[k], 'gy', ahead[k])  9.62 us
    ppermute x1, starting transfers between devices, on_device(): below = lax.ppermute(up_row, 'gy', to_up)  4.01 us
    ppermute x1, starting transfers between devices, on_device(): left = lax.ppermute(last, 'gx', to_right)  3.94 us
    ppermute x1, starting transfers between devices, on_device(): theirs = lax.ppermute(theirs, 'gy', swap)  3.79 us
    ppermute x1, starting transfers between devices, on_device(): above = lax.ppermute(down_row, 'gy', to_down)  3.1 us
  transfers between devices with their start and end apart: 22, of which 10 were waited for; matrix products, arithmetic and copies ran while one was open for 0% of the time, Pallas kernels for 32%

profile of v5, /device:TPU:1, one launch (start us, length us, event | category | flops | bytes accessed | tf_op | source)
XLA Modules:
  0.0 99.6 jit_solution(2968420594901967273)
XLA Ops:
  0.0 1.3 %fusion = (bf16[16,96,1]{2,1,0:T(8,128)(2,1)S(1)}, bf16[16,96,1]{2,1,0:T(8,128)(2,1)S(1)}) fusion(bf16[16,96,128]{2,1,0:T(8,128)(2,1)} %refs_1_.3), kind=kLoop, calls=%fused_computation | loop fusion | bytes 12288 | tf_op jit(solution)/shard_map/slice | solution.py:729
  1.6 3.9 %collective-permute-start = (bf16[16,96]{1,0:T(8,128)(2,1)S(1)}, bf16[16,96]{1,0:T(8,128)(2,1)S(1)}, u32[]{:S(2)}, u32[]{:S(2)}) collective-permute-start(bf16[16,96]{1,0:T(8,128)(2,1)S(1)} %bitcast.4), channel_id=1, source_target_pairs={{0,1},{1,2},{2,3},{3,4},{4,5},{5,6},{6,7},{7,8},{8,9},{9,10},{10,1... | collective-permute-start | bytes 9224 | tf_op jit(solution)/shard_map/ppermute | solution.py:730
  7.1 2.7 %shard_map.91 = (bf16[16,2,128,128]{3,2,1,0:T(8,128)(2,1)S(1)}, f32[16,2,128,128]{3,2,1,0:T(8,128)S(1)}, f32[16,8,128]{2,1,0:T(8,128)S(1)}, f32[16,8,128]{2,1,0:...) custom-call(bf16[16,96,128]{2,1,0:T(8,128)(2,1)S(1)} %copy-done, bf16[96,419]{1,0:T(8,128)(2,1)S(1)} %copy-done.1, ...), custom_call_target="tpu_custom_call" | custom-call | tf_op jit(solution)/shard_map/pallas_call | solution.py:699
  10.1 4.0 %collective-permute-start.3 = (bf16[112,128]{1,0:T(8,128)(2,1)S(1)}, bf16[112,128]{1,0:T(8,128)(2,1)S(1)}, u32[]{:S(2)}, u32[]{:S(2)}) collective-permute-start(bf16[112,128]{1,0:T(8,128)(2,1)S(1)} %get-tuple-element.56.refs_9_), channel_id=1, source_target_pairs={{32,0},{64,32},{96,64},{128,96},{160,128},{192,160},{224,192},{33,... | collective-permute-start | bytes 86024 | tf_op jit(solution)/shard_map/ppermute | solution.py:752
  14.1 3.1 %collective-permute-start.2 = (bf16[112,128]{1,0:T(8,128)(2,1)S(1)}, bf16[112,128]{1,0:T(8,128)(2,1)S(1)}, u32[]{:S(2)}, u32[]{:S(2)}) collective-permute-start(bf16[112,128]{1,0:T(8,128)(2,1)S(1)} %get-tuple-element.57.refs_10_), channel_id=1, source_target_pairs={{0,32},{32,64},{64,96},{96,128},{128,160},{160,192},{192,224},{1,3... | collective-permute-start | bytes 86024 | tf_op jit(solution)/shard_map/ppermute | solution.py:751
  17.2 3.2 %shard_map.93 = (f32[16,2,128,128]{3,2,1,0:T(8,128)S(1)}, f32[16,2,128,128]{3,2,1,0:T(8,128)S(1)}, bf16[16,2,128,128]{3,2,1,0:T(8,128)(2,1)S(1)}, f32[16,32,128]...) custom-call(bf16[16,2,128,128]{3,2,1,0:T(8,128)(2,1)S(1)} %get-tuple-element.51.refs_0_, ...), custom_call_target="tpu_custom_call" | custom-call | tf_op jit(solution)/shard_map/pallas_call | solution.py:699
  21.1 1.3 %collective-permute-start.4 = (f32[8,16,128]{2,1,0:T(8,128)S(1)}, f32[8,16,128]{2,1,0:T(8,128)S(1)}, u32[]{:S(2)}, u32[]{:S(2)}) collective-permute-start(f32[8,16,128]{2,1,0:T(8,128)S(1)} %get-tuple-element.61), channel_id=1, source_target_pairs={{0,1},{1,2},{2,3},{3,0},{4,5},{5,6},{6,7},{7,4},{8,9},{9,10},{10,1... | collective-permute-start | bytes 196616 | tf_op jit(solution)/shard_map/ppermute | solution.py:807
  22.4 4.9 %collective-permute-start.5 = (f32[8,16,128]{2,1,0:T(8,128)S(1)}, f32[8,16,128]{2,1,0:T(8,128)S(1)}, u32[]{:S(2)}, u32[]{:S(2)}) collective-permute-start(f32[8,16,128]{2,1,0:T(8,128)S(1)} %get-tuple-element.62), channel_id=1, source_target_pairs={{0,2},{1,3},{2,0},{3,1},{4,6},{5,7},{6,4},{7,5},{8,10},{9,11},{10,... | collective-permute-start | bytes 196616 | tf_op jit(solution)/shard_map/ppermute | solution.py:807
  27.3 3.4 %shard_map.95 = (f32[4,416,128]{2,1,0:T(8,128)S(1)}, f32[48,8,128]{2,1,0:T(8,128)S(1)}) custom-call(f32[16,2,128,128]{3,2,1,0:T(8,128)S(1)} %get-tuple-element.64.refs_0_, f32[2,2,128,128]{3,2,1,0:T(8,128)S(1)} %get-tuple-element.65.refs_1_, f32[16,2,128,128]{3,2,1,0:T(8,128)S(1)} %get-tuple-element.58.refs_2_.refs_0_.refs_1_, ...), custom_call_target="tpu_custom_call" | custom-call | tf_op jit(solution)/shard_map/pallas_call | solution.py:699
  31.1 1.7 %collective-permute-start.7 = (f32[8,16,128]{2,1,0:T(8,128)S(1)}, f32[8,16,128]{2,1,0:T(8,128)S(1)}, u32[]{:S(2)}, u32[]{:S(2)}) collective-permute-start(f32[8,16,128]{2,1,0:T(8,128)S(1)} %shard_map.96.refs_3_.refs_0_), channel_id=1, source_target_pairs={{0,4},{1,5},{2,6},{3,7},{4,0},{5,1},{6,2},{7,3},{8,12},{9,13},{10,... | collective-permute-start | bytes 196616 | tf_op jit(solution)/shard_map/ppermute | solution.py:824
  32.9 1.5 %shard_map.97 = (f32[16,2,128,128]{3,2,1,0:T(8,128)S(1)}, f32[16,2,128,128]{3,2,1,0:T(8,128)S(1)}) custom-call(f32[16,2,128,128]{3,2,1,0:T(8,128)S(1)} %get-tuple-element.58.refs_2_.refs_0_.refs_1_, bf16[16,96,128]{2,1,0:T(8,128)(2,1)S(1)} %copy-done, bf16[96,419]{1,0:T(8,128)(2,1)S(1)} %copy-done.1, f32[8,16,128]{2,1,0:T(8,128)S(1)} %shard_map.96.refs_3_.refs_0_), custom_call_target="tpu_custom_call" | custom-call | tf_op jit(solution)/shard_map/pallas_call | solution.py:699
  34.6 6.9 %collective-permute-start.10 = (f32[8,16,128]{2,1,0:T(8,128)S(1)}, f32[8,16,128]{2,1,0:T(8,128)S(1)}, u32[]{:S(2)}, u32[]{:S(2)}) collective-permute-start(f32[8,16,128]{2,1,0:T(8,128)S(1)} %shard_map.98.refs_6_), channel_id=1, source_target_pairs={{0,24},{1,25},{2,26},{3,27},{4,28},{5,29},{6,30},{7,31},{32,56},{3... | collective-permute-start | bytes 196616 | tf_op jit(solution)/shard_map/ppermute | solution.py:846
  41.4 2.9 %collective-permute-start.9 = (f32[8,16,128]{2,1,0:T(8,128)S(1)}, f32[8,16,128]{2,1,0:T(8,128)S(1)}, u32[]{:S(2)}, u32[]{:S(2)}) collective-permute-start(f32[8,16,128]{2,1,0:T(8,128)S(1)} %shard_map.98.refs_6_), channel_id=1, source_target_pairs={{0,16},{1,17},{2,18},{3,19},{4,20},{5,21},{6,22},{7,23},{8,24},{9,... | collective-permute-start | bytes 196616 | tf_op jit(solution)/shard_map/ppermute | solution.py:846
  44.3 2.4 %collective-permute-start.8 = (f32[8,16,128]{2,1,0:T(8,128)S(1)}, f32[8,16,128]{2,1,0:T(8,128)S(1)}, u32[]{:S(2)}, u32[]{:S(2)}) collective-permute-start(f32[8,16,128]{2,1,0:T(8,128)S(1)} %shard_map.98.refs_6_), channel_id=1, source_target_pairs={{0,8},{1,9},{2,10},{3,11},{4,12},{5,13},{6,14},{7,15},{8,16},{9,17... | collective-permute-start | bytes 196616 | tf_op jit(solution)/shard_map/ppermute | solution.py:846
  46.7 3.4 %shard_map.99.refs_8_.refs_2_ = f32[4,416,128]{2,1,0:T(8,128)S(1)} custom-call(f32[16,2,128,128]{3,2,1,0:T(8,128)S(1)} %get-tuple-element.64.refs_0_, f32[2,2,128,128]{3,2,1,0:T(8,128)S(1)} %get-tuple-element.65.refs_1_, f32[16,2,128,128]{3,2,1,0:T(8,128)S(1)} %get-tuple-element.58.refs_2_.refs_0_.refs_1_, f32[16,32,128]{2,1,0:T(8,128)S(1)} %get-tuple-element.66.refs_3_, ...), custom_call_target="tpu_custom_call" | custom-call | tf_op jit(solution)/shard_map/pallas_call | solution.py:699
  50.3 1.7 %collective-permute-start.11 = (f32[8,16,128]{2,1,0:T(8,128)S(1)}, f32[8,16,128]{2,1,0:T(8,128)S(1)}, u32[]{:S(2)}, u32[]{:S(2)}) collective-permute-start(f32[8,16,128]{2,1,0:T(8,128)S(1)} %get-tuple-element.72), channel_id=1, source_target_pairs={{0,1},{1,2},{2,3},{3,0},{4,5},{5,6},{6,7},{7,4},{8,9},{9,10},{10,1... | collective-permute-start | bytes 196616 | tf_op jit(solution)/shard_map/ppermute | solution.py:807
  52.0 2.1 %collective-permute-start.12 = (f32[8,16,128]{2,1,0:T(8,128)S(1)}, f32[8,16,128]{2,1,0:T(8,128)S(1)}, u32[]{:S(2)}, u32[]{:S(2)}) collective-permute-start(f32[8,16,128]{2,1,0:T(8,128)S(1)} %get-tuple-element.73), channel_id=1, source_target_pairs={{0,2},{1,3},{2,0},{3,1},{4,6},{5,7},{6,4},{7,5},{8,10},{9,11},{10,... | collective-permute-start | bytes 196616 | tf_op jit(solution)/shard_map/ppermute | solution.py:807
  54.5 1.7 %shard_map.101.refs_0_ = f32[16,2,128,128]{3,2,1,0:T(8,128)S(1)} custom-call(f32[16,2,128,128]{3,2,1,0:T(8,128)S(1)} %get-tuple-element.50.refs_3_.refs_5_.refs_0_, f32[16,2,128,128]{3,2,1,0:T(8,128)S(1)} %get-tuple-element.58.refs_2_.refs_0_.refs_1_, f32[3]{0:T(128)S(1)} %copy-done.4, f32[8,16,128]{2,1,0:T(8,128)S(1)} %get-tuple-element.70.refs_3_), custom_call_target="tpu_custom_call" | custom-call | tf_op jit(solution)/shard_map/pallas_call | solution.py:699
  57.5 2.2 %shard_map.102 = (f32[4,416,128]{2,1,0:T(8,128)S(1)}, f32[4,416,128]{2,1,0:T(8,128)S(1)}, f32[32,16,128]{2,1,0:T(8,128)S(1)}) custom-call(f32[16,2,128,128]{3,2,1,0:T(8,128)S(1)} %shard_map.101.refs_0_, f32[4,416,128]{2,1,0:T(8,128)S(1)} %get-tuple-element.71.refs_1_, f32[4,416,128]{2,1,0:T(8,128)S(1)} %shard_map.99.refs_8_.refs_2_, ...), custom_call_target="tpu_custom_call" | custom-call | tf_op jit(solution)/shard_map/pallas_call | solution.py:699
  59.7 3.8 %collective-permute-start.14 = (f32[4,416,128]{2,1,0:T(8,128)S(1)}, f32[4,416,128]{2,1,0:T(8,128)S(1)}, u32[]{:S(2)}, u32[]{:S(2)}) collective-permute-start(f32[4,416,128]{2,1,0:T(8,128)S(1)} %get-tuple-element.76), channel_id=1, source_target_pairs={{0,32},{32,0},{64,96},{96,64},{128,160},{160,128},{192,224},{224,1... | collective-permute-start | bytes 2555912 | tf_op jit(solution)/shard_map/ppermute | solution.py:877
  63.5 2.0 %collective-permute-done.14.refs_1_.refs_5_ = f32[4,416,128]{2,1,0:T(8,128)S(1)} collective-permute-done((f32[4,416,128]{2,1,0:T(8,128)S(1)}, f32[4,416,128]{2,1,0:T(8,128)S(1)}, u32[]{:S(2)}, u32[]{:S(2)}) %collective-permute-start.14) | collective-permute-done | bytes 852000 | tf_op jit(solution)/shard_map/ppermute | solution.py:877
  65.7 1.4 %collective-permute-start.15 = (f32[416,128]{1,0:T(8,128)S(1)}, f32[416,128]{1,0:T(8,128)S(1)}, u32[]{:S(2)}, u32[]{:S(2)}) collective-permute-start(f32[416,128]{1,0:T(8,128)S(1)} %get-tuple-element.78), channel_id=1, source_target_pairs={{0,64},{32,96},{64,128},{96,160},{128,192},{160,224},{192,0},{224,... | collective-permute-start | bytes 638984 | tf_op jit(solution)/shard_map/ppermute | solution.py:874
  67.1 1.5 %collective-permute-start.16 = (f32[416,128]{1,0:T(8,128)S(1)}, f32[416,128]{1,0:T(8,128)S(1)}, u32[]{:S(2)}, u32[]{:S(2)}) collective-permute-start(f32[416,128]{1,0:T(8,128)S(1)} %get-tuple-element.79), channel_id=1, source_target_pairs={{0,128},{32,160},{64,192},{96,224},{128,0},{160,32},{192,64},{224,... | collective-permute-start | bytes 638984 | tf_op jit(solution)/shard_map/ppermute | solution.py:874
  68.6 1.9 %collective-permute-start.17 = (f32[416,128]{1,0:T(8,128)S(1)}, f32[416,128]{1,0:T(8,128)S(1)}, u32[]{:S(2)}, u32[]{:S(2)}) collective-permute-start(f32[416,128]{1,0:T(8,128)S(1)} %get-tuple-element.80), channel_id=1, source_target_pairs={{0,192},{32,224},{64,0},{96,32},{128,64},{160,96},{192,128},{224,1... | collective-permute-start | bytes 638984 | tf_op jit(solution)/shard_map/ppermute | solution.py:874
  71.2 6.9 %shard_map.104 = (f32[8,2,128,128]{3,2,1,0:T(8,128)S(1)}, f32[8,384,128]{2,1,0:T(8,128)S(1)}) custom-call(f32[16,2,128,128]{3,2,1,0:T(8,128)S(1)} %get-tuple-element.64.refs_0_, f32[2,2,128,128]{3,2,1,0:T(8,128)S(1)} %get-tuple-element.65.refs_1_, f32[16,2,128,128]{3,2,1,0:T(8,128)S(1)} %get-tuple-element.58.refs_2_.refs_0_.refs_1_, ...), custom_call_target="tpu_custom_call" | custom-call | tf_op jit(solution)/shard_map/pallas_call | solution.py:699
  78.5 1.9 %collective-permute-start.18 = (f32[384,128]{1,0:T(8,128)S(1)}, f32[384,128]{1,0:T(8,128)S(1)}, u32[]{:S(2)}, u32[]{:S(2)}) collective-permute-start(f32[384,128]{1,0:T(8,128)S(1)} %get-tuple-element.89), channel_id=1, source_target_pairs={{0,64},{32,96},{64,128},{96,160},{128,192},{160,224},{192,0},{224,... | collective-permute-start | bytes 589832 | tf_op jit(solution)/shard_map/ppermute | solution.py:874
  80.5 2.7 %collective-permute-start.19 = (f32[384,128]{1,0:T(8,128)S(1)}, f32[384,128]{1,0:T(8,128)S(1)}, u32[]{:S(2)}, u32[]{:S(2)}) collective-permute-start(f32[384,128]{1,0:T(8,128)S(1)} %get-tuple-element.90), channel_id=1, source_target_pairs={{0,128},{32,160},{64,192},{96,224},{128,0},{160,32},{192,64},{224,... | collective-permute-start | bytes 589832 | tf_op jit(solution)/shard_map/ppermute | solution.py:874
  83.4 6.9 %shard_map.107.refs_6_.refs_4_ = f32[8,2,128,128]{3,2,1,0:T(8,128)S(1)} custom-call(f32[16,2,128,128]{3,2,1,0:T(8,128)S(1)} %get-tuple-element.64.refs_0_, f32[2,2,128,128]{3,2,1,0:T(8,128)S(1)} %get-tuple-element.65.refs_1_, f32[16,2,128,128]{3,2,1,0:T(8,128)S(1)} %get-tuple-element.58.refs_2_.refs_0_.refs_1_, ...), custom_call_target="tpu_custom_call" | custom-call | tf_op jit(solution)/shard_map/pallas_call | solution.py:699
  90.3 1.6 %collective-permute-done.19.refs_2_ = f32[384,128]{1,0:T(8,128)S(1)} collective-permute-done((f32[384,128]{1,0:T(8,128)S(1)}, f32[384,128]{1,0:T(8,128)S(1)}, u32[]{:S(2)}, u32[]{:S(2)}) %collective-permute-start.19) | collective-permute-done | bytes 196640 | tf_op jit(solution)/shard_map/ppermute | solution.py:874
  92.3 1.4 %collective-permute-start.21 = (f32[4,384,128]{2,1,0:T(8,128)S(1)}, f32[4,384,128]{2,1,0:T(8,128)S(1)}, u32[]{:S(2)}, u32[]{:S(2)}) collective-permute-start(f32[4,384,128]{2,1,0:T(8,128)S(1)} %get-tuple-element.93.refs_2_), channel_id=1, source_target_pairs={{0,32},{32,0},{64,96},{96,64},{128,160},{160,128},{192,224},{224,1... | collective-permute-start | bytes 2359304 | tf_op jit(solution)/shard_map/ppermute | solution.py:916
  93.7 1.6 %shard_map.109.refs_0_ = f32[16,2,64,128]{3,2,1,0:T(8,128)S(1)} custom-call(f32[4,384,128]{2,1,0:T(8,128)S(1)} %get-tuple-element.92.refs_0_, f32[128,16,128]{2,1,0:T(8,128)S(1)} %shard_map.105.refs_5_.refs_1_.refs_2_, f32[4,384,128]{2,1,0:T(8,128)S(1)} %get-tuple-element.93.refs_2_), custom_call_target="tpu_custom_call" | custom-call | tf_op jit(solution)/shard_map/pallas_call | solution.py:699
  95.6 4.0 %shard_map.110 = bf16[16,96,128]{2,1,0:T(8,128)(2,1)} custom-call(f32[16,2,64,128]{3,2,1,0:T(8,128)S(1)} %shard_map.109.refs_0_, f32[4,384,128]{2,1,0:T(8,128)S(1)} %collective-permute-done.21.refs_1_, f32[128,16,128]{2,1,0:T(8,128)S(1)} %shard_map.105.refs_5_.refs_1_.refs_2_, f32[8,2,128,128]{3,2,1,0:T(8,128)S(1)} %get-tuple-element.94.refs_3_, ...), custom_call_target="tpu_custom_call" | custom-call | tf_op jit(solution)/shard_map/pallas_call | solution.py:699
  (53 shorter events, 7.2 us)
Async XLA Ops:
  0.0 7.0 %copy-start = (bf16[16,96,128]{2,1,0:T(8,128)(2,1)S(1)}, bf16[16,96,128]{2,1,0:T(8,128)(2,1)}, u32[]{:S(2)}) copy-start(bf16[16,96,128]{2,1,0:T(8,128)(2,1)} %refs_1_.3) | copy-start | bytes 1179652
  0.0 7.0 %copy-start.4 = (f32[3]{0:T(128)S(1)}, f32[3]{0:T(128)}, u32[]{:S(2)}) copy-start(f32[3]{0:T(128)} %refs_2_.5) | copy-start | bytes 40
  0.0 7.0 %copy-start.1 = (bf16[96,419]{1,0:T(8,128)(2,1)S(1)}, bf16[96,419]{1,0:T(8,128)(2,1)}, u32[]{:S(2)}) copy-start(bf16[96,419]{1,0:T(8,128)(2,1)} %refs_2_.4) | copy-start | bytes 241348
  0.0 7.0 %copy-start.8 = (f32[3]{0:T(128)S(1)}, f32[3]{0:T(128)}, u32[]{:S(2)}) copy-start(f32[3]{0:T(128)} %refs_4_.1) | copy-start | bytes 40
  0.0 7.0 %copy-start.6 = (f32[224]{0:T(256)S(1)}, f32[224]{0:T(256)}, u32[]{:S(2)}) copy-start(f32[224]{0:T(256)} %param.12) | copy-start | bytes 2692
  0.0 7.0 %copy-start.3 = (f32[3,3,224]{2,1,0:T(4,128)S(1)}, f32[3,3,224]{2,1,0:T(4,128)}, u32[]{:S(2)}) copy-start(f32[3,3,224]{2,1,0:T(4,128)} %refs_2_.3) | copy-start | bytes 24196
  1.6 8.2 %collective-permute-start = (bf16[16,96]{1,0:T(8,128)(2,1)S(1)}, bf16[16,96]{1,0:T(8,128)(2,1)S(1)}, u32[]{:S(2)}, u32[]{:S(2)}) collective-permute-start(bf16[16,96]{1,0:T(8,128)(2,1)S(1)} %bitcast.4), channel_id=1, source_target_pairs={{0,1},{1,2},{2,3},{3,4},{4,5},{5,6},{6,7},{7,8},{8,9},{9,10},{10,1... | collective-permute-start | bytes 9224 | tf_op jit(solution)/shard_map/ppermute | solution.py:730
  5.7 4.3 %collective-permute-start.1 = (bf16[16,96]{1,0:T(8,128)(2,1)S(1)}, bf16[16,96]{1,0:T(8,128)(2,1)S(1)}, u32[]{:S(2)}, u32[]{:S(2)}) collective-permute-start(bf16[16,96]{1,0:T(8,128)(2,1)S(1)} %bitcast.6), channel_id=1, source_target_pairs={{1,0},{2,1},{3,2},{4,3},{5,4},{6,5},{7,6},{8,7},{9,8},{10,9},{11,1... | collective-permute-start | bytes 9224 | tf_op jit(solution)/shard_map/ppermute | solution.py:731
  10.1 10.3 %collective-permute-start.3 = (bf16[112,128]{1,0:T(8,128)(2,1)S(1)}, bf16[112,128]{1,0:T(8,128)(2,1)S(1)}, u32[]{:S(2)}, u32[]{:S(2)}) collective-permute-start(bf16[112,128]{1,0:T(8,128)(2,1)S(1)} %get-tuple-element.56.refs_9_), channel_id=1, source_target_pairs={{32,0},{64,32},{96,64},{128,96},{160,128},{192,160},{224,192},{33,... | collective-permute-start | bytes 86024 | tf_op jit(solution)/shard_map/ppermute | solution.py:752
  14.1 6.3 %collective-permute-start.2 = (bf16[112,128]{1,0:T(8,128)(2,1)S(1)}, bf16[112,128]{1,0:T(8,128)(2,1)S(1)}, u32[]{:S(2)}, u32[]{:S(2)}) collective-permute-start(bf16[112,128]{1,0:T(8,128)(2,1)S(1)} %get-tuple-element.57.refs_10_), channel_id=1, source_target_pairs={{0,32},{32,64},{64,96},{96,128},{128,160},{160,192},{192,224},{1,3... | collective-permute-start | bytes 86024 | tf_op jit(solution)/shard_map/ppermute | solution.py:751
  21.1 9.7 %collective-permute-start.4 = (f32[8,16,128]{2,1,0:T(8,128)S(1)}, f32[8,16,128]{2,1,0:T(8,128)S(1)}, u32[]{:S(2)}, u32[]{:S(2)}) collective-permute-start(f32[8,16,128]{2,1,0:T(8,128)S(1)} %get-tuple-element.61), channel_id=1, source_target_pairs={{0,1},{1,2},{2,3},{3,0},{4,5},{5,6},{6,7},{7,4},{8,9},{9,10},{10,1... | collective-permute-start | bytes 196616 | tf_op jit(solution)/shard_map/ppermute | solution.py:807
  22.4 8.5 %collective-permute-start.5 = (f32[8,16,128]{2,1,0:T(8,128)S(1)}, f32[8,16,128]{2,1,0:T(8,128)S(1)}, u32[]{:S(2)}, u32[]{:S(2)}) collective-permute-start(f32[8,16,128]{2,1,0:T(8,128)S(1)} %get-tuple-element.62), channel_id=1, source_target_pairs={{0,2},{1,3},{2,0},{3,1},{4,6},{5,7},{6,4},{7,5},{8,10},{9,11},{10,... | collective-permute-start | bytes 196616 | tf_op jit(solution)/shard_map/ppermute | solution.py:807
  27.3 3.8 %collective-permute-start.6 = (f32[8,16,128]{2,1,0:T(8,128)S(1)}, f32[8,16,128]{2,1,0:T(8,128)S(1)}, u32[]{:S(2)}, u32[]{:S(2)}) collective-permute-start(f32[8,16,128]{2,1,0:T(8,128)S(1)} %get-tuple-element.63), channel_id=1, source_target_pairs={{0,3},{1,0},{2,1},{3,2},{4,7},{5,4},{6,5},{7,6},{8,11},{9,8},{10,9... | collective-permute-start | bytes 196616 | tf_op jit(solution)/shard_map/ppermute | solution.py:807
  31.1 3.4 %collective-permute-start.7 = (f32[8,16,128]{2,1,0:T(8,128)S(1)}, f32[8,16,128]{2,1,0:T(8,128)S(1)}, u32[]{:S(2)}, u32[]{:S(2)}) collective-permute-start(f32[8,16,128]{2,1,0:T(8,128)S(1)} %shard_map.96.refs_3_.refs_0_), channel_id=1, source_target_pairs={{0,4},{1,5},{2,6},{3,7},{4,0},{5,1},{6,2},{7,3},{8,12},{9,13},{10,... | collective-permute-start | bytes 196616 | tf_op jit(solution)/shard_map/ppermute | solution.py:824
  34.6 15.6 %collective-permute-start.10 = (f32[8,16,128]{2,1,0:T(8,128)S(1)}, f32[8,16,128]{2,1,0:T(8,128)S(1)}, u32[]{:S(2)}, u32[]{:S(2)}) collective-permute-start(f32[8,16,128]{2,1,0:T(8,128)S(1)} %shard_map.98.refs_6_), channel_id=1, source_target_pairs={{0,24},{1,25},{2,26},{3,27},{4,28},{5,29},{6,30},{7,31},{32,56},{3... | collective-permute-start | bytes 196616 | tf_op jit(solution)/shard_map/ppermute | solution.py:846
  41.4 8.8 %collective-permute-start.9 = (f32[8,16,128]{2,1,0:T(8,128)S(1)}, f32[8,16,128]{2,1,0:T(8,128)S(1)}, u32[]{:S(2)}, u32[]{:S(2)}) collective-permute-start(f32[8,16,128]{2,1,0:T(8,128)S(1)} %shard_map.98.refs_6_), channel_id=1, source_target_pairs={{0,16},{1,17},{2,18},{3,19},{4,20},{5,21},{6,22},{7,23},{8,24},{9,... | collective-permute-start | bytes 196616 | tf_op jit(solution)/shard_map/ppermute | solution.py:846
  44.3 5.9 %collective-permute-start.8 = (f32[8,16,128]{2,1,0:T(8,128)S(1)}, f32[8,16,128]{2,1,0:T(8,128)S(1)}, u32[]{:S(2)}, u32[]{:S(2)}) collective-permute-start(f32[8,16,128]{2,1,0:T(8,128)S(1)} %shard_map.98.refs_6_), channel_id=1, source_target_pairs={{0,8},{1,9},{2,10},{3,11},{4,12},{5,13},{6,14},{7,15},{8,16},{9,17... | collective-permute-start | bytes 196616 | tf_op jit(solution)/shard_map/ppermute | solution.py:846
  50.3 5.9 %collective-permute-start.11 = (f32[8,16,128]{2,1,0:T(8,128)S(1)}, f32[8,16,128]{2,1,0:T(8,128)S(1)}, u32[]{:S(2)}, u32[]{:S(2)}) collective-permute-start(f32[8,16,128]{2,1,0:T(8,128)S(1)} %get-tuple-element.72), channel_id=1, source_target_pairs={{0,1},{1,2},{2,3},{3,0},{4,5},{5,6},{6,7},{7,4},{8,9},{9,10},{10,1... | collective-permute-start | bytes 196616 | tf_op jit(solution)/shard_map/ppermute | solution.py:807
  52.0 4.6 %collective-permute-start.12 = (f32[8,16,128]{2,1,0:T(8,128)S(1)}, f32[8,16,128]{2,1,0:T(8,128)S(1)}, u32[]{:S(2)}, u32[]{:S(2)}) collective-permute-start(f32[8,16,128]{2,1,0:T(8,128)S(1)} %get-tuple-element.73), channel_id=1, source_target_pairs={{0,2},{1,3},{2,0},{3,1},{4,6},{5,7},{6,4},{7,5},{8,10},{9,11},{10,... | collective-permute-start | bytes 196616 | tf_op jit(solution)/shard_map/ppermute | solution.py:807
  54.1 3.4 %collective-permute-start.13 = (f32[8,16,128]{2,1,0:T(8,128)S(1)}, f32[8,16,128]{2,1,0:T(8,128)S(1)}, u32[]{:S(2)}, u32[]{:S(2)}) collective-permute-start(f32[8,16,128]{2,1,0:T(8,128)S(1)} %get-tuple-element.74), channel_id=1, source_target_pairs={{0,3},{1,0},{2,1},{3,2},{4,7},{5,4},{6,5},{7,6},{8,11},{9,8},{10,9... | collective-permute-start | bytes 196616 | tf_op jit(solution)/shard_map/ppermute | solution.py:807
  59.7 11.6 %copy-start.5 = (f32[3]{0:T(128)S(1)}, f32[3]{0:T(128)}, u32[]{:S(2)}) copy-start(f32[3]{0:T(128)} %refs_9_.3) | copy-start | bytes 40
  59.7 5.8 %collective-permute-start.14 = (f32[4,416,128]{2,1,0:T(8,128)S(1)}, f32[4,416,128]{2,1,0:T(8,128)S(1)}, u32[]{:S(2)}, u32[]{:S(2)}) collective-permute-start(f32[4,416,128]{2,1,0:T(8,128)S(1)} %get-tuple-element.76), channel_id=1, source_target_pairs={{0,32},{32,0},{64,96},{96,64},{128,160},{160,128},{192,224},{224,1... | collective-permute-start | bytes 2555912 | tf_op jit(solution)/shard_map/ppermute | solution.py:877
  65.7 12.4 %collective-permute-start.15 = (f32[416,128]{1,0:T(8,128)S(1)}, f32[416,128]{1,0:T(8,128)S(1)}, u32[]{:S(2)}, u32[]{:S(2)}) collective-permute-start(f32[416,128]{1,0:T(8,128)S(1)} %get-tuple-element.78), channel_id=1, source_target_pairs={{0,64},{32,96},{64,128},{96,160},{128,192},{160,224},{192,0},{224,... | collective-permute-start | bytes 638984 | tf_op jit(solution)/shard_map/ppermute | solution.py:874
  67.1 11.1 %collective-permute-start.16 = (f32[416,128]{1,0:T(8,128)S(1)}, f32[416,128]{1,0:T(8,128)S(1)}, u32[]{:S(2)}, u32[]{:S(2)}) collective-permute-start(f32[416,128]{1,0:T(8,128)S(1)} %get-tuple-element.79), channel_id=1, source_target_pairs={{0,128},{32,160},{64,192},{96,224},{128,0},{160,32},{192,64},{224,... | collective-permute-start | bytes 638984 | tf_op jit(solution)/shard_map/ppermute | solution.py:874
  68.6 9.7 %collective-permute-start.17 = (f32[416,128]{1,0:T(8,128)S(1)}, f32[416,128]{1,0:T(8,128)S(1)}, u32[]{:S(2)}, u32[]{:S(2)}) collective-permute-start(f32[416,128]{1,0:T(8,128)S(1)} %get-tuple-element.80), channel_id=1, source_target_pairs={{0,192},{32,224},{64,0},{96,32},{128,64},{160,96},{192,128},{224,1... | collective-permute-start | bytes 638984 | tf_op jit(solution)/shard_map/ppermute | solution.py:874
  78.5 11.7 %collective-permute-start.18 = (f32[384,128]{1,0:T(8,128)S(1)}, f32[384,128]{1,0:T(8,128)S(1)}, u32[]{:S(2)}, u32[]{:S(2)}) collective-permute-start(f32[384,128]{1,0:T(8,128)S(1)} %get-tuple-element.89), channel_id=1, source_target_pairs={{0,64},{32,96},{64,128},{96,160},{128,192},{160,224},{192,0},{224,... | collective-permute-start | bytes 589832 | tf_op jit(solution)/shard_map/ppermute | solution.py:874
  80.5 11.4 %collective-permute-start.19 = (f32[384,128]{1,0:T(8,128)S(1)}, f32[384,128]{1,0:T(8,128)S(1)}, u32[]{:S(2)}, u32[]{:S(2)}) collective-permute-start(f32[384,128]{1,0:T(8,128)S(1)} %get-tuple-element.90), channel_id=1, source_target_pairs={{0,128},{32,160},{64,192},{96,224},{128,0},{160,32},{192,64},{224,... | collective-permute-start | bytes 589832 | tf_op jit(solution)/shard_map/ppermute | solution.py:874
  83.2 8.7 %collective-permute-start.20 = (f32[384,128]{1,0:T(8,128)S(1)}, f32[384,128]{1,0:T(8,128)S(1)}, u32[]{:S(2)}, u32[]{:S(2)}) collective-permute-start(f32[384,128]{1,0:T(8,128)S(1)} %get-tuple-element.91), channel_id=1, source_target_pairs={{0,192},{32,224},{64,0},{96,32},{128,64},{160,96},{192,128},{224,1... | collective-permute-start | bytes 589832 | tf_op jit(solution)/shard_map/ppermute | solution.py:874
  92.2 3.4 %copy-start.2 = (bf16[192,96]{1,0:T(8,128)(2,1)S(1)}, bf16[192,96]{1,0:T(8,128)(2,1)}, u32[]{:S(2)}) copy-start(bf16[192,96]{1,0:T(8,128)(2,1)} %refs_7_.1) | copy-start | bytes 110596
  92.2 3.4 %copy-start.7 = (f32[192]{0:T(256)S(1)}, f32[192]{0:T(256)}, u32[]{:S(2)}) copy-start(f32[192]{0:T(256)} %param.16) | copy-start | bytes 2308
  92.3 3.3 %collective-permute-start.21 = (f32[4,384,128]{2,1,0:T(8,128)S(1)}, f32[4,384,128]{2,1,0:T(8,128)S(1)}, u32[]{:S(2)}, u32[]{:S(2)}) collective-permute-start(f32[4,384,128]{2,1,0:T(8,128)S(1)} %get-tuple-element.93.refs_2_), channel_id=1, source_target_pairs={{0,32},{32,0},{64,96},{96,64},{128,160},{160,128},{192,224},{224,1... | collective-permute-start | bytes 2359304 | tf_op jit(solution)/shard_map/ppermute | solution.py:916

commit v6 on v5

--- a/solution.py
+++ b/solution.py
@@ -114,7 +114,7 @@
             raw = out[:, 256 + g * 128 : 384 + g * 128].astype(f32) + by_head(step_bias, g)
             steps[r, g] = softplus(raw)
 
-    each_row(own_row, 8)
+    each_row(own_row, 16)
 
     head = lax.broadcasted_iota(jnp.int32, (8, LANES), 0)
 
@@ -652,7 +652,7 @@
                 carried[:, g, at, :] = result[:, g * 128 : g * 128 + 128]
         return 0
 
-    lax.fori_loop(0, HALVED, block, 0)
+    lax.fori_loop(0, HALVED, block, 0, unroll=HALVED)
 
 
 def exit_kernel(
@@ -679,13 +679,8 @@
         out[r] = result.astype(bf16)
 
     for begins, gated in ((0, gated_a), (ROWS // 2, gated_b)):
-
-        def some(k, carry):
-            for i in range(4):
-                row(begins + 4 * k + i, begins, gated)
-            return carry
-
-        lax.fori_loop(0, ROWS // 8, some, 0)
+        for i in range(ROWS // 2):
+            row(begins + i, begins, gated)
 
 
 def call(kernel, spaces, shapes, scratch, *operands, after=()):

time: 99.8 us -> 98.4 us (0.986)
  Pallas kernels: 39.8 us -> 38 us
    pallas_call x20, Pallas kernels: 39.8 us -> 38 us  [call(): pl.pallas_call(inner, in_specs=[pl.BlockSpec(memory_space=kinds[k]) for k...]
where the time goes in v6:
time: 98.4 us; the launch traced here: 98.1 us
  starting transfers between devices  51.5 us (52%)
  Pallas kernels  38 us (39%)
  waiting for transfers between devices  6.42 us (7%)
  local copies, waits for them, and re-layouts  1.77 us (2%)
    pallas_call x20, Pallas kernels, call(): pl.pallas_call(inner, in_specs=[pl.BlockSpec(memory_space=kinds[k]) for k...  38 us
    ppermute x3, starting transfers between devices, on_device(): lax.ppermute(both, 'gx', [(i, i + 8 * k) for i in range(gx_count - 8 * k)])  12.1 us
    ppermute x6, starting transfers between devices, members(): moved[k] = lax.ppermute(pieces[k], 'gx', pairs)  10.4 us
    ppermute x6, starting transfers between devices, rotate(): moved[k] = lax.ppermute(pieces[k], 'gy', ahead[k])  9.62 us
    ppermute x1, starting transfers between devices, on_device(): below = lax.ppermute(up_row, 'gy', to_up)  4.01 us
    ppermute x1, starting transfers between devices, on_device(): left = lax.ppermute(last, 'gx', to_right)  3.94 us
    ppermute x1, starting transfers between devices, on_device(): theirs = lax.ppermute(theirs, 'gy', swap)  3.9 us
    ppermute x1, starting transfers between devices, on_device(): above = lax.ppermute(down_row, 'gy', to_down)  3.1 us
  transfers between devices with their start and end apart: 22, of which 10 were waited for; matrix products, arithmetic and copies ran while one was open for 0% of the time, Pallas kernels for 32%

profile of v6, /device:TPU:1, one launch (start us, length us, event | category | flops | bytes accessed | tf_op | source)
XLA Modules:
  0.0 98.1 jit_solution(12311021050297861001)
XLA Ops:
  0.0 1.3 %fusion = (bf16[16,96,1]{2,1,0:T(8,128)(2,1)S(1)}, bf16[16,96,1]{2,1,0:T(8,128)(2,1)S(1)}) fusion(bf16[16,96,128]{2,1,0:T(8,128)(2,1)} %refs_1_.3), kind=kLoop, calls=%fused_computation | loop fusion | bytes 12288 | tf_op jit(solution)/shard_map/slice | solution.py:724
  1.6 3.9 %collective-permute-start = (bf16[16,96]{1,0:T(8,128)(2,1)S(1)}, bf16[16,96]{1,0:T(8,128)(2,1)S(1)}, u32[]{:S(2)}, u32[]{:S(2)}) collective-permute-start(bf16[16,96]{1,0:T(8,128)(2,1)S(1)} %bitcast.4), channel_id=1, source_target_pairs={{0,1},{1,2},{2,3},{3,4},{4,5},{5,6},{6,7},{7,8},{8,9},{9,10},{10,1... | collective-permute-start | bytes 9224 | tf_op jit(solution)/shard_map/ppermute | solution.py:725
  5.7 1.3 %collective-permute-start.1 = (bf16[16,96]{1,0:T(8,128)(2,1)S(1)}, bf16[16,96]{1,0:T(8,128)(2,1)S(1)}, u32[]{:S(2)}, u32[]{:S(2)}) collective-permute-start(bf16[16,96]{1,0:T(8,128)(2,1)S(1)} %bitcast.6), channel_id=1, source_target_pairs={{1,0},{2,1},{3,2},{4,3},{5,4},{6,5},{7,6},{8,7},{9,8},{10,9},{11,1... | collective-permute-start | bytes 9224 | tf_op jit(solution)/shard_map/ppermute | solution.py:726
  7.1 2.3 %shard_map.91 = (bf16[16,2,128,128]{3,2,1,0:T(8,128)(2,1)S(1)}, f32[16,2,128,128]{3,2,1,0:T(8,128)S(1)}, f32[16,8,128]{2,1,0:T(8,128)S(1)}, f32[16,8,128]{2,1,0:...) custom-call(bf16[16,96,128]{2,1,0:T(8,128)(2,1)S(1)} %copy-done, bf16[96,419]{1,0:T(8,128)(2,1)S(1)} %copy-done.1, ...), custom_call_target="tpu_custom_call" | custom-call | tf_op jit(solution)/shard_map/pallas_call | solution.py:694
  10.1 4.0 %collective-permute-start.3 = (bf16[112,128]{1,0:T(8,128)(2,1)S(1)}, bf16[112,128]{1,0:T(8,128)(2,1)S(1)}, u32[]{:S(2)}, u32[]{:S(2)}) collective-permute-start(bf16[112,128]{1,0:T(8,128)(2,1)S(1)} %get-tuple-element.56.refs_9_), channel_id=1, source_target_pairs={{32,0},{64,32},{96,64},{128,96},{160,128},{192,160},{224,192},{33,... | collective-permute-start | bytes 86024 | tf_op jit(solution)/shard_map/ppermute | solution.py:747
  14.1 3.1 %collective-permute-start.2 = (bf16[112,128]{1,0:T(8,128)(2,1)S(1)}, bf16[112,128]{1,0:T(8,128)(2,1)S(1)}, u32[]{:S(2)}, u32[]{:S(2)}) collective-permute-start(bf16[112,128]{1,0:T(8,128)(2,1)S(1)} %get-tuple-element.57.refs_10_), channel_id=1, source_target_pairs={{0,32},{32,64},{64,96},{96,128},{128,160},{160,192},{192,224},{1,3... | collective-permute-start | bytes 86024 | tf_op jit(solution)/shard_map/ppermute | solution.py:746
  17.2 3.2 %shard_map.93 = (f32[16,2,128,128]{3,2,1,0:T(8,128)S(1)}, f32[16,2,128,128]{3,2,1,0:T(8,128)S(1)}, bf16[16,2,128,128]{3,2,1,0:T(8,128)(2,1)S(1)}, f32[16,32,128]...) custom-call(bf16[16,2,128,128]{3,2,1,0:T(8,128)(2,1)S(1)} %get-tuple-element.51.refs_0_, ...), custom_call_target="tpu_custom_call" | custom-call | tf_op jit(solution)/shard_map/pallas_call | solution.py:694
  21.1 1.3 %collective-permute-start.4 = (f32[8,16,128]{2,1,0:T(8,128)S(1)}, f32[8,16,128]{2,1,0:T(8,128)S(1)}, u32[]{:S(2)}, u32[]{:S(2)}) collective-permute-start(f32[8,16,128]{2,1,0:T(8,128)S(1)} %get-tuple-element.61), channel_id=1, source_target_pairs={{0,1},{1,2},{2,3},{3,0},{4,5},{5,6},{6,7},{7,4},{8,9},{9,10},{10,1... | collective-permute-start | bytes 196616 | tf_op jit(solution)/shard_map/ppermute | solution.py:802
  22.4 4.9 %collective-permute-start.5 = (f32[8,16,128]{2,1,0:T(8,128)S(1)}, f32[8,16,128]{2,1,0:T(8,128)S(1)}, u32[]{:S(2)}, u32[]{:S(2)}) collective-permute-start(f32[8,16,128]{2,1,0:T(8,128)S(1)} %get-tuple-element.62), channel_id=1, source_target_pairs={{0,2},{1,3},{2,0},{3,1},{4,6},{5,7},{6,4},{7,5},{8,10},{9,11},{10,... | collective-permute-start | bytes 196616 | tf_op jit(solution)/shard_map/ppermute | solution.py:802
  27.3 3.4 %shard_map.95 = (f32[4,416,128]{2,1,0:T(8,128)S(1)}, f32[48,8,128]{2,1,0:T(8,128)S(1)}) custom-call(f32[16,2,128,128]{3,2,1,0:T(8,128)S(1)} %get-tuple-element.64.refs_0_, f32[2,2,128,128]{3,2,1,0:T(8,128)S(1)} %get-tuple-element.65.refs_1_, f32[16,2,128,128]{3,2,1,0:T(8,128)S(1)} %get-tuple-element.58.refs_2_.refs_0_.refs_1_, ...), custom_call_target="tpu_custom_call" | custom-call | tf_op jit(solution)/shard_map/pallas_call | solution.py:694
  31.1 1.7 %collective-permute-start.7 = (f32[8,16,128]{2,1,0:T(8,128)S(1)}, f32[8,16,128]{2,1,0:T(8,128)S(1)}, u32[]{:S(2)}, u32[]{:S(2)}) collective-permute-start(f32[8,16,128]{2,1,0:T(8,128)S(1)} %shard_map.96.refs_3_.refs_0_), channel_id=1, source_target_pairs={{0,4},{1,5},{2,6},{3,7},{4,0},{5,1},{6,2},{7,3},{8,12},{9,13},{10,... | collective-permute-start | bytes 196616 | tf_op jit(solution)/shard_map/ppermute | solution.py:819
  32.9 1.5 %shard_map.97 = (f32[16,2,128,128]{3,2,1,0:T(8,128)S(1)}, f32[16,2,128,128]{3,2,1,0:T(8,128)S(1)}) custom-call(f32[16,2,128,128]{3,2,1,0:T(8,128)S(1)} %get-tuple-element.58.refs_2_.refs_0_.refs_1_, bf16[16,96,128]{2,1,0:T(8,128)(2,1)S(1)} %copy-done, bf16[96,419]{1,0:T(8,128)(2,1)S(1)} %copy-done.1, f32[8,16,128]{2,1,0:T(8,128)S(1)} %shard_map.96.refs_3_.refs_0_), custom_call_target="tpu_custom_call" | custom-call | tf_op jit(solution)/shard_map/pallas_call | solution.py:694
  34.6 6.9 %collective-permute-start.10 = (f32[8,16,128]{2,1,0:T(8,128)S(1)}, f32[8,16,128]{2,1,0:T(8,128)S(1)}, u32[]{:S(2)}, u32[]{:S(2)}) collective-permute-start(f32[8,16,128]{2,1,0:T(8,128)S(1)} %shard_map.98.refs_6_), channel_id=1, source_target_pairs={{0,24},{1,25},{2,26},{3,27},{4,28},{5,29},{6,30},{7,31},{32,56},{3... | collective-permute-start | bytes 196616 | tf_op jit(solution)/shard_map/ppermute | solution.py:841
  41.4 2.6 %collective-permute-start.9 = (f32[8,16,128]{2,1,0:T(8,128)S(1)}, f32[8,16,128]{2,1,0:T(8,128)S(1)}, u32[]{:S(2)}, u32[]{:S(2)}) collective-permute-start(f32[8,16,128]{2,1,0:T(8,128)S(1)} %shard_map.98.refs_6_), channel_id=1, source_target_pairs={{0,16},{1,17},{2,18},{3,19},{4,20},{5,21},{6,22},{7,23},{8,24},{9,... | collective-permute-start | bytes 196616 | tf_op jit(solution)/shard_map/ppermute | solution.py:841
  44.0 2.7 %collective-permute-start.8 = (f32[8,16,128]{2,1,0:T(8,128)S(1)}, f32[8,16,128]{2,1,0:T(8,128)S(1)}, u32[]{:S(2)}, u32[]{:S(2)}) collective-permute-start(f32[8,16,128]{2,1,0:T(8,128)S(1)} %shard_map.98.refs_6_), channel_id=1, source_target_pairs={{0,8},{1,9},{2,10},{3,11},{4,12},{5,13},{6,14},{7,15},{8,16},{9,17... | collective-permute-start | bytes 196616 | tf_op jit(solution)/shard_map/ppermute | solution.py:841
  46.7 3.4 %shard_map.99.refs_8_.refs_2_ = f32[4,416,128]{2,1,0:T(8,128)S(1)} custom-call(f32[16,2,128,128]{3,2,1,0:T(8,128)S(1)} %get-tuple-element.64.refs_0_, f32[2,2,128,128]{3,2,1,0:T(8,128)S(1)} %get-tuple-element.65.refs_1_, f32[16,2,128,128]{3,2,1,0:T(8,128)S(1)} %get-tuple-element.58.refs_2_.refs_0_.refs_1_, f32[16,32,128]{2,1,0:T(8,128)S(1)} %get-tuple-element.66.refs_3_, ...), custom_call_target="tpu_custom_call" | custom-call | tf_op jit(solution)/shard_map/pallas_call | solution.py:694
  50.3 1.7 %collective-permute-start.11 = (f32[8,16,128]{2,1,0:T(8,128)S(1)}, f32[8,16,128]{2,1,0:T(8,128)S(1)}, u32[]{:S(2)}, u32[]{:S(2)}) collective-permute-start(f32[8,16,128]{2,1,0:T(8,128)S(1)} %get-tuple-element.72), channel_id=1, source_target_pairs={{0,1},{1,2},{2,3},{3,0},{4,5},{5,6},{6,7},{7,4},{8,9},{9,10},{10,1... | collective-permute-start | bytes 196616 | tf_op jit(solution)/shard_map/ppermute | solution.py:802
  52.0 1.8 %collective-permute-start.12 = (f32[8,16,128]{2,1,0:T(8,128)S(1)}, f32[8,16,128]{2,1,0:T(8,128)S(1)}, u32[]{:S(2)}, u32[]{:S(2)}) collective-permute-start(f32[8,16,128]{2,1,0:T(8,128)S(1)} %get-tuple-element.73), channel_id=1, source_target_pairs={{0,2},{1,3},{2,0},{3,1},{4,6},{5,7},{6,4},{7,5},{8,10},{9,11},{10,... | collective-permute-start | bytes 196616 | tf_op jit(solution)/shard_map/ppermute | solution.py:802
  54.5 1.7 %shard_map.101.refs_0_ = f32[16,2,128,128]{3,2,1,0:T(8,128)S(1)} custom-call(f32[16,2,128,128]{3,2,1,0:T(8,128)S(1)} %get-tuple-element.50.refs_3_.refs_5_.refs_0_, f32[16,2,128,128]{3,2,1,0:T(8,128)S(1)} %get-tuple-element.58.refs_2_.refs_0_.refs_1_, f32[3]{0:T(128)S(1)} %copy-done.4, f32[8,16,128]{2,1,0:T(8,128)S(1)} %get-tuple-element.70.refs_3_), custom_call_target="tpu_custom_call" | custom-call | tf_op jit(solution)/shard_map/pallas_call | solution.py:694
  56.9 2.4 %shard_map.102 = (f32[4,416,128]{2,1,0:T(8,128)S(1)}, f32[4,416,128]{2,1,0:T(8,128)S(1)}, f32[32,16,128]{2,1,0:T(8,128)S(1)}) custom-call(f32[16,2,128,128]{3,2,1,0:T(8,128)S(1)} %shard_map.101.refs_0_, f32[4,416,128]{2,1,0:T(8,128)S(1)} %get-tuple-element.71.refs_1_, f32[4,416,128]{2,1,0:T(8,128)S(1)} %shard_map.99.refs_8_.refs_2_, ...), custom_call_target="tpu_custom_call" | custom-call | tf_op jit(solution)/shard_map/pallas_call | solution.py:694
  59.2 3.9 %collective-permute-start.14 = (f32[4,416,128]{2,1,0:T(8,128)S(1)}, f32[4,416,128]{2,1,0:T(8,128)S(1)}, u32[]{:S(2)}, u32[]{:S(2)}) collective-permute-start(f32[4,416,128]{2,1,0:T(8,128)S(1)} %get-tuple-element.76), channel_id=1, source_target_pairs={{0,32},{32,0},{64,96},{96,64},{128,160},{160,128},{192,224},{224,1... | collective-permute-start | bytes 2555912 | tf_op jit(solution)/shard_map/ppermute | solution.py:872
  63.1 2.0 %collective-permute-done.14.refs_1_.refs_5_ = f32[4,416,128]{2,1,0:T(8,128)S(1)} collective-permute-done((f32[4,416,128]{2,1,0:T(8,128)S(1)}, f32[4,416,128]{2,1,0:T(8,128)S(1)}, u32[]{:S(2)}, u32[]{:S(2)}) %collective-permute-start.14) | collective-permute-done | bytes 852000 | tf_op jit(solution)/shard_map/ppermute | solution.py:872
  65.4 1.4 %collective-permute-start.15 = (f32[416,128]{1,0:T(8,128)S(1)}, f32[416,128]{1,0:T(8,128)S(1)}, u32[]{:S(2)}, u32[]{:S(2)}) collective-permute-start(f32[416,128]{1,0:T(8,128)S(1)} %get-tuple-element.78), channel_id=1, source_target_pairs={{0,64},{32,96},{64,128},{96,160},{128,192},{160,224},{192,0},{224,... | collective-permute-start | bytes 638984 | tf_op jit(solution)/shard_map/ppermute | solution.py:869
  66.8 1.6 %collective-permute-start.16 = (f32[416,128]{1,0:T(8,128)S(1)}, f32[416,128]{1,0:T(8,128)S(1)}, u32[]{:S(2)}, u32[]{:S(2)}) collective-permute-start(f32[416,128]{1,0:T(8,128)S(1)} %get-tuple-element.79), channel_id=1, source_target_pairs={{0,128},{32,160},{64,192},{96,224},{128,0},{160,32},{192,64},{224,... | collective-permute-start | bytes 638984 | tf_op jit(solution)/shard_map/ppermute | solution.py:869
  68.4 1.8 %collective-permute-start.17 = (f32[416,128]{1,0:T(8,128)S(1)}, f32[416,128]{1,0:T(8,128)S(1)}, u32[]{:S(2)}, u32[]{:S(2)}) collective-permute-start(f32[416,128]{1,0:T(8,128)S(1)} %get-tuple-element.80), channel_id=1, source_target_pairs={{0,192},{32,224},{64,0},{96,32},{128,64},{160,96},{192,128},{224,1... | collective-permute-start | bytes 638984 | tf_op jit(solution)/shard_map/ppermute | solution.py:869
  70.9 6.9 %shard_map.104 = (f32[8,2,128,128]{3,2,1,0:T(8,128)S(1)}, f32[8,384,128]{2,1,0:T(8,128)S(1)}) custom-call(f32[16,2,128,128]{3,2,1,0:T(8,128)S(1)} %get-tuple-element.64.refs_0_, f32[2,2,128,128]{3,2,1,0:T(8,128)S(1)} %get-tuple-element.65.refs_1_, f32[16,2,128,128]{3,2,1,0:T(8,128)S(1)} %get-tuple-element.58.refs_2_.refs_0_.refs_1_, ...), custom_call_target="tpu_custom_call" | custom-call | tf_op jit(solution)/shard_map/pallas_call | solution.py:694
  78.2 1.9 %collective-permute-start.18 = (f32[384,128]{1,0:T(8,128)S(1)}, f32[384,128]{1,0:T(8,128)S(1)}, u32[]{:S(2)}, u32[]{:S(2)}) collective-permute-start(f32[384,128]{1,0:T(8,128)S(1)} %get-tuple-element.89), channel_id=1, source_target_pairs={{0,64},{32,96},{64,128},{96,160},{128,192},{160,224},{192,0},{224,... | collective-permute-start | bytes 589832 | tf_op jit(solution)/shard_map/ppermute | solution.py:869
  80.1 2.7 %collective-permute-start.19 = (f32[384,128]{1,0:T(8,128)S(1)}, f32[384,128]{1,0:T(8,128)S(1)}, u32[]{:S(2)}, u32[]{:S(2)}) collective-permute-start(f32[384,128]{1,0:T(8,128)S(1)} %get-tuple-element.90), channel_id=1, source_target_pairs={{0,128},{32,160},{64,192},{96,224},{128,0},{160,32},{192,64},{224,... | collective-permute-start | bytes 589832 | tf_op jit(solution)/shard_map/ppermute | solution.py:869
  83.1 6.9 %shard_map.107.refs_6_.refs_4_ = f32[8,2,128,128]{3,2,1,0:T(8,128)S(1)} custom-call(f32[16,2,128,128]{3,2,1,0:T(8,128)S(1)} %get-tuple-element.64.refs_0_, f32[2,2,128,128]{3,2,1,0:T(8,128)S(1)} %get-tuple-element.65.refs_1_, f32[16,2,128,128]{3,2,1,0:T(8,128)S(1)} %get-tuple-element.58.refs_2_.refs_0_.refs_1_, ...), custom_call_target="tpu_custom_call" | custom-call | tf_op jit(solution)/shard_map/pallas_call | solution.py:694
  90.0 1.6 %collective-permute-done.19.refs_2_ = f32[384,128]{1,0:T(8,128)S(1)} collective-permute-done((f32[384,128]{1,0:T(8,128)S(1)}, f32[384,128]{1,0:T(8,128)S(1)}, u32[]{:S(2)}, u32[]{:S(2)}) %collective-permute-start.19) | collective-permute-done | bytes 196640 | tf_op jit(solution)/shard_map/ppermute | solution.py:869
  91.9 1.4 %collective-permute-start.21 = (f32[4,384,128]{2,1,0:T(8,128)S(1)}, f32[4,384,128]{2,1,0:T(8,128)S(1)}, u32[]{:S(2)}, u32[]{:S(2)}) collective-permute-start(f32[4,384,128]{2,1,0:T(8,128)S(1)} %get-tuple-element.93.refs_2_), channel_id=1, source_target_pairs={{0,32},{32,0},{64,96},{96,64},{128,160},{160,128},{192,224},{224,1... | collective-permute-start | bytes 2359304 | tf_op jit(solution)/shard_map/ppermute | solution.py:911
  95.3 2.8 %shard_map.110 = bf16[16,96,128]{2,1,0:T(8,128)(2,1)} custom-call(f32[16,2,64,128]{3,2,1,0:T(8,128)S(1)} %shard_map.109.refs_0_, f32[4,384,128]{2,1,0:T(8,128)S(1)} %collective-permute-done.21.refs_1_, f32[128,16,128]{2,1,0:T(8,128)S(1)} %shard_map.105.refs_5_.refs_1_.refs_2_, f32[8,2,128,128]{3,2,1,0:T(8,128)S(1)} %get-tuple-element.94.refs_3_, ...), custom_call_target="tpu_custom_call" | custom-call | tf_op jit(solution)/shard_map/pallas_call | solution.py:694
  (53 shorter events, 7.6 us)
Async XLA Ops:
  0.0 7.0 %copy-start = (bf16[16,96,128]{2,1,0:T(8,128)(2,1)S(1)}, bf16[16,96,128]{2,1,0:T(8,128)(2,1)}, u32[]{:S(2)}) copy-start(bf16[16,96,128]{2,1,0:T(8,128)(2,1)} %refs_1_.3) | copy-start | bytes 1179652
  0.0 7.0 %copy-start.4 = (f32[3]{0:T(128)S(1)}, f32[3]{0:T(128)}, u32[]{:S(2)}) copy-start(f32[3]{0:T(128)} %refs_2_.5) | copy-start | bytes 40
  0.0 7.0 %copy-start.1 = (bf16[96,419]{1,0:T(8,128)(2,1)S(1)}, bf16[96,419]{1,0:T(8,128)(2,1)}, u32[]{:S(2)}) copy-start(bf16[96,419]{1,0:T(8,128)(2,1)} %refs_2_.4) | copy-start | bytes 241348
  0.0 7.0 %copy-start.8 = (f32[3]{0:T(128)S(1)}, f32[3]{0:T(128)}, u32[]{:S(2)}) copy-start(f32[3]{0:T(128)} %refs_4_.1) | copy-start | bytes 40
  0.0 7.0 %copy-start.6 = (f32[224]{0:T(256)S(1)}, f32[224]{0:T(256)}, u32[]{:S(2)}) copy-start(f32[224]{0:T(256)} %param.12) | copy-start | bytes 2692
  0.0 7.0 %copy-start.3 = (f32[3,3,224]{2,1,0:T(4,128)S(1)}, f32[3,3,224]{2,1,0:T(4,128)}, u32[]{:S(2)}) copy-start(f32[3,3,224]{2,1,0:T(4,128)} %refs_2_.3) | copy-start | bytes 24196
  1.6 7.9 %collective-permute-start = (bf16[16,96]{1,0:T(8,128)(2,1)S(1)}, bf16[16,96]{1,0:T(8,128)(2,1)S(1)}, u32[]{:S(2)}, u32[]{:S(2)}) collective-permute-start(bf16[16,96]{1,0:T(8,128)(2,1)S(1)} %bitcast.4), channel_id=1, source_target_pairs={{0,1},{1,2},{2,3},{3,4},{4,5},{5,6},{6,7},{7,8},{8,9},{9,10},{10,1... | collective-permute-start | bytes 9224 | tf_op jit(solution)/shard_map/ppermute | solution.py:725
  5.7 4.3 %collective-permute-start.1 = (bf16[16,96]{1,0:T(8,128)(2,1)S(1)}, bf16[16,96]{1,0:T(8,128)(2,1)S(1)}, u32[]{:S(2)}, u32[]{:S(2)}) collective-permute-start(bf16[16,96]{1,0:T(8,128)(2,1)S(1)} %bitcast.6), channel_id=1, source_target_pairs={{1,0},{2,1},{3,2},{4,3},{5,4},{6,5},{7,6},{8,7},{9,8},{10,9},{11,1... | collective-permute-start | bytes 9224 | tf_op jit(solution)/shard_map/ppermute | solution.py:726
  10.1 10.3 %collective-permute-start.3 = (bf16[112,128]{1,0:T(8,128)(2,1)S(1)}, bf16[112,128]{1,0:T(8,128)(2,1)S(1)}, u32[]{:S(2)}, u32[]{:S(2)}) collective-permute-start(bf16[112,128]{1,0:T(8,128)(2,1)S(1)} %get-tuple-element.56.refs_9_), channel_id=1, source_target_pairs={{32,0},{64,32},{96,64},{128,96},{160,128},{192,160},{224,192},{33,... | collective-permute-start | bytes 86024 | tf_op jit(solution)/shard_map/ppermute | solution.py:747
  14.1 6.3 %collective-permute-start.2 = (bf16[112,128]{1,0:T(8,128)(2,1)S(1)}, bf16[112,128]{1,0:T(8,128)(2,1)S(1)}, u32[]{:S(2)}, u32[]{:S(2)}) collective-permute-start(bf16[112,128]{1,0:T(8,128)(2,1)S(1)} %get-tuple-element.57.refs_10_), channel_id=1, source_target_pairs={{0,32},{32,64},{64,96},{96,128},{128,160},{160,192},{192,224},{1,3... | collective-permute-start | bytes 86024 | tf_op jit(solution)/shard_map/ppermute | solution.py:746
  21.1 9.7 %collective-permute-start.4 = (f32[8,16,128]{2,1,0:T(8,128)S(1)}, f32[8,16,128]{2,1,0:T(8,128)S(1)}, u32[]{:S(2)}, u32[]{:S(2)}) collective-permute-start(f32[8,16,128]{2,1,0:T(8,128)S(1)} %get-tuple-element.61), channel_id=1, source_target_pairs={{0,1},{1,2},{2,3},{3,0},{4,5},{5,6},{6,7},{7,4},{8,9},{9,10},{10,1... | collective-permute-start | bytes 196616 | tf_op jit(solution)/shard_map/ppermute | solution.py:802
  22.4 8.5 %collective-permute-start.5 = (f32[8,16,128]{2,1,0:T(8,128)S(1)}, f32[8,16,128]{2,1,0:T(8,128)S(1)}, u32[]{:S(2)}, u32[]{:S(2)}) collective-permute-start(f32[8,16,128]{2,1,0:T(8,128)S(1)} %get-tuple-element.62), channel_id=1, source_target_pairs={{0,2},{1,3},{2,0},{3,1},{4,6},{5,7},{6,4},{7,5},{8,10},{9,11},{10,... | collective-permute-start | bytes 196616 | tf_op jit(solution)/shard_map/ppermute | solution.py:802
  27.3 3.8 %collective-permute-start.6 = (f32[8,16,128]{2,1,0:T(8,128)S(1)}, f32[8,16,128]{2,1,0:T(8,128)S(1)}, u32[]{:S(2)}, u32[]{:S(2)}) collective-permute-start(f32[8,16,128]{2,1,0:T(8,128)S(1)} %get-tuple-element.63), channel_id=1, source_target_pairs={{0,3},{1,0},{2,1},{3,2},{4,7},{5,4},{6,5},{7,6},{8,11},{9,8},{10,9... | collective-permute-start | bytes 196616 | tf_op jit(solution)/shard_map/ppermute | solution.py:802
  31.1 3.4 %collective-permute-start.7 = (f32[8,16,128]{2,1,0:T(8,128)S(1)}, f32[8,16,128]{2,1,0:T(8,128)S(1)}, u32[]{:S(2)}, u32[]{:S(2)}) collective-permute-start(f32[8,16,128]{2,1,0:T(8,128)S(1)} %shard_map.96.refs_3_.refs_0_), channel_id=1, source_target_pairs={{0,4},{1,5},{2,6},{3,7},{4,0},{5,1},{6,2},{7,3},{8,12},{9,13},{10,... | collective-permute-start | bytes 196616 | tf_op jit(solution)/shard_map/ppermute | solution.py:819
  34.6 15.6 %collective-permute-start.10 = (f32[8,16,128]{2,1,0:T(8,128)S(1)}, f32[8,16,128]{2,1,0:T(8,128)S(1)}, u32[]{:S(2)}, u32[]{:S(2)}) collective-permute-start(f32[8,16,128]{2,1,0:T(8,128)S(1)} %shard_map.98.refs_6_), channel_id=1, source_target_pairs={{0,24},{1,25},{2,26},{3,27},{4,28},{5,29},{6,30},{7,31},{32,56},{3... | collective-permute-start | bytes 196616 | tf_op jit(solution)/shard_map/ppermute | solution.py:841
  41.4 8.8 %collective-permute-start.9 = (f32[8,16,128]{2,1,0:T(8,128)S(1)}, f32[8,16,128]{2,1,0:T(8,128)S(1)}, u32[]{:S(2)}, u32[]{:S(2)}) collective-permute-start(f32[8,16,128]{2,1,0:T(8,128)S(1)} %shard_map.98.refs_6_), channel_id=1, source_target_pairs={{0,16},{1,17},{2,18},{3,19},{4,20},{5,21},{6,22},{7,23},{8,24},{9,... | collective-permute-start | bytes 196616 | tf_op jit(solution)/shard_map/ppermute | solution.py:841
  44.0 6.2 %collective-permute-start.8 = (f32[8,16,128]{2,1,0:T(8,128)S(1)}, f32[8,16,128]{2,1,0:T(8,128)S(1)}, u32[]{:S(2)}, u32[]{:S(2)}) collective-permute-start(f32[8,16,128]{2,1,0:T(8,128)S(1)} %shard_map.98.refs_6_), channel_id=1, source_target_pairs={{0,8},{1,9},{2,10},{3,11},{4,12},{5,13},{6,14},{7,15},{8,16},{9,17... | collective-permute-start | bytes 196616 | tf_op jit(solution)/shard_map/ppermute | solution.py:841
  50.3 5.9 %collective-permute-start.11 = (f32[8,16,128]{2,1,0:T(8,128)S(1)}, f32[8,16,128]{2,1,0:T(8,128)S(1)}, u32[]{:S(2)}, u32[]{:S(2)}) collective-permute-start(f32[8,16,128]{2,1,0:T(8,128)S(1)} %get-tuple-element.72), channel_id=1, source_target_pairs={{0,1},{1,2},{2,3},{3,0},{4,5},{5,6},{6,7},{7,4},{8,9},{9,10},{10,1... | collective-permute-start | bytes 196616 | tf_op jit(solution)/shard_map/ppermute | solution.py:802
  52.0 4.6 %collective-permute-start.12 = (f32[8,16,128]{2,1,0:T(8,128)S(1)}, f32[8,16,128]{2,1,0:T(8,128)S(1)}, u32[]{:S(2)}, u32[]{:S(2)}) collective-permute-start(f32[8,16,128]{2,1,0:T(8,128)S(1)} %get-tuple-element.73), channel_id=1, source_target_pairs={{0,2},{1,3},{2,0},{3,1},{4,6},{5,7},{6,4},{7,5},{8,10},{9,11},{10,... | collective-permute-start | bytes 196616 | tf_op jit(solution)/shard_map/ppermute | solution.py:802
  53.7 3.1 %collective-permute-start.13 = (f32[8,16,128]{2,1,0:T(8,128)S(1)}, f32[8,16,128]{2,1,0:T(8,128)S(1)}, u32[]{:S(2)}, u32[]{:S(2)}) collective-permute-start(f32[8,16,128]{2,1,0:T(8,128)S(1)} %get-tuple-element.74), channel_id=1, source_target_pairs={{0,3},{1,0},{2,1},{3,2},{4,7},{5,4},{6,5},{7,6},{8,11},{9,8},{10,9... | collective-permute-start | bytes 196616 | tf_op jit(solution)/shard_map/ppermute | solution.py:802
  59.2 11.7 %copy-start.5 = (f32[3]{0:T(128)S(1)}, f32[3]{0:T(128)}, u32[]{:S(2)}) copy-start(f32[3]{0:T(128)} %refs_9_.3) | copy-start | bytes 40
  59.2 5.9 %collective-permute-start.14 = (f32[4,416,128]{2,1,0:T(8,128)S(1)}, f32[4,416,128]{2,1,0:T(8,128)S(1)}, u32[]{:S(2)}, u32[]{:S(2)}) collective-permute-start(f32[4,416,128]{2,1,0:T(8,128)S(1)} %get-tuple-element.76), channel_id=1, source_target_pairs={{0,32},{32,0},{64,96},{96,64},{128,160},{160,128},{192,224},{224,1... | collective-permute-start | bytes 2555912 | tf_op jit(solution)/shard_map/ppermute | solution.py:872
  65.4 12.4 %collective-permute-start.15 = (f32[416,128]{1,0:T(8,128)S(1)}, f32[416,128]{1,0:T(8,128)S(1)}, u32[]{:S(2)}, u32[]{:S(2)}) collective-permute-start(f32[416,128]{1,0:T(8,128)S(1)} %get-tuple-element.78), channel_id=1, source_target_pairs={{0,64},{32,96},{64,128},{96,160},{128,192},{160,224},{192,0},{224,... | collective-permute-start | bytes 638984 | tf_op jit(solution)/shard_map/ppermute | solution.py:869
  66.8 11.2 %collective-permute-start.16 = (f32[416,128]{1,0:T(8,128)S(1)}, f32[416,128]{1,0:T(8,128)S(1)}, u32[]{:S(2)}, u32[]{:S(2)}) collective-permute-start(f32[416,128]{1,0:T(8,128)S(1)} %get-tuple-element.79), channel_id=1, source_target_pairs={{0,128},{32,160},{64,192},{96,224},{128,0},{160,32},{192,64},{224,... | collective-permute-start | bytes 638984 | tf_op jit(solution)/shard_map/ppermute | solution.py:869
  68.4 9.6 %collective-permute-start.17 = (f32[416,128]{1,0:T(8,128)S(1)}, f32[416,128]{1,0:T(8,128)S(1)}, u32[]{:S(2)}, u32[]{:S(2)}) collective-permute-start(f32[416,128]{1,0:T(8,128)S(1)} %get-tuple-element.80), channel_id=1, source_target_pairs={{0,192},{32,224},{64,0},{96,32},{128,64},{160,96},{192,128},{224,1... | collective-permute-start | bytes 638984 | tf_op jit(solution)/shard_map/ppermute | solution.py:869
  78.2 11.7 %collective-permute-start.18 = (f32[384,128]{1,0:T(8,128)S(1)}, f32[384,128]{1,0:T(8,128)S(1)}, u32[]{:S(2)}, u32[]{:S(2)}) collective-permute-start(f32[384,128]{1,0:T(8,128)S(1)} %get-tuple-element.89), channel_id=1, source_target_pairs={{0,64},{32,96},{64,128},{96,160},{128,192},{160,224},{192,0},{224,... | collective-permute-start | bytes 589832 | tf_op jit(solution)/shard_map/ppermute | solution.py:869
  80.1 11.4 %collective-permute-start.19 = (f32[384,128]{1,0:T(8,128)S(1)}, f32[384,128]{1,0:T(8,128)S(1)}, u32[]{:S(2)}, u32[]{:S(2)}) collective-permute-start(f32[384,128]{1,0:T(8,128)S(1)} %get-tuple-element.90), channel_id=1, source_target_pairs={{0,128},{32,160},{64,192},{96,224},{128,0},{160,32},{192,64},{224,... | collective-permute-start | bytes 589832 | tf_op jit(solution)/shard_map/ppermute | solution.py:869
  82.9 8.7 %collective-permute-start.20 = (f32[384,128]{1,0:T(8,128)S(1)}, f32[384,128]{1,0:T(8,128)S(1)}, u32[]{:S(2)}, u32[]{:S(2)}) collective-permute-start(f32[384,128]{1,0:T(8,128)S(1)} %get-tuple-element.91), channel_id=1, source_target_pairs={{0,192},{32,224},{64,0},{96,32},{128,64},{160,96},{192,128},{224,1... | collective-permute-start | bytes 589832 | tf_op jit(solution)/shard_map/ppermute | solution.py:869
  91.9 3.4 %copy-start.2 = (bf16[192,96]{1,0:T(8,128)(2,1)S(1)}, bf16[192,96]{1,0:T(8,128)(2,1)}, u32[]{:S(2)}) copy-start(bf16[192,96]{1,0:T(8,128)(2,1)} %refs_7_.1) | copy-start | bytes 110596
  91.9 3.4 %copy-start.7 = (f32[192]{0:T(256)S(1)}, f32[192]{0:T(256)}, u32[]{:S(2)}) copy-start(f32[192]{0:T(256)} %param.16) | copy-start | bytes 2308
  91.9 3.3 %collective-permute-start.21 = (f32[4,384,128]{2,1,0:T(8,128)S(1)}, f32[4,384,128]{2,1,0:T(8,128)S(1)}, u32[]{:S(2)}, u32[]{:S(2)}) collective-permute-start(f32[4,384,128]{2,1,0:T(8,128)S(1)} %get-tuple-element.93.refs_2_), channel_id=1, source_target_pairs={{0,32},{32,0},{64,96},{96,64},{128,160},{160,128},{192,224},{224,1... | collective-permute-start | bytes 2359304 | tf_op jit(solution)/shard_map/ppermute | solution.py:911

commit v7 on v6

--- a/solution.py
+++ b/solution.py
@@ -80,12 +80,14 @@
     decay_log,
     inner,
     steps,
+    decay,
     compact,
     totals,
     conv_w,
     taps,
     weight,
 ):
+    rate = [-jnp.exp(by_head(decay_log, g)) for g in range(2)]
     load_taps(conv_weight, conv_bias, taps)
     source = in_weight[...].astype(f32)
     chan_b, chan_c = source[:, 384:400], source[:, 400:416]
@@ -113,6 +115,7 @@
             inner[r, g] = out[:, g * 128 : g * 128 + 128]
             raw = out[:, 256 + g * 128 : 384 + g * 128].astype(f32) + by_head(step_bias, g)
             steps[r, g] = softplus(raw)
+            decay[r, g] = jnp.exp(rate[g] * steps[r, g])
 
     each_row(own_row, 16)
 
@@ -208,9 +211,7 @@
     totals,
     conv_w,
     taps,
-    decay_log,
     xdt,
-    decay,
     act,
     bct,
     maps,
@@ -218,12 +219,10 @@
     proj,
 ):
     put_sides(left, right, conv_w, proj, 0, 0, ROWS)
-    rate = [-jnp.exp(by_head(decay_log, g)) for g in range(2)]
 
     def own_row(r):
         for g in range(2):
             proj[r, g, 8:136, :] = inner[r, g].astype(f32)
-            decay[r, g] = jnp.exp(rate[g] * steps[r, g])
 
     each_row(own_row, 4)
 
@@ -235,7 +234,7 @@
             finish_row(parts, *refs, ends.at[pl.ds(2 * r, 2)])
         return carry
 
-    lax.fori_loop(0, 2, some, 0)
+    lax.fori_loop(0, 2, some, 0, unroll=2)
 
 
 def edge_kernel(
@@ -725,10 +724,10 @@
     left = lax.ppermute(last, "gx", to_right)
     right = lax.ppermute(first, "gx", to_left)
     rows8 = ((ROWS, 8, LANES), f32, "v")
-    inner, step, compact, totals, conv_w, taps = call(
+    inner, step, decay, compact, totals, conv_w, taps = call(
         project_kernel,
         "vvvvss",
-        [(PLANE, bf16, "v"), (PLANE, f32, "v"), rows8, rows8]
+        [(PLANE, bf16, "v"), (PLANE, f32, "v"), (PLANE, f32, "v"), rows8, rows8]
         + [((WIDTH, 256), bf16, "v"), ((2, 16, LANES), f32, "v")],
         [vmem((WIDTH, 512), bf16)],
         tokens,
@@ -749,11 +748,10 @@
     quarters = vmem((CHIPS,) + packet[0], f32)
     all_ends = ((2 * ROWS, 16, LANES), f32, "v")
     cells = ((COLS, ROWS, LANES), f32, "v")
-    xdt, decay, act, bct, maps, ends = call(
+    xdt, act, bct, maps, ends = call(
         inside_kernel,
-        "v" * 8 + "s",
+        "v" * 8,
         [
-            (PLANE, f32, "v"),
             (PLANE, f32, "v"),
             (PLANE, bf16, "v"),
             ((ROWS, 32, COLS), f32, "v"),
@@ -769,7 +767,6 @@
         totals,
         conv_w,
         taps,
-        decay_log,
         after=(up_row, down_row),
     )
     two = (2,) + PLANE[1:]

time: 98.4 us -> 97.8 us (level)
    ppermute x1, starting transfers between devices: 3.1 us -> 5.19 us  [on_device(): above = lax.ppermute(down_row, 'gy', to_down)]
    ppermute x1, starting transfers between devices: 4.01 us -> 1.92 us  [on_device(): below = lax.ppermute(up_row, 'gy', to_up)]
    ppermute x6, starting transfers between devices: 9.62 us -> 11.5 us  [rotate(): moved[k] = lax.ppermute(pieces[k], 'gy', ahead[k])]
    ppermute x1, starting transfers between devices: 3.9 us -> 2.56 us  [on_device(): theirs = lax.ppermute(theirs, 'gy', swap)]
    ppermute x6, waiting for transfers between devices: 1.82 us -> 0.79 us  [rotate(): moved[k] = lax.ppermute(pieces[k], 'gy', ahead[k])]
  transfers between devices with their start and end apart: 22 -> 22, of which waited for: 10 -> 8; matrix products, arithmetic and copies ran while one was open for 0% -> 0% of each run, Pallas kernels for 32% -> 31%
where the time goes in v7:
time: 97.8 us; the launch traced here: 97.6 us
  starting transfers between devices  52 us (53%)
  Pallas kernels  37.2 us (38%)
  waiting for transfers between devices  6.29 us (6%)
  local copies, waits for them, and re-layouts  1.77 us (2%)
    pallas_call x20, Pallas kernels, call(): pl.pallas_call(inner, in_specs=[pl.BlockSpec(memory_space=kinds[k]) for k...  37.2 us
    ppermute x3, starting transfers between devices, on_device(): lax.ppermute(both, 'gx', [(i, i + 8 * k) for i in range(gx_count - 8 * k)])  12.4 us
    ppermute x6, starting transfers between devices, rotate(): moved[k] = lax.ppermute(pieces[k], 'gy', ahead[k])  11.5 us
    ppermute x6, starting transfers between devices, members(): moved[k] = lax.ppermute(pieces[k], 'gx', pairs)  9.72 us
    ppermute x1, starting transfers between devices, on_device(): above = lax.ppermute(down_row, 'gy', to_down)  5.19 us
    ppermute x1, starting transfers between devices, on_device(): left = lax.ppermute(last, 'gx', to_right)  3.94 us
    ppermute x1, starting transfers between devices, on_device(): theirs = lax.ppermute(theirs, 'gy', swap)  2.56 us
    ppermute x1, waiting for transfers between devices, on_device(): theirs = lax.ppermute(theirs, 'gy', swap)  2.01 us
  transfers between devices with their start and end apart: 22, of which 8 were waited for; matrix products, arithmetic and copies ran while one was open for 0% of the time, Pallas kernels for 31%

profile of v7, /device:TPU:1, one launch (start us, length us, event | category | flops | bytes accessed | tf_op | source)
XLA Modules:
  0.0 97.6 jit_solution(14954940041531710147)
XLA Ops:
  0.0 1.3 %fusion = (bf16[16,96,1]{2,1,0:T(8,128)(2,1)S(1)}, bf16[16,96,1]{2,1,0:T(8,128)(2,1)S(1)}) fusion(bf16[16,96,128]{2,1,0:T(8,128)(2,1)} %refs_1_.3), kind=kLoop, calls=%fused_computation | loop fusion | bytes 12288 | tf_op jit(solution)/shard_map/slice | solution.py:723
  1.6 3.9 %collective-permute-start = (bf16[16,96]{1,0:T(8,128)(2,1)S(1)}, bf16[16,96]{1,0:T(8,128)(2,1)S(1)}, u32[]{:S(2)}, u32[]{:S(2)}) collective-permute-start(bf16[16,96]{1,0:T(8,128)(2,1)S(1)} %bitcast.4), channel_id=1, source_target_pairs={{0,1},{1,2},{2,3},{3,4},{4,5},{5,6},{6,7},{7,8},{8,9},{9,10},{10,1... | collective-permute-start | bytes 9224 | tf_op jit(solution)/shard_map/ppermute | solution.py:724
  5.7 1.3 %collective-permute-start.1 = (bf16[16,96]{1,0:T(8,128)(2,1)S(1)}, bf16[16,96]{1,0:T(8,128)(2,1)S(1)}, u32[]{:S(2)}, u32[]{:S(2)}) collective-permute-start(bf16[16,96]{1,0:T(8,128)(2,1)S(1)} %bitcast.6), channel_id=1, source_target_pairs={{1,0},{2,1},{3,2},{4,3},{5,4},{6,5},{7,6},{8,7},{9,8},{10,9},{11,1... | collective-permute-start | bytes 9224 | tf_op jit(solution)/shard_map/ppermute | solution.py:725
  7.1 2.6 %shard_map.91 = (bf16[16,2,128,128]{3,2,1,0:T(8,128)(2,1)S(1)}, f32[16,2,128,128]{3,2,1,0:T(8,128)S(1)}, f32[16,2,128,128]{3,2,1,0:T(8,128)S(1)}, f32[16,8,128]{...) custom-call(bf16[16,96,128]{2,1,0:T(8,128)(2,1)S(1)} %copy-done, ...), custom_call_target="tpu_custom_call" | custom-call | tf_op jit(solution)/shard_map/pallas_call | solution.py:693
  10.1 5.2 %collective-permute-start.2 = (bf16[112,128]{1,0:T(8,128)(2,1)S(1)}, bf16[112,128]{1,0:T(8,128)(2,1)S(1)}, u32[]{:S(2)}, u32[]{:S(2)}) collective-permute-start(bf16[112,128]{1,0:T(8,128)(2,1)S(1)} %get-tuple-element.54.refs_9_), channel_id=1, source_target_pairs={{0,32},{32,64},{64,96},{96,128},{128,160},{160,192},{192,224},{1,3... | collective-permute-start | bytes 86024 | tf_op jit(solution)/shard_map/ppermute | solution.py:745
  15.3 1.9 %collective-permute-start.3 = (bf16[112,128]{1,0:T(8,128)(2,1)S(1)}, bf16[112,128]{1,0:T(8,128)(2,1)S(1)}, u32[]{:S(2)}, u32[]{:S(2)}) collective-permute-start(bf16[112,128]{1,0:T(8,128)(2,1)S(1)} %get-tuple-element.55.refs_8_), channel_id=1, source_target_pairs={{32,0},{64,32},{96,64},{128,96},{160,128},{192,160},{224,192},{33,... | collective-permute-start | bytes 86024 | tf_op jit(solution)/shard_map/ppermute | solution.py:746
  17.2 2.3 %shard_map.93 = (f32[16,2,128,128]{3,2,1,0:T(8,128)S(1)}, bf16[16,2,128,128]{3,2,1,0:T(8,128)(2,1)S(1)}, f32[16,32,128]{2,1,0:T(8,128)S(1)}, bf16[16,128,128]{2,1,0:T(8,128)(2,1)S(1)}, f32[32,16,128]{2,1,0:T(8,128)S(1)}) custom-call(bf16[16,2,128,128]{3,2,1,0:T(8,128)(2,1)S(1)} %get-tuple-element.52.refs_0_, ...), custom_call_target="tpu_custom_call" | custom-call | tf_op jit(solution)/shard_map/pallas_call | solution.py:693
  21.1 1.3 %collective-permute-start.4 = (f32[8,16,128]{2,1,0:T(8,128)S(1)}, f32[8,16,128]{2,1,0:T(8,128)S(1)}, u32[]{:S(2)}, u32[]{:S(2)}) collective-permute-start(f32[8,16,128]{2,1,0:T(8,128)S(1)} %get-tuple-element.61), channel_id=1, source_target_pairs={{0,1},{1,2},{2,3},{3,0},{4,5},{5,6},{6,7},{7,4},{8,9},{9,10},{10,1... | collective-permute-start | bytes 196616 | tf_op jit(solution)/shard_map/ppermute | solution.py:799
  22.4 4.9 %collective-permute-start.5 = (f32[8,16,128]{2,1,0:T(8,128)S(1)}, f32[8,16,128]{2,1,0:T(8,128)S(1)}, u32[]{:S(2)}, u32[]{:S(2)}) collective-permute-start(f32[8,16,128]{2,1,0:T(8,128)S(1)} %get-tuple-element.62), channel_id=1, source_target_pairs={{0,2},{1,3},{2,0},{3,1},{4,6},{5,7},{6,4},{7,5},{8,10},{9,11},{10,... | collective-permute-start | bytes 196616 | tf_op jit(solution)/shard_map/ppermute | solution.py:799
  27.3 3.4 %shard_map.95 = (f32[4,416,128]{2,1,0:T(8,128)S(1)}, f32[48,8,128]{2,1,0:T(8,128)S(1)}) custom-call(f32[16,2,128,128]{3,2,1,0:T(8,128)S(1)} %get-tuple-element.64.refs_0_, f32[2,2,128,128]{3,2,1,0:T(8,128)S(1)} %get-tuple-element.65.refs_1_, f32[16,2,128,128]{3,2,1,0:T(8,128)S(1)} %get-tuple-element.51.refs_2_.refs_0_.refs_1_, ...), custom_call_target="tpu_custom_call" | custom-call | tf_op jit(solution)/shard_map/pallas_call | solution.py:693
  30.9 1.7 %collective-permute-start.7 = (f32[8,16,128]{2,1,0:T(8,128)S(1)}, f32[8,16,128]{2,1,0:T(8,128)S(1)}, u32[]{:S(2)}, u32[]{:S(2)}) collective-permute-start(f32[8,16,128]{2,1,0:T(8,128)S(1)} %shard_map.96.refs_3_.refs_0_), channel_id=1, source_target_pairs={{0,4},{1,5},{2,6},{3,7},{4,0},{5,1},{6,2},{7,3},{8,12},{9,13},{10,... | collective-permute-start | bytes 196616 | tf_op jit(solution)/shard_map/ppermute | solution.py:816
  32.6 1.5 %shard_map.97 = (f32[16,2,128,128]{3,2,1,0:T(8,128)S(1)}, f32[16,2,128,128]{3,2,1,0:T(8,128)S(1)}) custom-call(f32[16,2,128,128]{3,2,1,0:T(8,128)S(1)} %get-tuple-element.51.refs_2_.refs_0_.refs_1_, bf16[16,96,128]{2,1,0:T(8,128)(2,1)S(1)} %copy-done, bf16[96,419]{1,0:T(8,128)(2,1)S(1)} %copy-done.1, f32[8,16,128]{2,1,0:T(8,128)S(1)} %shard_map.96.refs_3_.refs_0_), custom_call_target="tpu_custom_call" | custom-call | tf_op jit(solution)/shard_map/pallas_call | solution.py:693
  34.6 7.1 %collective-permute-start.10 = (f32[8,16,128]{2,1,0:T(8,128)S(1)}, f32[8,16,128]{2,1,0:T(8,128)S(1)}, u32[]{:S(2)}, u32[]{:S(2)}) collective-permute-start(f32[8,16,128]{2,1,0:T(8,128)S(1)} %shard_map.98.refs_6_), channel_id=1, source_target_pairs={{0,24},{1,25},{2,26},{3,27},{4,28},{5,29},{6,30},{7,31},{32,56},{3... | collective-permute-start | bytes 196616 | tf_op jit(solution)/shard_map/ppermute | solution.py:838
  41.7 1.7 %collective-permute-start.9 = (f32[8,16,128]{2,1,0:T(8,128)S(1)}, f32[8,16,128]{2,1,0:T(8,128)S(1)}, u32[]{:S(2)}, u32[]{:S(2)}) collective-permute-start(f32[8,16,128]{2,1,0:T(8,128)S(1)} %shard_map.98.refs_6_), channel_id=1, source_target_pairs={{0,16},{1,17},{2,18},{3,19},{4,20},{5,21},{6,22},{7,23},{8,24},{9,... | collective-permute-start | bytes 196616 | tf_op jit(solution)/shard_map/ppermute | solution.py:838
  43.4 3.6 %collective-permute-start.8 = (f32[8,16,128]{2,1,0:T(8,128)S(1)}, f32[8,16,128]{2,1,0:T(8,128)S(1)}, u32[]{:S(2)}, u32[]{:S(2)}) collective-permute-start(f32[8,16,128]{2,1,0:T(8,128)S(1)} %shard_map.98.refs_6_), channel_id=1, source_target_pairs={{0,8},{1,9},{2,10},{3,11},{4,12},{5,13},{6,14},{7,15},{8,16},{9,17... | collective-permute-start | bytes 196616 | tf_op jit(solution)/shard_map/ppermute | solution.py:838
  47.0 3.4 %shard_map.99.refs_8_.refs_2_ = f32[4,416,128]{2,1,0:T(8,128)S(1)} custom-call(f32[16,2,128,128]{3,2,1,0:T(8,128)S(1)} %get-tuple-element.64.refs_0_, f32[2,2,128,128]{3,2,1,0:T(8,128)S(1)} %get-tuple-element.65.refs_1_, f32[16,2,128,128]{3,2,1,0:T(8,128)S(1)} %get-tuple-element.51.refs_2_.refs_0_.refs_1_, f32[16,32,128]{2,1,0:T(8,128)S(1)} %get-tuple-element.66.refs_3_, ...), custom_call_target="tpu_custom_call" | custom-call | tf_op jit(solution)/shard_map/pallas_call | solution.py:693
  51.6 1.5 %collective-permute-start.12 = (f32[8,16,128]{2,1,0:T(8,128)S(1)}, f32[8,16,128]{2,1,0:T(8,128)S(1)}, u32[]{:S(2)}, u32[]{:S(2)}) collective-permute-start(f32[8,16,128]{2,1,0:T(8,128)S(1)} %get-tuple-element.73), channel_id=1, source_target_pairs={{0,2},{1,3},{2,0},{3,1},{4,6},{5,7},{6,4},{7,5},{8,10},{9,11},{10,... | collective-permute-start | bytes 196616 | tf_op jit(solution)/shard_map/ppermute | solution.py:799
  53.1 1.0 %collective-permute-start.13 = (f32[8,16,128]{2,1,0:T(8,128)S(1)}, f32[8,16,128]{2,1,0:T(8,128)S(1)}, u32[]{:S(2)}, u32[]{:S(2)}) collective-permute-start(f32[8,16,128]{2,1,0:T(8,128)S(1)} %get-tuple-element.74), channel_id=1, source_target_pairs={{0,3},{1,0},{2,1},{3,2},{4,7},{5,4},{6,5},{7,6},{8,11},{9,8},{10,9... | collective-permute-start | bytes 196616 | tf_op jit(solution)/shard_map/ppermute | solution.py:799
  54.1 1.7 %shard_map.101.refs_0_ = f32[16,2,128,128]{3,2,1,0:T(8,128)S(1)} custom-call(f32[16,2,128,128]{3,2,1,0:T(8,128)S(1)} %get-tuple-element.50.refs_3_.refs_5_.refs_0_, f32[16,2,128,128]{3,2,1,0:T(8,128)S(1)} %get-tuple-element.51.refs_2_.refs_0_.refs_1_, f32[3]{0:T(128)S(1)} %copy-done.5, f32[8,16,128]{2,1,0:T(8,128)S(1)} %get-tuple-element.70.refs_3_), custom_call_target="tpu_custom_call" | custom-call | tf_op jit(solution)/shard_map/pallas_call | solution.py:693
  56.7 2.2 %shard_map.102 = (f32[4,416,128]{2,1,0:T(8,128)S(1)}, f32[4,416,128]{2,1,0:T(8,128)S(1)}, f32[32,16,128]{2,1,0:T(8,128)S(1)}) custom-call(f32[16,2,128,128]{3,2,1,0:T(8,128)S(1)} %shard_map.101.refs_0_, f32[4,416,128]{2,1,0:T(8,128)S(1)} %get-tuple-element.71.refs_1_, f32[4,416,128]{2,1,0:T(8,128)S(1)} %shard_map.99.refs_8_.refs_2_, ...), custom_call_target="tpu_custom_call" | custom-call | tf_op jit(solution)/shard_map/pallas_call | solution.py:693
  58.9 2.6 %collective-permute-start.14 = (f32[4,416,128]{2,1,0:T(8,128)S(1)}, f32[4,416,128]{2,1,0:T(8,128)S(1)}, u32[]{:S(2)}, u32[]{:S(2)}) collective-permute-start(f32[4,416,128]{2,1,0:T(8,128)S(1)} %get-tuple-element.76), channel_id=1, source_target_pairs={{0,32},{32,0},{64,96},{96,64},{128,160},{160,128},{192,224},{224,1... | collective-permute-start | bytes 2555912 | tf_op jit(solution)/shard_map/ppermute | solution.py:869
  61.5 2.0 %collective-permute-done.14.refs_1_.refs_5_ = f32[4,416,128]{2,1,0:T(8,128)S(1)} collective-permute-done((f32[4,416,128]{2,1,0:T(8,128)S(1)}, f32[4,416,128]{2,1,0:T(8,128)S(1)}, u32[]{:S(2)}, u32[]{:S(2)}) %collective-permute-start.14) | collective-permute-done | bytes 852000 | tf_op jit(solution)/shard_map/ppermute | solution.py:869
  63.7 3.2 %collective-permute-start.15 = (f32[416,128]{1,0:T(8,128)S(1)}, f32[416,128]{1,0:T(8,128)S(1)}, u32[]{:S(2)}, u32[]{:S(2)}) collective-permute-start(f32[416,128]{1,0:T(8,128)S(1)} %get-tuple-element.78), channel_id=1, source_target_pairs={{0,64},{32,96},{64,128},{96,160},{128,192},{160,224},{192,0},{224,... | collective-permute-start | bytes 638984 | tf_op jit(solution)/shard_map/ppermute | solution.py:866
  66.9 1.6 %collective-permute-start.16 = (f32[416,128]{1,0:T(8,128)S(1)}, f32[416,128]{1,0:T(8,128)S(1)}, u32[]{:S(2)}, u32[]{:S(2)}) collective-permute-start(f32[416,128]{1,0:T(8,128)S(1)} %get-tuple-element.79), channel_id=1, source_target_pairs={{0,128},{32,160},{64,192},{96,224},{128,0},{160,32},{192,64},{224,... | collective-permute-start | bytes 638984 | tf_op jit(solution)/shard_map/ppermute | solution.py:866
  68.4 1.8 %collective-permute-start.17 = (f32[416,128]{1,0:T(8,128)S(1)}, f32[416,128]{1,0:T(8,128)S(1)}, u32[]{:S(2)}, u32[]{:S(2)}) collective-permute-start(f32[416,128]{1,0:T(8,128)S(1)} %get-tuple-element.80), channel_id=1, source_target_pairs={{0,192},{32,224},{64,0},{96,32},{128,64},{160,96},{192,128},{224,1... | collective-permute-start | bytes 638984 | tf_op jit(solution)/shard_map/ppermute | solution.py:866
  71.0 6.9 %shard_map.104 = (f32[8,2,128,128]{3,2,1,0:T(8,128)S(1)}, f32[8,384,128]{2,1,0:T(8,128)S(1)}) custom-call(f32[16,2,128,128]{3,2,1,0:T(8,128)S(1)} %get-tuple-element.64.refs_0_, f32[2,2,128,128]{3,2,1,0:T(8,128)S(1)} %get-tuple-element.65.refs_1_, f32[16,2,128,128]{3,2,1,0:T(8,128)S(1)} %get-tuple-element.51.refs_2_.refs_0_.refs_1_, ...), custom_call_target="tpu_custom_call" | custom-call | tf_op jit(solution)/shard_map/pallas_call | solution.py:693
  79.1 3.0 %collective-permute-start.19 = (f32[384,128]{1,0:T(8,128)S(1)}, f32[384,128]{1,0:T(8,128)S(1)}, u32[]{:S(2)}, u32[]{:S(2)}) collective-permute-start(f32[384,128]{1,0:T(8,128)S(1)} %get-tuple-element.90), channel_id=1, source_target_pairs={{0,128},{32,160},{64,192},{96,224},{128,0},{160,32},{192,64},{224,... | collective-permute-start | bytes 589832 | tf_op jit(solution)/shard_map/ppermute | solution.py:866
  82.1 1.1 %collective-permute-start.20 = (f32[384,128]{1,0:T(8,128)S(1)}, f32[384,128]{1,0:T(8,128)S(1)}, u32[]{:S(2)}, u32[]{:S(2)}) collective-permute-start(f32[384,128]{1,0:T(8,128)S(1)} %get-tuple-element.91), channel_id=1, source_target_pairs={{0,192},{32,224},{64,0},{96,32},{128,64},{160,96},{192,128},{224,1... | collective-permute-start | bytes 589832 | tf_op jit(solution)/shard_map/ppermute | solution.py:866
  83.2 6.9 %shard_map.107.refs_6_.refs_4_ = f32[8,2,128,128]{3,2,1,0:T(8,128)S(1)} custom-call(f32[16,2,128,128]{3,2,1,0:T(8,128)S(1)} %get-tuple-element.64.refs_0_, f32[2,2,128,128]{3,2,1,0:T(8,128)S(1)} %get-tuple-element.65.refs_1_, f32[16,2,128,128]{3,2,1,0:T(8,128)S(1)} %get-tuple-element.51.refs_2_.refs_0_.refs_1_, ...), custom_call_target="tpu_custom_call" | custom-call | tf_op jit(solution)/shard_map/pallas_call | solution.py:693
  91.1 1.8 %collective-permute-start.21 = (f32[4,384,128]{2,1,0:T(8,128)S(1)}, f32[4,384,128]{2,1,0:T(8,128)S(1)}, u32[]{:S(2)}, u32[]{:S(2)}) collective-permute-start(f32[4,384,128]{2,1,0:T(8,128)S(1)} %get-tuple-element.93.refs_2_), channel_id=1, source_target_pairs={{0,32},{32,0},{64,96},{96,64},{128,160},{160,128},{192,224},{224,1... | collective-permute-start | bytes 2359304 | tf_op jit(solution)/shard_map/ppermute | solution.py:908
  92.9 1.1 %shard_map.109.refs_0_ = f32[16,2,64,128]{3,2,1,0:T(8,128)S(1)} custom-call(f32[4,384,128]{2,1,0:T(8,128)S(1)} %get-tuple-element.92.refs_0_, f32[128,16,128]{2,1,0:T(8,128)S(1)} %shard_map.105.refs_5_.refs_1_.refs_2_, f32[4,384,128]{2,1,0:T(8,128)S(1)} %get-tuple-element.93.refs_2_), custom_call_target="tpu_custom_call" | custom-call | tf_op jit(solution)/shard_map/pallas_call | solution.py:693
  94.8 2.8 %shard_map.110 = bf16[16,96,128]{2,1,0:T(8,128)(2,1)} custom-call(f32[16,2,64,128]{3,2,1,0:T(8,128)S(1)} %shard_map.109.refs_0_, f32[4,384,128]{2,1,0:T(8,128)S(1)} %collective-permute-done.21.refs_1_, f32[128,16,128]{2,1,0:T(8,128)S(1)} %shard_map.105.refs_5_.refs_1_.refs_2_, f32[8,2,128,128]{3,2,1,0:T(8,128)S(1)} %get-tuple-element.94.refs_3_, ...), custom_call_target="tpu_custom_call" | custom-call | tf_op jit(solution)/shard_map/pallas_call | solution.py:693
  (53 shorter events, 9.0 us)
Async XLA Ops:
  0.0 7.0 %copy-start = (bf16[16,96,128]{2,1,0:T(8,128)(2,1)S(1)}, bf16[16,96,128]{2,1,0:T(8,128)(2,1)}, u32[]{:S(2)}) copy-start(bf16[16,96,128]{2,1,0:T(8,128)(2,1)} %refs_1_.3) | copy-start | bytes 1179652
  0.0 7.0 %copy-start.5 = (f32[3]{0:T(128)S(1)}, f32[3]{0:T(128)}, u32[]{:S(2)}) copy-start(f32[3]{0:T(128)} %refs_2_.5) | copy-start | bytes 40
  0.0 7.0 %copy-start.1 = (bf16[96,419]{1,0:T(8,128)(2,1)S(1)}, bf16[96,419]{1,0:T(8,128)(2,1)}, u32[]{:S(2)}) copy-start(bf16[96,419]{1,0:T(8,128)(2,1)} %refs_2_.4) | copy-start | bytes 241348
  0.0 7.0 %copy-start.8 = (f32[3]{0:T(128)S(1)}, f32[3]{0:T(128)}, u32[]{:S(2)}) copy-start(f32[3]{0:T(128)} %refs_4_.1) | copy-start | bytes 40
  0.0 7.0 %copy-start.6 = (f32[224]{0:T(256)S(1)}, f32[224]{0:T(256)}, u32[]{:S(2)}) copy-start(f32[224]{0:T(256)} %param.12) | copy-start | bytes 2692
  0.0 7.0 %copy-start.3 = (f32[3,3,224]{2,1,0:T(4,128)S(1)}, f32[3,3,224]{2,1,0:T(4,128)}, u32[]{:S(2)}) copy-start(f32[3,3,224]{2,1,0:T(4,128)} %refs_2_.3) | copy-start | bytes 24196
  1.6 8.1 %collective-permute-start = (bf16[16,96]{1,0:T(8,128)(2,1)S(1)}, bf16[16,96]{1,0:T(8,128)(2,1)S(1)}, u32[]{:S(2)}, u32[]{:S(2)}) collective-permute-start(bf16[16,96]{1,0:T(8,128)(2,1)S(1)} %bitcast.4), channel_id=1, source_target_pairs={{0,1},{1,2},{2,3},{3,4},{4,5},{5,6},{6,7},{7,8},{8,9},{9,10},{10,1... | collective-permute-start | bytes 9224 | tf_op jit(solution)/shard_map/ppermute | solution.py:724
  5.7 4.3 %collective-permute-start.1 = (bf16[16,96]{1,0:T(8,128)(2,1)S(1)}, bf16[16,96]{1,0:T(8,128)(2,1)S(1)}, u32[]{:S(2)}, u32[]{:S(2)}) collective-permute-start(bf16[16,96]{1,0:T(8,128)(2,1)S(1)} %bitcast.6), channel_id=1, source_target_pairs={{1,0},{2,1},{3,2},{4,3},{5,4},{6,5},{7,6},{8,7},{9,8},{10,9},{11,1... | collective-permute-start | bytes 9224 | tf_op jit(solution)/shard_map/ppermute | solution.py:725
  10.1 9.4 %collective-permute-start.2 = (bf16[112,128]{1,0:T(8,128)(2,1)S(1)}, bf16[112,128]{1,0:T(8,128)(2,1)S(1)}, u32[]{:S(2)}, u32[]{:S(2)}) collective-permute-start(bf16[112,128]{1,0:T(8,128)(2,1)S(1)} %get-tuple-element.54.refs_9_), channel_id=1, source_target_pairs={{0,32},{32,64},{64,96},{96,128},{128,160},{160,192},{192,224},{1,3... | collective-permute-start | bytes 86024 | tf_op jit(solution)/shard_map/ppermute | solution.py:745
  15.3 5.2 %collective-permute-start.3 = (bf16[112,128]{1,0:T(8,128)(2,1)S(1)}, bf16[112,128]{1,0:T(8,128)(2,1)S(1)}, u32[]{:S(2)}, u32[]{:S(2)}) collective-permute-start(bf16[112,128]{1,0:T(8,128)(2,1)S(1)} %get-tuple-element.55.refs_8_), channel_id=1, source_target_pairs={{32,0},{64,32},{96,64},{128,96},{160,128},{192,160},{224,192},{33,... | collective-permute-start | bytes 86024 | tf_op jit(solution)/shard_map/ppermute | solution.py:746
  21.1 9.7 %collective-permute-start.4 = (f32[8,16,128]{2,1,0:T(8,128)S(1)}, f32[8,16,128]{2,1,0:T(8,128)S(1)}, u32[]{:S(2)}, u32[]{:S(2)}) collective-permute-start(f32[8,16,128]{2,1,0:T(8,128)S(1)} %get-tuple-element.61), channel_id=1, source_target_pairs={{0,1},{1,2},{2,3},{3,0},{4,5},{5,6},{6,7},{7,4},{8,9},{9,10},{10,1... | collective-permute-start | bytes 196616 | tf_op jit(solution)/shard_map/ppermute | solution.py:799
  22.4 8.4 %collective-permute-start.5 = (f32[8,16,128]{2,1,0:T(8,128)S(1)}, f32[8,16,128]{2,1,0:T(8,128)S(1)}, u32[]{:S(2)}, u32[]{:S(2)}) collective-permute-start(f32[8,16,128]{2,1,0:T(8,128)S(1)} %get-tuple-element.62), channel_id=1, source_target_pairs={{0,2},{1,3},{2,0},{3,1},{4,6},{5,7},{6,4},{7,5},{8,10},{9,11},{10,... | collective-permute-start | bytes 196616 | tf_op jit(solution)/shard_map/ppermute | solution.py:799
  27.3 3.5 %collective-permute-start.6 = (f32[8,16,128]{2,1,0:T(8,128)S(1)}, f32[8,16,128]{2,1,0:T(8,128)S(1)}, u32[]{:S(2)}, u32[]{:S(2)}) collective-permute-start(f32[8,16,128]{2,1,0:T(8,128)S(1)} %get-tuple-element.63), channel_id=1, source_target_pairs={{0,3},{1,0},{2,1},{3,2},{4,7},{5,4},{6,5},{7,6},{8,11},{9,8},{10,9... | collective-permute-start | bytes 196616 | tf_op jit(solution)/shard_map/ppermute | solution.py:799
  30.9 3.6 %collective-permute-start.7 = (f32[8,16,128]{2,1,0:T(8,128)S(1)}, f32[8,16,128]{2,1,0:T(8,128)S(1)}, u32[]{:S(2)}, u32[]{:S(2)}) collective-permute-start(f32[8,16,128]{2,1,0:T(8,128)S(1)} %shard_map.96.refs_3_.refs_0_), channel_id=1, source_target_pairs={{0,4},{1,5},{2,6},{3,7},{4,0},{5,1},{6,2},{7,3},{8,12},{9,13},{10,... | collective-permute-start | bytes 196616 | tf_op jit(solution)/shard_map/ppermute | solution.py:816
  34.6 15.9 %collective-permute-start.10 = (f32[8,16,128]{2,1,0:T(8,128)S(1)}, f32[8,16,128]{2,1,0:T(8,128)S(1)}, u32[]{:S(2)}, u32[]{:S(2)}) collective-permute-start(f32[8,16,128]{2,1,0:T(8,128)S(1)} %shard_map.98.refs_6_), channel_id=1, source_target_pairs={{0,24},{1,25},{2,26},{3,27},{4,28},{5,29},{6,30},{7,31},{32,56},{3... | collective-permute-start | bytes 196616 | tf_op jit(solution)/shard_map/ppermute | solution.py:838
  41.7 8.8 %collective-permute-start.9 = (f32[8,16,128]{2,1,0:T(8,128)S(1)}, f32[8,16,128]{2,1,0:T(8,128)S(1)}, u32[]{:S(2)}, u32[]{:S(2)}) collective-permute-start(f32[8,16,128]{2,1,0:T(8,128)S(1)} %shard_map.98.refs_6_), channel_id=1, source_target_pairs={{0,16},{1,17},{2,18},{3,19},{4,20},{5,21},{6,22},{7,23},{8,24},{9,... | collective-permute-start | bytes 196616 | tf_op jit(solution)/shard_map/ppermute | solution.py:838
  43.4 7.1 %collective-permute-start.8 = (f32[8,16,128]{2,1,0:T(8,128)S(1)}, f32[8,16,128]{2,1,0:T(8,128)S(1)}, u32[]{:S(2)}, u32[]{:S(2)}) collective-permute-start(f32[8,16,128]{2,1,0:T(8,128)S(1)} %shard_map.98.refs_6_), channel_id=1, source_target_pairs={{0,8},{1,9},{2,10},{3,11},{4,12},{5,13},{6,14},{7,15},{8,16},{9,17... | collective-permute-start | bytes 196616 | tf_op jit(solution)/shard_map/ppermute | solution.py:838
  50.6 5.2 %collective-permute-start.11 = (f32[8,16,128]{2,1,0:T(8,128)S(1)}, f32[8,16,128]{2,1,0:T(8,128)S(1)}, u32[]{:S(2)}, u32[]{:S(2)}) collective-permute-start(f32[8,16,128]{2,1,0:T(8,128)S(1)} %get-tuple-element.72), channel_id=1, source_target_pairs={{0,1},{1,2},{2,3},{3,0},{4,5},{5,6},{6,7},{7,4},{8,9},{9,10},{10,1... | collective-permute-start | bytes 196616 | tf_op jit(solution)/shard_map/ppermute | solution.py:799
  51.6 5.1 %collective-permute-start.12 = (f32[8,16,128]{2,1,0:T(8,128)S(1)}, f32[8,16,128]{2,1,0:T(8,128)S(1)}, u32[]{:S(2)}, u32[]{:S(2)}) collective-permute-start(f32[8,16,128]{2,1,0:T(8,128)S(1)} %get-tuple-element.73), channel_id=1, source_target_pairs={{0,2},{1,3},{2,0},{3,1},{4,6},{5,7},{6,4},{7,5},{8,10},{9,11},{10,... | collective-permute-start | bytes 196616 | tf_op jit(solution)/shard_map/ppermute | solution.py:799
  53.1 3.6 %collective-permute-start.13 = (f32[8,16,128]{2,1,0:T(8,128)S(1)}, f32[8,16,128]{2,1,0:T(8,128)S(1)}, u32[]{:S(2)}, u32[]{:S(2)}) collective-permute-start(f32[8,16,128]{2,1,0:T(8,128)S(1)} %get-tuple-element.74), channel_id=1, source_target_pairs={{0,3},{1,0},{2,1},{3,2},{4,7},{5,4},{6,5},{7,6},{8,11},{9,8},{10,9... | collective-permute-start | bytes 196616 | tf_op jit(solution)/shard_map/ppermute | solution.py:799
  58.9 12.1 %copy-start.4 = (f32[3]{0:T(128)S(1)}, f32[3]{0:T(128)}, u32[]{:S(2)}) copy-start(f32[3]{0:T(128)} %refs_9_.3) | copy-start | bytes 40
  58.9 4.6 %collective-permute-start.14 = (f32[4,416,128]{2,1,0:T(8,128)S(1)}, f32[4,416,128]{2,1,0:T(8,128)S(1)}, u32[]{:S(2)}, u32[]{:S(2)}) collective-permute-start(f32[4,416,128]{2,1,0:T(8,128)S(1)} %get-tuple-element.76), channel_id=1, source_target_pairs={{0,32},{32,0},{64,96},{96,64},{128,160},{160,128},{192,224},{224,1... | collective-permute-start | bytes 2555912 | tf_op jit(solution)/shard_map/ppermute | solution.py:869
  63.7 14.2 %collective-permute-start.15 = (f32[416,128]{1,0:T(8,128)S(1)}, f32[416,128]{1,0:T(8,128)S(1)}, u32[]{:S(2)}, u32[]{:S(2)}) collective-permute-start(f32[416,128]{1,0:T(8,128)S(1)} %get-tuple-element.78), channel_id=1, source_target_pairs={{0,64},{32,96},{64,128},{96,160},{128,192},{160,224},{192,0},{224,... | collective-permute-start | bytes 638984 | tf_op jit(solution)/shard_map/ppermute | solution.py:866
  66.9 11.1 %collective-permute-start.16 = (f32[416,128]{1,0:T(8,128)S(1)}, f32[416,128]{1,0:T(8,128)S(1)}, u32[]{:S(2)}, u32[]{:S(2)}) collective-permute-start(f32[416,128]{1,0:T(8,128)S(1)} %get-tuple-element.79), channel_id=1, source_target_pairs={{0,128},{32,160},{64,192},{96,224},{128,0},{160,32},{192,64},{224,... | collective-permute-start | bytes 638984 | tf_op jit(solution)/shard_map/ppermute | solution.py:866
  68.4 9.6 %collective-permute-start.17 = (f32[416,128]{1,0:T(8,128)S(1)}, f32[416,128]{1,0:T(8,128)S(1)}, u32[]{:S(2)}, u32[]{:S(2)}) collective-permute-start(f32[416,128]{1,0:T(8,128)S(1)} %get-tuple-element.80), channel_id=1, source_target_pairs={{0,192},{32,224},{64,0},{96,32},{128,64},{160,96},{192,128},{224,1... | collective-permute-start | bytes 638984 | tf_op jit(solution)/shard_map/ppermute | solution.py:866
  78.2 11.8 %collective-permute-start.18 = (f32[384,128]{1,0:T(8,128)S(1)}, f32[384,128]{1,0:T(8,128)S(1)}, u32[]{:S(2)}, u32[]{:S(2)}) collective-permute-start(f32[384,128]{1,0:T(8,128)S(1)} %get-tuple-element.89), channel_id=1, source_target_pairs={{0,64},{32,96},{64,128},{96,160},{128,192},{160,224},{192,0},{224,... | collective-permute-start | bytes 589832 | tf_op jit(solution)/shard_map/ppermute | solution.py:866
  79.1 11.7 %collective-permute-start.19 = (f32[384,128]{1,0:T(8,128)S(1)}, f32[384,128]{1,0:T(8,128)S(1)}, u32[]{:S(2)}, u32[]{:S(2)}) collective-permute-start(f32[384,128]{1,0:T(8,128)S(1)} %get-tuple-element.90), channel_id=1, source_target_pairs={{0,128},{32,160},{64,192},{96,224},{128,0},{160,32},{192,64},{224,... | collective-permute-start | bytes 589832 | tf_op jit(solution)/shard_map/ppermute | solution.py:866
  82.1 8.7 %collective-permute-start.20 = (f32[384,128]{1,0:T(8,128)S(1)}, f32[384,128]{1,0:T(8,128)S(1)}, u32[]{:S(2)}, u32[]{:S(2)}) collective-permute-start(f32[384,128]{1,0:T(8,128)S(1)} %get-tuple-element.91), channel_id=1, source_target_pairs={{0,192},{32,224},{64,0},{96,32},{128,64},{160,96},{192,128},{224,1... | collective-permute-start | bytes 589832 | tf_op jit(solution)/shard_map/ppermute | solution.py:866
  91.1 3.7 %copy-start.2 = (bf16[192,96]{1,0:T(8,128)(2,1)S(1)}, bf16[192,96]{1,0:T(8,128)(2,1)}, u32[]{:S(2)}) copy-start(bf16[192,96]{1,0:T(8,128)(2,1)} %refs_7_.1) | copy-start | bytes 110596
  91.1 3.7 %copy-start.7 = (f32[192]{0:T(256)S(1)}, f32[192]{0:T(256)}, u32[]{:S(2)}) copy-start(f32[192]{0:T(256)} %param.16) | copy-start | bytes 2308
  91.1 3.7 %collective-permute-start.21 = (f32[4,384,128]{2,1,0:T(8,128)S(1)}, f32[4,384,128]{2,1,0:T(8,128)S(1)}, u32[]{:S(2)}, u32[]{:S(2)}) collective-permute-start(f32[4,384,128]{2,1,0:T(8,128)S(1)} %get-tuple-element.93.refs_2_), channel_id=1, source_target_pairs={{0,32},{32,0},{64,96},{96,64},{128,160},{160,128},{192,224},{224,1... | collective-permute-start | bytes 2359304 | tf_op jit(solution)/shard_map/ppermute | solution.py:908
